TPU v7x, 32 devices: a whole 2x2x4 slice. The times are simulated.
32 devices in a mesh: dp: 4 (over y, x), heads: 2 (over core), tensor: 4 (over z).
Axes of the slice: x: 2, y: 2, z: 4, core: 2. Of those that a mesh axis runs over, the one named last changes fastest.
Arguments:
- inputs: bfloat16 [6304, 512], P(('dp', 'heads', 'tensor')), may hold values from -6 to 6
- cotangent: bfloat16 [6304, 512], P(('dp', 'heads', 'tensor')), may hold values from -6 to 6
- routes: int32 [6304, 2], P(('dp', 'heads')), may hold values from 0 to 31, all different within a row; in each aligned block of 788 rows (0 to 787, 788 to 1575, ...) at most 64 rows name the same one
- gain_attn: float32 [512], replicated, may hold values from 0.25 to 1.75
- gain_expert: float32 [512], replicated, may hold values from 0.25 to 1.75
- tau: float32 [8], replicated, may hold values from 2 to 12
- w_qkv: bfloat16 [3, 512, 512], P(None, ('dp', 'tensor'), 'heads'), may hold values from -0.25 to 0.25
- w_out_attn: bfloat16 [512, 512], P('heads', ('dp', 'tensor')), may hold values from -2 to 2
- w_router: bfloat16 [512, 32], P(('dp', 'heads')), may hold values from -0.21875 to 0.21875
- w_in: bfloat16 [32, 512, 2048], P(('dp', 'heads'), None, 'tensor'), may hold values from -0.25 to 0.25
- w_out: bfloat16 [32, 2048, 512], P(('dp', 'heads'), 'tensor'), may hold values from -0.125 to 0.125
Outputs:
- output: bfloat16 [6304, 512], P(('dp', 'heads', 'tensor'))
- grad_input: bfloat16 [6304, 512], P(('dp', 'heads', 'tensor'))
- grad_gain_attn: float32 [512], replicated
- grad_gain_expert: float32 [512], replicated
- grad_qkv: float32 [3, 512, 512], P(None, ('dp', 'tensor'), 'heads')
- grad_out_attn: float32 [512, 512], P('heads', ('dp', 'tensor'))
- grad_router: float32 [512, 32], P(('dp', 'heads'))
- grad_in: float32 [32, 512, 2048], P(('dp', 'heads'), None, 'tensor')
- grad_out: float32 [32, 2048, 512], P(('dp', 'heads'), 'tensor')
- clipped_qk: bfloat16 [2, 512, 512], P(None, ('dp', 'tensor'), 'heads')
Inputs may be any that keep to these rules, and one draw needn't show every extreme that they name: `routes`: each row names two different experts. In each aligned block of 788 rows, no expert is named by more than 64 rows, a bound that some block reaches.
All inputs are finite; a program needn't handle non-finite values.
Results may differ from a plain program's by a relative error of at most 0.017.
Values may be sent and summed in bfloat16 or wider, within the bound.
A program may use at most 192 MiB of HBM per device.

v0:
```python
import jax
import jax.numpy as jnp
from jax import lax
from jax.sharding import PartitionSpec as P

HEADS = 8
HEAD_DIM = 64
SEQ = 197


def gelu_tanh(inputs):
    return (
        0.5
        * inputs
        * (1.0 + jnp.tanh(0.7978845608028654 * (inputs + 0.044715 * inputs * inputs * inputs)))
    )


def normalize(inputs):
    centered = inputs - jnp.mean(inputs, -1, keepdims=True)
    factor = lax.rsqrt(jnp.mean(centered * centered, -1, keepdims=True) + 1e-06)
    return (centered * factor, factor)


def norm_back(grad_norm, unit_rows, factor, gain):
    grad_hat = grad_norm * gain
    inner_sum = (
        grad_hat
        - jnp.mean(grad_hat, -1, keepdims=True)
        - unit_rows * jnp.mean(grad_hat * unit_rows, -1, keepdims=True)
    )
    return (factor * inner_sum, jnp.sum(grad_norm * unit_rows, 0))


def attn_forward(block_parts):
    queries, key_rows, value_rows = block_parts
    scores = jnp.einsum(
        "bhqd,bhkd->bhqk", queries, key_rows, preferred_element_type=jnp.float32
    ) * HEAD_DIM ** (-0.5)
    row_peak = jnp.max(scores, -1, keepdims=True)
    exponent = jnp.exp(scores - row_peak)
    summed = jnp.sum(exponent, -1, keepdims=True)
    soft_weights = (exponent / summed).astype(jnp.bfloat16)
    mixed = jnp.einsum(
        "bhqk,bhkd->bhqd", soft_weights, value_rows, preferred_element_type=jnp.float32
    ).astype(jnp.bfloat16)
    return (mixed, (row_peak + jnp.log(summed))[..., 0], jnp.max(row_peak, axis=(0, 2, 3)))


def attn_backward(block_parts):
    queries, key_rows, value_rows, grad_mixed, log_total = block_parts
    score_scale = HEAD_DIM ** (-0.5)
    scores = (
        jnp.einsum("bhqd,bhkd->bhqk", queries, key_rows, preferred_element_type=jnp.float32)
        * score_scale
    )
    soft_weights = jnp.exp(scores - log_total[..., None])
    grad_soft = jnp.einsum(
        "bhqd,bhkd->bhqk", grad_mixed, value_rows, preferred_element_type=jnp.float32
    )
    inner_sum = jnp.sum(soft_weights * grad_soft, -1, keepdims=True)
    grad_scores = (soft_weights * (grad_soft - inner_sum)).astype(jnp.bfloat16)
    grad_query = (
        jnp.einsum("bhqk,bhkd->bhqd", grad_scores, key_rows, preferred_element_type=jnp.float32)
        * score_scale
    ).astype(jnp.bfloat16)
    grad_key = (
        jnp.einsum("bhqk,bhqd->bhkd", grad_scores, queries, preferred_element_type=jnp.float32)
        * score_scale
    ).astype(jnp.bfloat16)
    grad_value = jnp.einsum(
        "bhqk,bhqd->bhkd",
        soft_weights.astype(jnp.bfloat16),
        grad_mixed,
        preferred_element_type=jnp.float32,
    ).astype(jnp.bfloat16)
    return (grad_query, grad_key, grad_value)


def body(
    inputs, cotangent, routes, gain_attn, gain_expert, tau, w_qkv, w_out_attn, w_router, w_in, w_out
):
    row_count, width = inputs.shape
    n_dp = lax.axis_size("dp")
    n_heads = lax.axis_size("heads")
    n_tensor = lax.axis_size("tensor")
    row_piece = w_qkv.shape[1]
    col_piece = w_qkv.shape[2]
    own_heads = col_piece // HEAD_DIM
    head_start = lax.axis_index("heads") * col_piece
    x_float = inputs.astype(jnp.float32)
    unit_one, factor_one = normalize(x_float)
    normed_one = (unit_one * gain_attn).astype(jnp.bfloat16)
    stack_qkv, stack_out = (
        lax.all_gather(w_qkv[None], ("dp", "heads", "tensor"), axis=0, tiled=True),
        lax.all_gather(w_out_attn[None], ("dp", "heads", "tensor"), axis=0, tiled=True),
    )
    full_qkv = (
        stack_qkv.reshape(n_dp, n_heads, n_tensor, 3, row_piece, col_piece)
        .transpose(3, 0, 2, 4, 1, 5)
        .reshape(3, width, width)
    )
    full_out = (
        stack_out.reshape(n_dp, n_heads, n_tensor, col_piece, row_piece)
        .transpose(1, 3, 0, 2, 4)
        .reshape(width, width)
    )
    proj_w = lax.dynamic_slice_in_dim(full_qkv, head_start, col_piece, 2)
    attn_w = lax.dynamic_slice_in_dim(full_out, head_start, col_piece, 0)
    normed_all = lax.all_gather(normed_one, "heads", axis=0, tiled=True)
    head_cols = attn_w.shape[0]
    local_heads = head_cols // HEAD_DIM
    joined_w = jnp.concatenate([proj_w[0], proj_w[1], proj_w[2]], 1)
    projected = jnp.dot(normed_all, joined_w, preferred_element_type=jnp.float32).astype(
        jnp.bfloat16
    )
    images = normed_all.shape[0] // SEQ
    per_block = 4 if images % 4 == 0 else 3 if images % 3 == 0 else 2 if images % 2 == 0 else 1
    block_shape = (images // per_block, per_block, SEQ, local_heads, HEAD_DIM)

    def to_blocks(row_matrix):
        return row_matrix.reshape(block_shape).transpose(0, 1, 3, 2, 4)

    def from_blocks(block_array):
        return block_array.transpose(0, 1, 3, 2, 4).reshape(-1, head_cols)

    queries = to_blocks(projected[:, :head_cols])
    key_rows = to_blocks(projected[:, head_cols : 2 * head_cols])
    value_rows = to_blocks(projected[:, 2 * head_cols :])
    mixed, log_total, head_peaks = lax.map(attn_forward, (queries, key_rows, value_rows))
    mixed_rows = from_blocks(mixed)
    block_peak = jnp.max(head_peaks, 0)
    attn_out = lax.psum_scatter(
        jnp.dot(mixed_rows, attn_w, preferred_element_type=jnp.float32),
        "heads",
        scatter_dimension=0,
        tiled=True,
    )
    peak_full = lax.dynamic_update_slice_in_dim(
        jnp.full((HEADS,), -1e30, jnp.float32), block_peak, lax.axis_index("heads") * local_heads, 0
    )
    hidden = x_float + attn_out
    peak_all = lax.pmax(peak_full, ("dp", "heads", "tensor"))
    peak_logit = lax.dynamic_slice_in_dim(
        peak_all, lax.axis_index("heads") * own_heads, own_heads, 0
    )
    unit_two, factor_two = normalize(hidden)
    normed_two = (unit_two * gain_expert).astype(jnp.bfloat16)
    group_rows, group_cot = (
        lax.all_gather(normed_two, "tensor", axis=0, tiled=True),
        lax.all_gather(cotangent, "tensor", axis=0, tiled=True),
    )
    first_w, second_w, router_w = (
        lax.all_gather(w_in, ("dp", "heads"), axis=0, tiled=True),
        lax.all_gather(w_out, ("dp", "heads"), axis=0, tiled=True),
        lax.all_gather(w_router, ("dp", "heads"), axis=0, tiled=True),
    )
    logits = jnp.dot(group_rows, router_w, preferred_element_type=jnp.float32)
    chosen = jnp.take_along_axis(logits, routes, 1)
    exponent = jnp.exp(chosen - jnp.max(chosen, -1, keepdims=True))
    gate_values = exponent / jnp.sum(exponent, -1, keepdims=True)
    group_count = routes.shape[0]
    experts = router_w.shape[1]
    capacity = (group_count * 5 // (16 * experts) + 1) * 8
    flat_ids = routes.reshape(-1)
    ordering = jnp.argsort(flat_ids, stable=True)
    sorted_ids = flat_ids[ordering]
    counts = jnp.sum(
        (flat_ids[:, None] == jnp.arange(experts, dtype=jnp.int32)[None, :]).astype(jnp.int32), 0
    )
    starts = jnp.cumsum(counts) - counts
    slot_rank = jnp.arange(2 * group_count, dtype=jnp.int32) - starts[sorted_ids]
    slot_table = (
        jnp.full((experts * capacity,), 2 * group_count, jnp.int32)
        .at[sorted_ids * capacity + slot_rank]
        .set(ordering)
    )
    slot_token = slot_table // 2
    padded_rows = jnp.concatenate([group_rows, jnp.zeros((1, width), jnp.bfloat16)], 0)
    slot_in = padded_rows[slot_token].reshape(experts, capacity, width)
    slot_gate = jnp.concatenate([gate_values.reshape(-1), jnp.zeros((1,), jnp.float32)], 0)[
        slot_table
    ]
    pre_gelu = jnp.einsum("ecd,edf->ecf", slot_in, first_w, preferred_element_type=jnp.float32)
    activated = gelu_tanh(pre_gelu).astype(jnp.bfloat16)
    slot_out = jnp.einsum(
        "ecf,efd->ecd", activated, second_w, preferred_element_type=jnp.float32
    ).reshape(-1, width)
    partial_value = (
        jnp.zeros((group_count + 1, width), jnp.float32)
        .at[slot_token]
        .add(slot_gate[:, None] * slot_out)[:group_count]
    )
    expert_mix = lax.psum_scatter(
        partial_value.astype(jnp.bfloat16), "tensor", scatter_dimension=0, tiled=True
    ).astype(jnp.float32)
    output = (hidden + expert_mix).astype(jnp.bfloat16)
    padded_cot = jnp.concatenate([group_cot, jnp.zeros((1, width), jnp.bfloat16)], 0)
    slot_cot = padded_cot[slot_token].astype(jnp.float32)
    grad_slot_out = (
        (slot_gate[:, None] * slot_cot).astype(jnp.bfloat16).reshape(experts, capacity, width)
    )
    gate_part = (
        jnp.zeros((2 * group_count + 1,), jnp.float32)
        .at[slot_table]
        .add(jnp.sum(slot_cot * slot_out, -1))[: 2 * group_count]
        .reshape(group_count, 2)
    )
    grad_act = jnp.einsum(
        "ecd,efd->ecf", grad_slot_out, second_w, preferred_element_type=jnp.float32
    )
    grad_pre = jax.vjp(gelu_tanh, pre_gelu)[1](grad_act)[0].astype(jnp.bfloat16)
    grad_first = jnp.einsum("ecd,ecf->edf", slot_in, grad_pre, preferred_element_type=jnp.float32)
    grad_second = jnp.einsum(
        "ecf,ecd->efd", activated, grad_slot_out, preferred_element_type=jnp.float32
    )
    grad_slots = jnp.einsum(
        "ecf,edf->ecd", grad_pre, first_w, preferred_element_type=jnp.float32
    ).reshape(-1, width)
    grad_part = (
        jnp.zeros((group_count + 1, width), jnp.float32)
        .at[slot_token]
        .add(grad_slots)[:group_count]
    )
    grad_normed_two, grad_gates = (
        lax.psum_scatter(
            grad_part.astype(jnp.bfloat16), "tensor", scatter_dimension=0, tiled=True
        ).astype(jnp.float32),
        lax.psum_scatter(
            gate_part.astype(jnp.bfloat16), "tensor", scatter_dimension=0, tiled=True
        ).astype(jnp.float32),
    )
    shard_first, shard_second = (
        lax.psum_scatter(
            grad_first.astype(jnp.bfloat16), ("dp", "heads"), scatter_dimension=0, tiled=True
        ).astype(jnp.float32),
        lax.psum_scatter(
            grad_second.astype(jnp.bfloat16), ("dp", "heads"), scatter_dimension=0, tiled=True
        ).astype(jnp.float32),
    )
    offset = lax.axis_index("tensor") * row_count
    local_gates = lax.dynamic_slice_in_dim(gate_values, offset, row_count, 0)
    local_routes = lax.dynamic_slice_in_dim(routes, offset, row_count, 0)
    grad_chosen = local_gates * (grad_gates - jnp.sum(local_gates * grad_gates, -1, keepdims=True))
    columns = jnp.arange(experts, dtype=jnp.int32)[None, :]
    grad_logits = (
        jnp.where(local_routes[:, 0:1] == columns, grad_chosen[:, 0:1], 0.0)
        + jnp.where(local_routes[:, 1:2] == columns, grad_chosen[:, 1:2], 0.0)
    ).astype(jnp.bfloat16)
    grad_normed_two = grad_normed_two + jnp.einsum(
        "re,de->rd", grad_logits, router_w, preferred_element_type=jnp.float32
    )
    router_term = jnp.einsum(
        "rd,re->de", normed_two, grad_logits, preferred_element_type=jnp.float32
    )
    grad_hidden_norm, gain_two_term = norm_back(grad_normed_two, unit_two, factor_two, gain_expert)
    grad_hidden = cotangent.astype(jnp.float32) + grad_hidden_norm
    grad_attn = lax.all_gather(grad_hidden.astype(jnp.bfloat16), "heads", axis=0, tiled=True)
    grad_mixed = jnp.einsum(
        "rd,cd->rc", grad_attn, attn_w, preferred_element_type=jnp.float32
    ).astype(jnp.bfloat16)
    out_term = jnp.einsum("rc,rd->cd", mixed_rows, grad_attn, preferred_element_type=jnp.float32)
    grad_query, grad_key, grad_value = lax.map(
        attn_backward, (queries, key_rows, value_rows, to_blocks(grad_mixed), log_total)
    )
    grad_proj = jnp.concatenate(
        [from_blocks(grad_query), from_blocks(grad_key), from_blocks(grad_value)], 1
    )
    grad_normed_one = lax.psum_scatter(
        jnp.einsum("rc,dc->rd", grad_proj, joined_w, preferred_element_type=jnp.float32).astype(
            jnp.bfloat16
        ),
        "heads",
        scatter_dimension=0,
        tiled=True,
    ).astype(jnp.float32)
    proj_term = jnp.einsum("rd,rc->dc", normed_all, grad_proj, preferred_element_type=jnp.float32)
    proj_stack = jnp.stack(
        [
            proj_term[:, :head_cols],
            proj_term[:, head_cols : 2 * head_cols],
            proj_term[:, 2 * head_cols :],
        ],
        0,
    )
    whole_proj = lax.dynamic_update_slice_in_dim(
        jnp.zeros((3, width, width), jnp.float32), proj_stack, head_start, 2
    )
    whole_out = lax.dynamic_update_slice_in_dim(
        jnp.zeros((width, width), jnp.float32), out_term, head_start, 0
    )
    send_qkv = (
        whole_proj.reshape(3, n_dp, n_tensor, row_piece, n_heads, col_piece)
        .transpose(1, 4, 2, 0, 3, 5)
        .reshape(-1, 3, row_piece, col_piece)
    )
    send_out = (
        whole_out.reshape(n_heads, col_piece, n_dp, n_tensor, row_piece)
        .transpose(2, 0, 3, 1, 4)
        .reshape(-1, col_piece, row_piece)
    )
    shard_proj, shard_attn = (
        lax.psum_scatter(send_qkv, ("dp", "heads", "tensor"), scatter_dimension=0, tiled=True),
        lax.psum_scatter(send_out, ("dp", "heads", "tensor"), scatter_dimension=0, tiled=True),
    )
    grad_input_norm, gain_one_term = norm_back(grad_normed_one, unit_one, factor_one, gain_attn)
    grad_input = (grad_hidden + grad_input_norm).astype(jnp.bfloat16)
    gain_one_grad, gain_two_grad, router_all = lax.psum(
        (gain_one_term, gain_two_term, router_term), ("dp", "heads", "tensor")
    )
    router_grad = lax.dynamic_slice_in_dim(
        router_all, lax.axis_index(("dp", "heads")) * w_router.shape[0], w_router.shape[0], 0
    )
    local_tau = lax.dynamic_slice_in_dim(tau, lax.axis_index("heads") * own_heads, own_heads, 0)
    clip_factor = jnp.sqrt(local_tau / jnp.maximum(peak_logit, local_tau))
    clipped = (w_qkv[:2].astype(jnp.float32) * jnp.repeat(clip_factor, HEAD_DIM)).astype(
        jnp.bfloat16
    )
    return (
        output,
        grad_input,
        gain_one_grad,
        gain_two_grad,
        shard_proj[0],
        shard_attn[0],
        router_grad,
        shard_first,
        shard_second,
        clipped,
    )


def solution(mesh):
    return jax.shard_map(
        body,
        mesh=mesh,
        in_specs=(
            P(("dp", "heads", "tensor"), None),
            P(("dp", "heads", "tensor"), None),
            P(("dp", "heads"), None),
            P(),
            P(),
            P(),
            P(None, ("dp", "tensor"), "heads"),
            P("heads", ("dp", "tensor")),
            P(("dp", "heads"), None),
            P(("dp", "heads"), None, "tensor"),
            P(("dp", "heads"), "tensor", None),
        ),
        out_specs=(
            P(("dp", "heads", "tensor"), None),
            P(("dp", "heads", "tensor"), None),
            P(),
            P(),
            P(None, ("dp", "tensor"), "heads"),
            P("heads", ("dp", "tensor")),
            P(("dp", "heads"), None),
            P(("dp", "heads"), None, "tensor"),
            P(("dp", "heads"), "tensor", None),
            P(None, ("dp", "tensor"), "heads"),
        ),
        check_vma=False,
    )
```

profile of v0, /device:TPU:0, one launch (start us, length us, event | category | flops | bytes accessed | tf_op | source)
XLA Modules:
  0.0 1010.6 jit_solution(5997331086487536329)
XLA Ops:
  10.0 2.2 all-gather.2
  12.3 75.6 %all-gather.1 = bf16[8192,32]{0,1:T(8,128)(2,1)S(1)} all-gather(bf16[256,32]{0,1:T(8,128)(2,1)S(1)} %copy-done.43), channel_id=3, replica_groups=mesh['dp'=4,'heads'=2,'tensor'=4] {'dp','heads','tensor'}, dimensions={0}, use_global_device_ids=true | all-gather | bytes 540672 | tf_op jit(solution)/shard_map/all_gather | solution.py:96
  91.8 5.1 sort.17
  96.9 8.8 gather_fusion
  106.4 4.6 fusion.64
  112.1 15.9 %select_select_fusion = s32[1576]{0:T(1024)S(1)} fusion(pred[1576]{0:T(1024)(128)(4,1)S(1)} %get-tuple-element.92, pred[1576]{0:T(1024)(128)(4,1)S(1)} %get-tuple-element.91, pred[1576]{0:T(1024)(128)(4,1)S(1)} %get-tuple-element.90, pred[1576]{0:T(1024)(128)(4,1)S(1)} %get-tuple-element.89, pred[1576]{0:T(1024)(128)(4,1)S(1)} %get-tuple-element.88, ...), kind=kLoop, calls=%fused_computation.164 | loop fusion | flops 39400 | bytes 52108 | tf_op jit(solution)/shard_map/gather | solution.py:172
  128.1 8.8 scatter_custom_fusion
  138.8 17.7 %all-gather.5 = bf16[4,197,512]{2,1,0:T(8,128)(2,1)S(1)} all-gather(bf16[1,197,512]{2,1,0:T(8,128)(2,1)S(1)} %bitcast.200), channel_id=1, replica_groups=mesh['dp'=4,'heads'=2,'tensor'=4] {'tensor'}, dimensions={0}, use_global_device_ids=true | all-gather | bytes 1008640 | tf_op jit(solution)/shard_map/all_gather | solution.py:151
  156.4 3.0 copy.196
  159.5 2.3 reshape.248
  167.6 3.6 fusion
  171.8 2.9 collective-permute-start
  174.7 8.2 all-gather.4
  185.1 7.5 gather_fusion.3
  193.3 2.8 concatenate.23
  199.3 18.3 %all-gather.3 = bf16[4,197,512]{2,1,0:T(8,128)(2,1)S(1)} all-gather(bf16[1,197,512]{2,1,0:T(8,128)(2,1)S(1)} %fusion.117), channel_id=1, replica_groups=mesh['dp'=4,'heads'=2,'tensor'=4] {'tensor'}, dimensions={0}, use_global_device_ids=true | all-gather | bytes 1008640 | tf_op jit(solution)/shard_map/all_gather | solution.py:150
  219.9 9.1 gather_fusion.2
  230.6 20.0 %gather_fusion.4 = f32[1576]{0:T(1024)S(1)} fusion(f32[788,32]{0,1:T(8,128)S(1)} %fusion.91, s32[1576]{0:T(1024)S(1)} %reshape.342), kind=kCustom, calls=%fused_computation.4 | custom fusion | bytes 25216 | tf_op jit(solution)/shard_map/jit(take_along_axis)/gather | solution.py:159
  251.7 11.8 %gather_fusion.1 = f32[2048]{0:T(1024)S(1)} fusion(f32[1577]{0:T(1024)S(1)} %pad_maximum_fusion.3, s32[2048]{0:T(1024)S(1)} %get-tuple-element.122), kind=kCustom, calls=%fused_computation.1 | custom fusion | bytes 24576 | tf_op jit(solution)/shard_map/gather | solution.py:181
  263.6 11.4 %fusion.92 = f32[32,64,512]{2,1,0:T(8,128)} fusion(bf16[32,64,512]{2,1,0:T(8,128)(2,1)} %bitcast.186, bf16[32,512,512]{2,1,0:T(8,128)(2,1)} %all-gather.11.cloned.1.call-done), kind=kOutput, calls=%fused_computation.216 | convolution fusion | flops 1073741824 | bytes 23068672 | tf_op jit(solution)/shard_map/ecd,edf->ecf/dot_general | solution.py:184
  275.0 9.0 fusion.6
  284.0 2.4 bitcast_multiply_fusion
  286.4 14.9 %scatter_custom_fusion.1 = f32[789,512]{1,0:T(8,128)} fusion(s32[2048]{0:T(1024)} %get-tuple-element.124, f32[2048,512]{1,0:T(8,128)} %bitcast_multiply_fusion, f32[]{:T(128)} %constant.61.clone.1), kind=kCustom, calls=%fused_computation.57 | custom fusion | flops 1048576 | bytes 1616384 | tf_op jit(solution)/shard_map/scatter-add | solution.py:192
  302.7 10.9 %fusion.10 = bf16[32,64,512]{2,1,0:T(8,128)(2,1)} fusion(f32[32,64,512]{2,1,0:T(8,128)} %fusion.92, bf16[32,512,512]{2,1,0:T(8,128)(2,1)} %all-gather.13.cloned.1.call-done, bf16[32,64,512]{2,1,0:T(8,128)(2,1)S(1)} %bitcast.184, f32[32,64]{1,0:T(8,128)S(1)} %mul.259), kind=kOutput, calls=%fused_computation.22 | convolution fusion | flops 1102053376 | bytes 25174016 | tf_op jit(solution)/shard_map/ecd,efd->ecf/dot_general | solution.py:209
  313.6 13.5 %fusion.93 = f32[32,64,512]{2,1,0:T(8,128)} fusion(bf16[32,64,512]{2,1,0:T(8,128)(2,1)} %fusion.10, bf16[32,512,512]{2,1,0:T(8,128)(2,1)} %all-gather.11.cloned.1.call-done), kind=kOutput, calls=%fused_computation.217 | convolution fusion | flops 1073741824 | bytes 23068672 | tf_op jit(solution)/shard_map/ecf,edf->ecd/dot_general | solution.py:217
  327.2 14.8 %scatter_custom_fusion.2 = f32[789,512]{1,0:T(8,128)} fusion(s32[2048]{0:T(1024)} %get-tuple-element.124, f32[2048,512]{1,0:T(8,128)} %bitcast.193, f32[]{:T(128)} %constant.61.clone.1), kind=kCustom, calls=%fused_computation.55 | custom fusion | flops 1048576 | bytes 1616384 | tf_op jit(solution)/shard_map/scatter-add | solution.py:223
  341.9 2.4 slice.137
  344.4 14.6 %scatter_custom_fusion.3 = f32[1577]{0:T(1024)S(1)} fusion(s32[2048]{0:T(1024)} %get-tuple-element.121, f32[2048]{0:T(1024)S(1)} %reshape.376, f32[]{:T(128)} %constant.61.clone.1), kind=kCustom, calls=%fused_computation.177 | custom fusion | flops 2048 | bytes 6820 | tf_op jit(solution)/shard_map/scatter-add | solution.py:206
  360.1 36.5 %fusion.83 = (bf16[200,512]{1,0:T(8,128)(2,1)S(1)}, bf16[200,512]{1,0:T(8,128)(2,1)}, bf16[208,2]{1,0:T(8,128)(2,1)}) fusion(bf16[788,512]{1,0:T(8,128)(2,1)S(1)} %slice.138, bf16[788,512]{1,0:T(8,128)(2,1)} %slice.137, bf16[788,2]{1,0:T(8,128)(2,1)} %convert_element_type.134), kind=kCustom, calls=%all-reduce-scatter.5 | all-reduce-scatter fusion | flops 820866 | bytes 2027920
  401.3 1.7 fusion.60
  403.3 12.5 %convolution_convert_fusion.1 = bf16[32,512,512]{2,1,0:T(8,128)(2,1)} fusion(bf16[32,64,512]{2,1,0:T(8,128)(2,1)} %bitcast.187, bf16[32,64,512]{2,1,0:T(8,128)(2,1)} %fusion.10), kind=kOutput, calls=%fused_computation.10 | convolution fusion | flops 1082130432 | bytes 20971520 | tf_op jit(solution)/shard_map/ecd,ecf->edf/dot_general | solution.py:213
  415.9 9.8 convolution_convert_fusion
  426.7 4.2 collective-permute-start.2
  430.9 2.7 collective-permute-start.1
  436.9 2.1 all-gather.6
  442.9 2.4 copy.176
  454.1 3.3 reshape.266
  457.4 4.0 copy.174
  463.4 3.2 fusion.4
  466.9 2.3 collective-permute-start.4
  469.2 40.2 %pmax.7 = f32[8]{0:T(128)S(1)} all-reduce(f32[8]{0:T(128)S(1)} %dynamic_update_slice.26), channel_id=1, replica_groups=mesh['dp'=4,'heads'=2,'tensor'=4] {'dp','heads','tensor'}, use_global_device_ids=true, to_apply=%region_37.38 | all-reduce | flops 8 | bytes 64 | tf_op jit(solution)/shard_map/pmax | solution.py:143
  510.9 39.9 %all-reduce.12 = (f32[512]{0:T(512)}, f32[512]{0:T(512)}) all-reduce(f32[512]{0:T(512)S(1)} %get-tuple-element.64, f32[512]{0:T(512)S(1)} %get-tuple-element.53), channel_id=1, replica_groups=mesh['dp'=4,'heads'=2,'tensor'=4] {'dp','heads','tensor'}, use_global_device_ids=true, to_apply=%region_28.29 | all-reduce | flops 1024 | bytes 8192 | tf_op jit(solution)/shard_map/psum | solution.py:308
  553.1 87.6 %reduce-scatter.19.cloned.1.call-done = bf16[4,512,512]{2,1,0:T(8,128)(2,1)} async-done(((bf16[32,512,512]{2,1,0:T(8,128)(2,1)}), bf16[4,512,512]{2,1,0:T(8,128)(2,1)}) %reduce-scatter.19.cloned.1.call-update) | async-done | bytes 2097168 | tf_op jit(solution)/shard_map/reduce_scatter | solution.py:234
  640.7 4.2 convert_element_type.148
  644.9 115.2 %reduce-scatter.21.cloned.1.call-done = bf16[4,512,512]{2,1,0:T(8,128)(2,1)} async-done(((bf16[32,512,512]{2,1,0:T(8,128)(2,1)}), bf16[4,512,512]{2,1,0:T(8,128)(2,1)}) %reduce-scatter.21.cloned.1.call-update) | async-done | bytes 2097168 | tf_op jit(solution)/shard_map/reduce_scatter | solution.py:237
  760.1 4.2 convert_element_type.150
  764.3 134.0 %reduce-scatter.17.cloned.1.call-done = f32[1,256,32]{1,2,0:T(8,128)} async-done(((f32[32,256,32]{1,2,0:T(8,128)}), f32[1,256,32]{1,2,0:T(8,128)}) %reduce-scatter.17.cloned.1.call-update) | async-done | bytes 32784 | tf_op jit(solution)/shard_map/reduce_scatter | solution.py:304
  898.3 105.0 %reduce-scatter.15.cloned.1.call-done = f32[1,3,32,256]{3,2,1,0:T(8,128)} async-done(((f32[32,3,32,256]{3,2,1,0:T(8,128)}), f32[1,3,32,256]{3,2,1,0:T(8,128)}) %reduce-scatter.15.cloned.1.call-update) | async-done | bytes 98320 | tf_op jit(solution)/shard_map/reduce_scatter | solution.py:303
  (261 shorter events, 55.7 us)
Async XLA Ops:
  7.2 2.3 copy-start.2
  7.2 2.7 copy-start.39
  7.2 149.2 %all-gather.15.cloned.1.call-start = ((), (), s32[]{:S(2)}) async-start(), calls=%async_computation.11 | async-start | bytes 1622016 | tf_op jit(solution)/shard_map/all_gather | solution.py:95
  7.9 4.4 copy-start.43
  7.9 255.7 %all-gather.11.cloned.1.call-start = ((), (), s32[]{:S(2)}) async-start(), calls=%async_computation.4 | async-start | bytes 18874368 | tf_op jit(solution)/shard_map/all_gather | solution.py:154
  8.7 266.3 %all-gather.13.cloned.1.call-start = ((), (), s32[]{:S(2)}) async-start(), calls=%async_computation.5 | async-start | bytes 18874368 | tf_op jit(solution)/shard_map/all_gather | solution.py:155
  9.4 80.2 %copy-start.53 = (u32[32]{0:T(128)S(1)}, u32[32]{0:T(128)}, u32[]{:S(2)}) copy-start(u32[32]{0:T(128)} %constant.205) | copy-start | bytes 388
  9.4 81.5 %copy-start.31 = (s32[788,2]{0,1:T(2,128)S(1)}, s32[788,2]{0,1:T(2,128)}, u32[]{:S(2)}) copy-start(s32[788,2]{0,1:T(2,128)} %param.13) | copy-start | bytes 18916
  9.5 542.3 %all-reduce.16.cloned.1.call-start = ((), (), s32[]{:S(2)}) async-start(), calls=%async_computation.8 | async-start | bytes 131072 | tf_op jit(solution)/shard_map/psum | solution.py:308
  9.6 81.7 %copy-start.37 = (f32[197]{0:T(256)}, f32[197]{0:T(256)S(1)}, u32[]{:S(2)}) copy-start(f32[197]{0:T(256)S(1)} %broadcast_multiply_fusion.5) | copy-start | bytes 2368
  9.9 81.4 %copy-start.44 = (f32[197]{0:T(256)}, f32[197]{0:T(256)S(1)}, u32[]{:S(2)}) copy-start(f32[197]{0:T(256)S(1)} %add_rsqrt_fusion.1) | copy-start | bytes 2368
  12.3 150.6 %copy-start.13 = (bf16[394,512]{1,0:T(8,128)(2,1)}, bf16[394,512]{1,0:T(8,128)(2,1)S(1)}, u32[]{:S(2)}) copy-start(bf16[394,512]{1,0:T(8,128)(2,1)S(1)} %reshape.466) | copy-start | bytes 1210372
  96.9 41.9 %copy-start.20 = (bf16[197,512]{1,0:T(8,128)(2,1)S(1)}, bf16[197,512]{1,0:T(8,128)(2,1)}, u32[]{:S(2)}) copy-start(bf16[197,512]{1,0:T(8,128)(2,1)} %param.12) | copy-start | bytes 605188
  166.8 7.9 copy-start.49
  166.8 17.1 %copy-start.36 = (s32[788,2,1]{0,1,2:T(2,128)S(1)}, s32[788,2,1]{0,1,2:T(2,128)}, u32[]{:S(2)}) copy-start(s32[788,2,1]{0,1,2:T(2,128)} %bitcast_or_fusion) | copy-start | bytes 18916
  166.8 17.5 %copy-start.52 = (u32[32]{0:T(128)S(1)}, u32[32]{0:T(128)}, u32[]{:S(2)}) copy-start(u32[32]{0:T(128)} %constant.209) | copy-start | bytes 388
  167.3 17.1 %copy-start.6 = (bf16[394,256]{0,1:T(8,128)(2,1)}, bf16[394,256]{0,1:T(8,128)(2,1)S(1)}, u32[]{:S(2)}) copy-start(bf16[394,256]{0,1:T(8,128)(2,1)S(1)} %reshape.252) | copy-start | bytes 605188
  171.8 21.5 %collective-permute-start = (f32[3,512]{1,0:T(4,128)}, f32[3,512]{1,0:T(4,128)}, u32[]{:S(2)}, u32[]{:S(2)}) collective-permute-start(f32[3,512]{1,0:T(4,128)} %slice.125), channel_id=1, source_target_pairs={{0,4},{1,5},{2,6},{3,7},{8,12},{9,13},{10,14},{11,15},{16,20},{17,... | collective-permute-start | bytes 18440
  197.3 20.3 %copy-start.4 = (f32[197,512]{1,0:T(8,128)}, f32[197,512]{1,0:T(8,128)S(1)}, u32[]{:S(2)}) copy-start(f32[197,512]{1,0:T(8,128)S(1)} %get-tuple-element.108) | copy-start | bytes 1210372
  219.9 9.2 copy-start.29
  327.2 74.2 %copy-start.5 = (f32[197,512]{1,0:T(8,128)S(1)}, f32[197,512]{1,0:T(8,128)}, u32[]{:S(2)}) copy-start(f32[197,512]{1,0:T(8,128)} %copy-done.4) | copy-start | bytes 1210372
  327.2 74.2 %copy-start.42 = (f32[197]{0:T(256)S(1)}, f32[197]{0:T(256)}, u32[]{:S(2)}) copy-start(f32[197]{0:T(256)} %copy-done.41) | copy-start | bytes 2368
  327.2 74.2 %copy-start.47 = (f32[197]{0:T(256)S(1)}, f32[197]{0:T(256)}, u32[]{:S(2)}) copy-start(f32[197]{0:T(256)} %copy-done.46) | copy-start | bytes 2368
  397.4 2.7 collective-permute-start.3
  403.0 237.7 %reduce-scatter.19.cloned.1.call-start = ((), (), s32[]{:S(2)}) async-start(), calls=%async_computation.9 | async-start | bytes 18874368 | tf_op jit(solution)/shard_map/reduce_scatter | solution.py:234
  415.8 344.3 %reduce-scatter.21.cloned.1.call-start = ((), (), s32[]{:S(2)}) async-start(), calls=%async_computation.10 | async-start | bytes 18874368 | tf_op jit(solution)/shard_map/reduce_scatter | solution.py:237
  425.6 8.0 copy-start.33
  425.6 8.0 copy-start.35
  425.6 9.7 copy-start.30
  425.6 9.7 copy-start.48
  425.7 9.7 copy-start.50
  425.7 9.7 copy-start.51
  425.7 10.2 %copy-start.21 = (bf16[197,512]{1,0:T(8,128)(2,1)S(1)}, bf16[197,512]{1,0:T(8,128)(2,1)}, u32[]{:S(2)}) copy-start(bf16[197,512]{1,0:T(8,128)(2,1)} %param.12) | copy-start | bytes 605188
  425.7 13.4 %copy-start.12 = (bf16[64,8,2,256]{3,1,2,0:T(8,128)(2,1)S(1)}, bf16[64,8,2,256]{3,1,2,0:T(8,128)(2,1)}, u32[]{:S(2)}) copy-start(bf16[64,8,2,256]{3,1,2,0:T(8,128)(2,1)} %copy.188) | copy-start | bytes 1572868
  425.7 472.6 %reduce-scatter.17.cloned.1.call-start = ((), (), s32[]{:S(2)}) async-start(), calls=%async_computation.7 | async-start | bytes 1081344 | tf_op jit(solution)/shard_map/reduce_scatter | solution.py:304
  426.7 7.0 collective-permute-start.2
  430.9 4.1 collective-permute-start.1
  439.8 5.8 copy-start.1
  445.3 558.0 %reduce-scatter.15.cloned.1.call-start = ((), (), s32[]{:S(2)}) async-start(), calls=%async_computation.6 | async-start | bytes 3244032 | tf_op jit(solution)/shard_map/reduce_scatter | solution.py:303
  447.2 2.8 copy-start.8
  461.5 47.8 %copy-start.54 = (f32[8]{0:T(128)S(1)}, f32[8]{0:T(128)}, u32[]{:S(2)}) copy-start(f32[8]{0:T(128)} %param.16) | copy-start | bytes 100
  461.5 48.1 %copy-start.28 = (bf16[3,32,256]{2,1,0:T(8,128)(2,1)S(1)}, bf16[3,32,256]{2,1,0:T(8,128)(2,1)}, u32[]{:S(2)}) copy-start(bf16[3,32,256]{2,1,0:T(8,128)(2,1)} %param.17) | copy-start | bytes 147460
  461.5 49.1 %copy-start.3 = (bf16[197,512]{1,0:T(8,128)(2,1)S(1)}, bf16[197,512]{1,0:T(8,128)(2,1)}, u32[]{:S(2)}) copy-start(bf16[197,512]{1,0:T(8,128)(2,1)} %param.11) | copy-start | bytes 605188
  461.5 49.1 %copy-start.38 = (f32[197]{0:T(256)S(1)}, f32[197]{0:T(256)}, u32[]{:S(2)}) copy-start(f32[197]{0:T(256)} %copy-done.37) | copy-start | bytes 2368
  461.5 49.1 %copy-start.40 = (f32[512]{0:T(512)S(1)}, f32[512]{0:T(512)}, u32[]{:S(2)}) copy-start(f32[512]{0:T(512)} %param.14) | copy-start | bytes 6148
  461.5 49.1 %copy-start.45 = (f32[197]{0:T(256)S(1)}, f32[197]{0:T(256)}, u32[]{:S(2)}) copy-start(f32[197]{0:T(256)} %copy-done.44) | copy-start | bytes 2368
  462.8 88.0 %copy-start.15 = (f32[197,512]{1,0:T(8,128)S(1)}, f32[197,512]{1,0:T(8,128)}, u32[]{:S(2)}) copy-start(f32[197,512]{1,0:T(8,128)} %get-tuple-element.102) | copy-start | bytes 1210372
  466.9 43.3 %collective-permute-start.4 = (bf16[3,512]{1,0:T(4,128)(2,1)S(1)}, bf16[3,512]{1,0:T(4,128)(2,1)S(1)}, u32[]{:S(2)}, u32[]{:S(2)}) collective-permute-start(bf16[3,512]{1,0:T(4,128)(2,1)S(1)} %slice.129), channel_id=1, source_target_pairs={{0,4},{1,5},{2,6},{3,7},{8,12},{9,13},{10,14},{11,15},{16,20},{17,... | collective-permute-start | bytes 9224
  (20 other events, 24.4 us)
Sparse Core Ops, SparseCore 0:
  10.9 58.0 all-gather.14
  70.9 89.1 all-gather.10
  162.0 90.0 all-gather.12
  403.2 117.2 all-reduce.15
  523.9 116.7 reduce-scatter.18
  644.1 115.9 reduce-scatter.20
  762.9 135.2 reduce-scatter.16
  905.2 98.0 reduce-scatter.14
where the time goes:
time: 1020 us; the launch traced here: 1010 us
  waiting for transfers between devices  446 us (44%)
  blocking collectives  247 us (24%)
  local copies, waits for them, and re-layouts  117 us (11%)
  other arithmetic  89.4 us (9%)
  matrix products  78 us (8%)
  between operations  18.1 us (2%)
  starting transfers between devices  14.1 us (1%)
    reduce_scatter x1, waiting for transfers between devices, body(): lax.psum_scatter(send_out, ('dp', 'heads', 'tensor'), scatter_dimension=0...  134 us
    reduce_scatter x1, waiting for transfers between devices, body(): lax.psum_scatter(grad_second.astype(jnp.bfloat16), ('dp', 'heads'), scatt...  115 us
    reduce_scatter x1, waiting for transfers between devices, body(): lax.psum_scatter(send_qkv, ('dp', 'heads', 'tensor'), scatter_dimension=0...  105 us
    reduce_scatter x1, waiting for transfers between devices, body(): lax.psum_scatter(grad_first.astype(jnp.bfloat16), ('dp', 'heads'), scatte...  87.6 us
    all_gather x1, blocking collectives, body(): lax.all_gather(w_out_attn[None], ('dp', 'heads', 'tensor'), axis=0, tiled...  75.6 us
    unnamed x3, blocking collectives  43.3 us
    pmax x1, blocking collectives, body(): peak_all = lax.pmax(peak_full, ('dp', 'heads', 'tensor'))  40.2 us
    psum x1, blocking collectives, body(): lax.psum((gain_one_term, gain_two_term, router_term), ('dp', 'heads', 'te...  39.9 us
  transfers between devices with their start and end apart: 13, of which 6 were waited for; matrix products, arithmetic and copies ran while one was open for 20% of the time, Pallas kernels for 0%

commit v1 on v0

--- a/solution.py
+++ b/solution.py
@@ -1,11 +1,776 @@
+import functools
 import jax
 import jax.numpy as jnp
 from jax import lax
+from jax.experimental import pallas as pl
+from jax.experimental.pallas import tpu as pltpu
 from jax.sharding import PartitionSpec as P
 
 HEADS = 8
 HEAD_DIM = 64
 SEQ = 197
+F32 = jnp.float32
+BF16 = jnp.bfloat16
+MESH = pl.DeviceIdType.MESH
+NEG = -1e30
+
+
+class Sizes:
+    def __init__(self, n_dp, n_heads, n_tensor, inputs, routes, w_qkv, w_router, w_in):
+        self.nd, self.nh, self.nt = n_dp, n_heads, n_tensor
+        self.groups = n_dp * n_heads
+        self.rows, self.width = inputs.shape
+        self.pad = -(-self.rows // 16) * 16
+        self.block = self.pad * n_tensor
+        self.block_rows = routes.shape[0]
+        self.own = w_in.shape[0]
+        self.hidden = w_in.shape[2]
+        self.experts = self.own * self.groups
+        self.cap = (self.block_rows * 5 // (16 * self.experts) + 1) * 8
+        self.group_slots = self.own * self.cap
+        self.slots = self.experts * self.cap
+        self.row_piece, self.col_piece = w_qkv.shape[1], w_qkv.shape[2]
+        self.band = self.row_piece * n_tensor
+        self.router_rows = w_router.shape[0]
+
+    def fits(self):
+        return (
+            self.rows == SEQ
+            and self.block_rows == self.rows * self.nt
+            and self.cap == 64
+            and self.experts == 32
+            and self.group_slots % 128 == 0
+            and self.col_piece % 128 == 0
+            and self.row_piece % 16 == 0
+            and self.router_rows % 16 == 0
+            and self.own * self.groups * 4 == 128
+            and self.width == HEADS * HEAD_DIM
+            and self.block * self.width * 2 <= 2**20
+        )
+
+
+def nn(a, b):
+    return jnp.dot(a, b, preferred_element_type=F32)
+
+
+def nt(a, b):
+    return lax.dot_general(a, b, (((1,), (1,)), ((), ())), preferred_element_type=F32)
+
+
+def tn(a, b):
+    return lax.dot_general(a, b, (((0,), (0,)), ((), ())), preferred_element_type=F32)
+
+
+def iota(shape, axis):
+    return lax.broadcasted_iota(jnp.int32, shape, axis)
+
+
+def normalize(rows):
+    centered = rows - jnp.mean(rows, -1, keepdims=True)
+    factor = lax.rsqrt(jnp.mean(centered * centered, -1, keepdims=True) + 1e-06)
+    return centered * factor, factor
+
+
+def norm_back(grad_norm, unit_rows, factor, gain):
+    grad_hat = grad_norm * gain
+    inner = (
+        grad_hat
+        - jnp.mean(grad_hat, -1, keepdims=True)
+        - unit_rows * jnp.mean(grad_hat * unit_rows, -1, keepdims=True)
+    )
+    return factor * inner, jnp.sum(grad_norm * unit_rows, 0, keepdims=True)
+
+
+def split_high_low(values):
+    high = values.astype(BF16)
+    low = (values - high.astype(F32)).astype(BF16)
+    return jnp.concatenate([high, low], 0)
+
+
+class Place:
+    def __init__(self, sz):
+        self.sz = sz
+        self.d = lax.axis_index("dp")
+        self.h = lax.axis_index("heads")
+        self.z = lax.axis_index("tensor")
+        self.group = self.d * sz.nh + self.h
+
+    def plane(self, group):
+        return (group // self.sz.nh, group % self.sz.nh, self.z)
+
+    def line(self, z):
+        return (self.d, self.h, z)
+
+    def next_group(self, k):
+        return (self.group + k) % self.sz.groups
+
+    def next_z(self, j):
+        return (self.z + j) % self.sz.nt
+
+    def enter(self):
+        sz = self.sz
+        barrier = pltpu.get_barrier_semaphore()
+        for k in range(1, sz.groups):
+            pl.semaphore_signal(barrier, inc=1, device_id=self.plane(self.next_group(k)), device_id_type=MESH)
+        for j in range(1, sz.nt):
+            pl.semaphore_signal(barrier, inc=1, device_id=self.line(self.next_z(j)), device_id_type=MESH)
+        pl.semaphore_wait(barrier, sz.groups + sz.nt - 2)
+
+
+def remote(src, dst, send, recv, device):
+    return pltpu.make_async_remote_copy(
+        src_ref=src, dst_ref=dst, send_sem=send, recv_sem=recv, device_id=device, device_id_type=MESH
+    )
+
+
+def route_table(sz, routes_ref, table):
+    table[...] = jnp.full_like(table, -1.0)
+    for z in range(sz.nt):
+        table[z * sz.pad : z * sz.pad + sz.rows, 0:2] = routes_ref[
+            z * sz.rows : (z + 1) * sz.rows, :
+        ].astype(F32)
+
+
+def front_kernel(
+    sz, x_ref, cot_ref, routes_ref, gain_one_ref, gain_two_ref, w_qkv_ref, w_out_ref, w_router_ref,
+    slots_out, cot_slots_out, gate_out, w_full, router_t, qkv_out, probs_out, mixed_out, hidden_out,
+    block_out, gates_out, peak_out,
+    w_own, router_own, router_full, table, select, cot_block, slots_send, cot_send, gate_send,
+    z_send, z_recv, x_send, x_recv, c_send, c_recv, r_send, r_recv, q_send, q_recv, n_send, n_recv,
+    s_send, s_recv, t_send, t_recv, g_send, g_recv, local_sem,
+):
+    at = Place(sz)
+    d, h, z, me = at.d, at.h, at.z, at.group
+    band, rp, cp, pad = sz.band, sz.row_piece, sz.col_piece, sz.pad
+
+    w_own[0:3] = w_qkv_ref[...]
+    w_own[3] = w_out_ref[...].astype(F32).T.astype(BF16)
+    router_own[...] = jnp.zeros_like(router_own)
+    router_own[:, 0 : sz.experts] = w_router_ref[...]
+
+    own_columns = pl.ds(pl.multiple_of(h * cp, cp), cp)
+
+    def rows_of(dp, tensor):
+        return pl.ds(pl.multiple_of((dp * sz.nt + tensor) * rp, rp), rp)
+
+    def band_of(dp):
+        return pl.ds(pl.multiple_of(dp * band, band), band)
+
+    at.enter()
+
+    w_z = [
+        remote(w_own, w_full.at[:, rows_of(d, z), own_columns], z_send.at[j - 1], z_recv.at[j - 1], at.line(at.next_z(j)))
+        for j in range(1, sz.nt)
+    ]
+    for copy in w_z:
+        copy.start()
+    router_rows = pl.ds(pl.multiple_of(me * sz.router_rows, sz.router_rows), sz.router_rows)
+    routers = [
+        remote(router_own, router_full.at[router_rows], r_send.at[k - 1], r_recv.at[k - 1], at.plane(at.next_group(k)))
+        for k in range(1, sz.groups)
+    ]
+    for copy in routers:
+        copy.start()
+
+    w_full[:, rows_of(d, z), own_columns] = w_own[...]
+    router_full[router_rows] = router_own[...]
+    cot_block[pl.ds(pl.multiple_of(z * pad, pad), pad)] = jnp.zeros((pad, sz.width), BF16)
+    cot_block[pl.ds(pl.multiple_of(z * pad, pad), sz.rows)] = cot_ref[...]
+    own_block = pl.ds(pl.multiple_of(z * pad, pad), pad)
+
+    x_rows = jnp.concatenate([x_ref[...].astype(F32), jnp.zeros((pad - sz.rows, sz.width), F32)], 0)
+    unit_one, _ = normalize(x_rows)
+    normed_one = (unit_one * gain_one_ref[...]).astype(BF16)
+
+    for copy in w_z:
+        copy.wait()
+
+    def peer_dp(k):
+        return (d + k) % sz.nd
+
+    w_x = [
+        remote(
+            w_full.at[:, band_of(d), own_columns], w_full.at[:, band_of(d), own_columns],
+            x_send.at[k - 1], x_recv.at[k - 1], (peer_dp(k), h, z),
+        )
+        for k in range(1, sz.nd)
+    ]
+    for copy in w_x:
+        copy.start()
+
+    def to_core(i, dp, other):
+        place = w_full.at[:, band_of(dp), own_columns]
+        return remote(place, place, c_send.at[i], c_recv.at[i], (d, (h + other) % sz.nh, z))
+
+    w_c = [to_core((other - 1) * sz.nd, d, other) for other in range(1, sz.nh)]
+    for copy in w_c:
+        copy.start()
+    cot_z = [
+        remote(cot_block.at[own_block], cot_block.at[own_block], q_send.at[j - 1], q_recv.at[j - 1], at.line(at.next_z(j)))
+        for j in range(1, sz.nt)
+    ]
+    for copy in cot_z:
+        copy.start()
+
+    route_table(sz, routes_ref, table)
+    turned = table[...].T
+    route_a, route_b = turned[0:1, :], turned[1:2, :]
+    expert = iota((sz.experts, sz.block), 0).astype(F32)
+    named_a, named_b = route_a == expert, route_b == expert
+    named = jnp.logical_or(named_a, named_b)
+    before = (iota((sz.block, sz.block), 0) < iota((sz.block, sz.block), 1)).astype(BF16)
+    rank = nn(named.astype(BF16), before) + expert * float(sz.cap)
+    slot_a = jnp.sum(jnp.where(named_a, rank, 0.0), 0, keepdims=True)
+    slot_b = jnp.sum(jnp.where(named_b, rank, 0.0), 0, keepdims=True)
+    slot_a = jnp.where(route_a < 0.0, -1.0, slot_a)
+    slot_b = jnp.where(route_b < 0.0, -1.0, slot_b)
+
+    def fill(g, carry):
+        slot = iota((sz.group_slots, sz.block), 0).astype(F32) + (g * sz.group_slots).astype(F32)
+        hit = jnp.logical_or(slot == slot_a, slot == slot_b)
+        select[pl.ds(pl.multiple_of(g * sz.group_slots, sz.group_slots), sz.group_slots), :] = jnp.where(
+            hit, 1.0, 0.0
+        ).astype(BF16)
+        return carry
+
+    lax.fori_loop(0, sz.groups, fill, 0)
+
+    for k in range(1, sz.nd):
+        w_x[k - 1].wait_recv()
+        source = (d - k + sz.nd) % sz.nd
+        for other in range(1, sz.nh):
+            copy = to_core((other - 1) * sz.nd + k, source, other)
+            copy.start()
+            w_c.append(copy)
+    for copy in w_c:
+        copy.wait()
+    for copy in w_x:
+        copy.wait_send()
+    for copy in routers:
+        copy.wait()
+    router_t[...] = router_full[...].astype(F32).T[0 : sz.experts].astype(BF16)
+
+    for i in range(3):
+        qkv_out[i] = nn(normed_one, w_full[i]).astype(BF16)
+    lane = iota((1, 2 * HEAD_DIM), 1)
+    halves = (lane < HEAD_DIM, lane >= HEAD_DIM)
+    key_valid = iota((1, pad), 1) < sz.rows
+    row_valid = iota((pad, 1), 0) < sz.rows
+    peak_lane = iota((1, 128), 1)
+    peak_out[...] = jnp.full_like(peak_out, NEG)
+
+    def attend(pair, carry):
+        columns = pl.ds(pl.multiple_of(pair * 2 * HEAD_DIM, 2 * HEAD_DIM), 2 * HEAD_DIM)
+        q_pair, k_pair, v_pair = (qkv_out[i, :, columns] for i in range(3))
+        mixed = []
+        for side in range(2):
+            q_own = jnp.where(halves[side], q_pair, jnp.zeros_like(q_pair))
+            scores = nt(q_own, k_pair) * HEAD_DIM ** (-0.5)
+            scores = jnp.where(key_valid, scores, NEG)
+            row_peak = jnp.max(scores, -1, keepdims=True)
+            exponent = jnp.exp(scores - row_peak)
+            probs = (exponent / jnp.sum(exponent, -1, keepdims=True)).astype(BF16)
+            head = pair * 2 + side
+            probs_out[head] = probs
+            mixed.append(nn(probs, v_pair))
+            peak = jnp.max(jnp.where(row_valid, row_peak, NEG), 0, keepdims=True)
+            peak_out[0:1, :] = jnp.where(peak_lane == head, peak, peak_out[0:1, :])
+        mixed_out[:, columns] = jnp.where(halves[0], mixed[0], mixed[1]).astype(BF16)
+        return carry
+
+    def dispatch(block, send, out, send_sems, recv_sems):
+        def step(i, carry):
+            k = sz.groups - 1 - i
+            g = (me + k) % sz.groups
+            rows = pl.ds(pl.multiple_of(g * sz.group_slots, sz.group_slots), sz.group_slots)
+            send[g] = nn(select[rows, :], block[...]).astype(BF16)
+
+            @pl.when(k > 0)
+            def _():
+                remote(send.at[g], out.at[me], send_sems.at[k], recv_sems.at[k], at.plane(g)).start()
+
+            return carry
+
+        lax.fori_loop(0, sz.groups, step, 0)
+
+    def collect(send, out, send_sems, recv_sems):
+        def step(i, carry):
+            k = i + 1
+            g = (me + k) % sz.groups
+            remote(send.at[g], out.at[me], send_sems.at[k], recv_sems.at[k], at.plane(g)).wait()
+            return carry
+
+        lax.fori_loop(0, sz.groups - 1, step, 0)
+
+    pairs = HEADS // 2
+    lax.fori_loop(0, pairs // 2, attend, 0)
+    for copy in cot_z:
+        copy.wait()
+    dispatch(cot_block, cot_send, cot_slots_out, t_send, t_recv)
+    cot_own = pltpu.make_async_copy(cot_send.at[me], cot_slots_out.at[me], local_sem.at[0])
+    cot_own.start()
+    lax.fori_loop(pairs // 2, pairs, attend, 0)
+
+    hidden = x_rows + nt(mixed_out[...], w_full[3])
+    hidden_out[...] = hidden
+    unit_two, _ = normalize(hidden)
+    normed_two = jnp.where(row_valid, unit_two * gain_two_ref[...], 0.0).astype(BF16)
+    block_out[own_block] = normed_two
+    rows_z = [
+        remote(block_out.at[own_block], block_out.at[own_block], n_send.at[j - 1], n_recv.at[j - 1], at.line(at.next_z(j)))
+        for j in range(1, sz.nt)
+    ]
+    for copy in rows_z:
+        copy.start()
+    for copy in rows_z:
+        copy.wait()
+    dispatch(block_out, slots_send, slots_out, s_send, s_recv)
+    rows_own = pltpu.make_async_copy(slots_send.at[me], slots_out.at[me], local_sem.at[1])
+    rows_own.start()
+
+    logits = jnp.where(named, nt(router_t[...], block_out[...]), NEG)
+    exponent = jnp.where(named, jnp.exp(logits - jnp.max(logits, 0, keepdims=True)), 0.0)
+    total = jnp.sum(exponent, 0, keepdims=True)
+    gates = exponent / jnp.where(total > 0.0, total, 1.0)
+    gates_out[...] = gates
+    by_slot = nt(split_high_low(gates), select[...])
+    by_slot = by_slot[0 : sz.experts] + by_slot[sz.experts :]
+    own_slot = iota((sz.experts, sz.slots), 1) // sz.cap == iota((sz.experts, sz.slots), 0)
+    by_slot = jnp.where(own_slot, by_slot, 0.0)
+    folded = by_slot[:, 0:128]
+    for i in range(1, sz.slots // 128):
+        folded = folded + by_slot[:, i * 128 : (i + 1) * 128]
+    gate_send[...] = folded
+    gate_copies = [
+        remote(gate_send, gate_out.at[me], g_send.at[k - 1], g_recv.at[k - 1], at.plane(at.next_group(k)))
+        for k in range(1, sz.groups)
+    ]
+    for copy in gate_copies:
+        copy.start()
+    gate_out[me] = folded
+
+    collect(cot_send, cot_slots_out, t_send, t_recv)
+    for copy in gate_copies:
+        copy.wait()
+    collect(slots_send, slots_out, s_send, s_recv)
+    cot_own.wait()
+    rows_own.wait()
+
+
+def expert_kernel(sz, slots_ref, cot_ref, gate_ref, first_ref, second_ref,
+                  grad_slots_ref, value_ref, dgate_ref, grad_first_ref, grad_second_ref):
+    e = pl.program_id(0)
+    me = lax.axis_index("dp") * sz.nh + lax.axis_index("heads")
+    many = sz.groups * sz.cap
+    gate_rows = gate_ref[:, pl.ds(me * sz.own + e, 1), :].reshape(sz.groups, 128)
+    turned = gate_rows.T
+    odd = (e % 2) == 1
+    gate_columns = jnp.where(odd, turned[sz.cap : 2 * sz.cap], turned[0 : sz.cap])
+    gate = jnp.concatenate([gate_columns[:, s : s + 1] for s in range(sz.groups)], 0)
+    rows = slots_ref[...].reshape(many, sz.width)
+    cot = cot_ref[...].reshape(many, sz.width).astype(F32)
+    first, second = first_ref[0], second_ref[0]
+    grad_value = (cot * gate).astype(BF16)
+    pre = nn(rows, first)
+    grad_act = nt(grad_value, second)
+    scale, cubic = 0.7978845608028654, 0.044715
+    square = pre * pre
+    bent = jnp.tanh(scale * pre * (1.0 + cubic * square))
+    half = 0.5 * (1.0 + bent)
+    act = (pre * half).astype(BF16)
+    slope = half + 0.5 * pre * (1.0 - bent * bent) * scale * (1.0 + 3.0 * cubic * square)
+    grad_pre = (grad_act * slope).astype(BF16)
+    value = nn(act, second)
+    value_ref[...] = (value * gate).astype(BF16).reshape(sz.groups, sz.cap, sz.width)
+    dgate = nt(jnp.ones((8, sz.width), BF16), (value * cot).astype(BF16))
+
+    @pl.when(e == 0)
+    def _():
+        dgate_ref[...] = jnp.zeros_like(dgate_ref)
+
+    dgate_ref[...] = jnp.where(iota((8, many), 0) == e, dgate, dgate_ref[...])
+    grad_slots_ref[...] = nt(grad_pre, first).astype(BF16).reshape(sz.groups, sz.cap, sz.width)
+    grad_first_ref[0] = tn(rows, grad_pre)
+    grad_second_ref[0] = tn(act, grad_value)
+
+
+def back_kernel(
+    sz, grad_slots, values, dgate_ref, x_ref, cot_ref, routes_ref, gain_one_ref, gain_two_ref, tau_ref, w_qkv_ref,
+    w_full, router_t, qkv, probs, mixed_ref, hidden_ref, block_ref, gates_ref, peak_ref,
+    output_out, grad_input_out, gains_out, weight_out, router_out, clipped_out,
+    table, select, slots_recv, values_recv, dgate_recv, dgate_rows, part, part_own, part_send, part_recv,
+    mix_own, mix_send, mix_recv, grad_mixed, grad_qkv, grad_w, w_half, core_recv, band_send, band_recv, line_send,
+    line_recv, small, small_send, small_core, small_x, small_z, rt, rt_core, rt_x, rt_z,
+    s_send, s_recv, v_send, v_recv, a_send, a_recv, p_send, p_recv, m_send, m_recv, c_send, c_recv, x_send, x_recv,
+    l_send, l_recv, local_sem,
+):
+    at = Place(sz)
+    d, h, z, me = at.d, at.h, at.z, at.group
+    pad, cp, rp, band = sz.pad, sz.col_piece, sz.row_piece, sz.band
+    at.enter()
+
+    def exchange(source, landing, send_sems, recv_sems, k):
+        g = at.next_group(k)
+        return remote(source.at[g], landing.at[me], send_sems.at[k], recv_sems.at[k], at.plane(g))
+
+    def start_all(source, landing, send_sems, recv_sems):
+        def step(i, carry):
+            exchange(source, landing, send_sems, recv_sems, sz.groups - 1 - i).start()
+            return carry
+
+        lax.fori_loop(0, sz.groups - 1, step, 0)
+
+    def wait_all(source, landing, send_sems, recv_sems):
+        def step(i, carry):
+            exchange(source, landing, send_sems, recv_sems, i + 1).wait()
+            return carry
+
+        lax.fori_loop(0, sz.groups - 1, step, 0)
+
+    start_all(grad_slots, slots_recv, s_send, s_recv)
+    dgates = [
+        remote(dgate_ref, dgate_recv.at[me], a_send.at[k - 1], a_recv.at[k - 1], at.plane(at.next_group(k)))
+        for k in range(1, sz.groups)
+    ]
+    for copy in dgates:
+        copy.start()
+    own_grad = pltpu.make_async_copy(grad_slots.at[me], slots_recv.at[me], local_sem.at[0])
+    own_grad.start()
+    own_value = pltpu.make_async_copy(values.at[me], values_recv.at[me], local_sem.at[1])
+    own_value.start()
+    dgate_recv[me] = dgate_ref[...]
+
+    route_table(sz, routes_ref, table)
+    route_a, route_b = table[:, 0:1], table[:, 1:2]
+    expert = iota((sz.block, 128), 1).astype(F32)
+    named_a, named_b = route_a == expert, route_b == expert
+    before = (iota((sz.block, sz.block), 1) < iota((sz.block, sz.block), 0)).astype(BF16)
+    rank = nn(before, jnp.logical_or(named_a, named_b).astype(BF16)) + expert * float(sz.cap)
+    slot_a = jnp.sum(jnp.where(named_a, rank, 0.0), 1, keepdims=True)
+    slot_b = jnp.sum(jnp.where(named_b, rank, 0.0), 1, keepdims=True)
+    table[:, 0:1] = jnp.where(route_a < 0.0, -1.0, slot_a)
+    table[:, 1:2] = jnp.where(route_b < 0.0, -1.0, slot_b)
+
+    def fill(i, carry):
+        rows = pl.ds(pl.multiple_of(i * pad, pad), pad)
+        slot = iota((pad, sz.slots), 1).astype(F32)
+        hit = jnp.logical_or(slot == table[rows, 0:1], slot == table[rows, 1:2])
+        select[rows, :] = jnp.where(hit, 1.0, 0.0).astype(BF16)
+        return carry
+
+    lax.fori_loop(0, sz.nt, fill, 0)
+
+    for copy in dgates:
+        copy.wait()
+    many = sz.groups * sz.cap
+    mine = iota((8, many), 1) // sz.cap == me
+    for g in range(sz.groups):
+        masked = jnp.where(mine, dgate_recv[g], 0.0)
+        folded = masked[:, 0:128]
+        for i in range(1, many // 128):
+            folded = folded + masked[:, i * 128 : (i + 1) * 128]
+        folded = folded + pltpu.roll(folded, 64, 1)
+        dgate_rows[g * sz.own : (g + 1) * sz.own, :] = folded[0 : sz.own]
+    spread = jnp.concatenate([dgate_rows[...]] * (sz.slots // 128), 1)
+    own_slot = iota((sz.experts, sz.slots), 1) // sz.cap == iota((sz.experts, sz.slots), 0)
+    dgate = nt(split_high_low(jnp.where(own_slot, spread, 0.0)), select[...])
+    dgate = dgate[0 : sz.experts] + dgate[sz.experts :]
+    gates = gates_ref[...]
+    dlogits = (gates * (dgate - jnp.sum(gates * dgate, 0, keepdims=True))).astype(BF16)
+    rt[...] = nn(dlogits, block_ref[...])
+    part[...] = tn(dlogits, router_t[...])
+
+    def block_rows(zz):
+        return pl.ds(pl.multiple_of(zz * pad, pad), pad)
+
+    def scatter(slots_recv, base, own, send, recv, send_sems, recv_sems):
+        copies = []
+        for j in [*range(1, sz.nt), 0]:
+            zz = at.next_z(j)
+            flat = slots_recv[...].reshape(sz.slots, sz.width)
+            sums = nn(select[block_rows(zz), :], flat)
+            if base is not None:
+                sums = sums + base[block_rows(zz), :]
+            if j == 0:
+                own[...] = sums
+            else:
+                send[j - 1] = sums.astype(BF16)
+                copy = remote(send.at[j - 1], recv.at[j - 1], send_sems.at[j - 1], recv_sems.at[j - 1], at.line(zz))
+                copy.start()
+                copies.append(copy)
+        return copies
+
+    def gathered(copies, own, recv):
+        for copy in copies:
+            copy.wait()
+        sums = own[...]
+        for j in range(1, sz.nt):
+            sums = sums + recv[j - 1].astype(F32)
+        return sums
+
+    own_grad.wait()
+    wait_all(grad_slots, slots_recv, s_send, s_recv)
+    start_all(values, values_recv, v_send, v_recv)
+    copies = scatter(slots_recv, part, part_own, part_send, part_recv, p_send, p_recv)
+
+    row_valid = iota((pad, 1), 0) < sz.rows
+    zeros = jnp.zeros((pad - sz.rows, sz.width), F32)
+    unit_two, factor_two = normalize(hidden_ref[...])
+    grad_normed = jnp.where(row_valid, gathered(copies, part_own, part_recv), 0.0)
+    grad_hidden, gain_two = norm_back(grad_normed, unit_two, factor_two, gain_two_ref[...])
+    grad_hidden = jnp.concatenate([cot_ref[...].astype(F32), zeros], 0) + jnp.where(row_valid, grad_hidden, 0.0)
+    grad_attn = grad_hidden.astype(BF16)
+    part_own[...] = grad_hidden
+    grad_mixed[...] = nn(grad_attn, w_full[3]).astype(BF16)
+    grad_w[3] = tn(grad_attn, mixed_ref[...]).astype(BF16)
+
+    lane = iota((1, 2 * HEAD_DIM), 1)
+    halves = (lane < HEAD_DIM, lane >= HEAD_DIM)
+    scale = HEAD_DIM ** (-0.5)
+
+    def attend_back(pair, carry):
+        columns = pl.ds(pl.multiple_of(pair * 2 * HEAD_DIM, 2 * HEAD_DIM), 2 * HEAD_DIM)
+        q_pair, k_pair, v_pair = (qkv[i, :, columns] for i in range(3))
+        g_pair = grad_mixed[:, columns]
+        dq, dk, dv = [], [], []
+        for side in range(2):
+            weights = probs[pair * 2 + side]
+            soft = weights.astype(F32)
+            g_own = jnp.where(halves[side], g_pair, jnp.zeros_like(g_pair))
+            grad_soft = nt(g_own, v_pair)
+            inner = jnp.sum(soft * grad_soft, -1, keepdims=True)
+            grad_scores = (soft * (grad_soft - inner)).astype(BF16)
+            dq.append(nn(grad_scores, k_pair))
+            dk.append(tn(grad_scores, q_pair))
+            dv.append(tn(weights, g_pair))
+        grad_qkv[0, :, columns] = (jnp.where(halves[0], dq[0], dq[1]) * scale).astype(BF16)
+        grad_qkv[1, :, columns] = (jnp.where(halves[0], dk[0], dk[1]) * scale).astype(BF16)
+        grad_qkv[2, :, columns] = jnp.where(halves[0], dv[0], dv[1]).astype(BF16)
+        return carry
+
+    lax.fori_loop(0, HEADS // 2, attend_back, 0)
+
+    own_value.wait()
+    wait_all(values, values_recv, v_send, v_recv)
+    mix_copies = scatter(values_recv, None, mix_own, mix_send, mix_recv, m_send, m_recv)
+
+    x_rows = jnp.concatenate([x_ref[...].astype(F32), zeros], 0)
+    unit_one, factor_one = normalize(x_rows)
+    normed_one = (unit_one * gain_one_ref[...]).astype(BF16)
+    grad_one = jnp.zeros((pad, sz.width), F32)
+    for i in range(3):
+        grad_w[i] = tn(normed_one, grad_qkv[i]).astype(BF16)
+        grad_one = grad_one + nt(grad_qkv[i], w_full[i])
+    grad_one = jnp.where(row_valid, grad_one, 0.0)
+    grad_input, gain_one = norm_back(grad_one, unit_one, factor_one, gain_one_ref[...])
+    grad_input_out[...] = (part_own[...] + grad_input)[0 : sz.rows].astype(BF16)
+
+    small[...] = jnp.zeros_like(small)
+    small[0:1, :] = gain_one
+    small[1:2, :] = gain_two
+    small[2:3, 0:128] = peak_ref[0:1, :]
+    peak_row = iota(small.shape, 0) == 2
+
+    def join(a, b):
+        return jnp.where(peak_row, jnp.maximum(a, b), a + b)
+
+    def columns_of(core):
+        return pl.ds(pl.multiple_of(core * cp, cp), cp)
+
+    core_copies = []
+    for other in range(1, sz.nh):
+        core = (h + other) % sz.nh
+        n, device = 3 * (other - 1), (d, core, z)
+        core_copies += [
+            remote(grad_w.at[:, :, columns_of(core)], core_recv.at[other - 1], c_send.at[n], c_recv.at[n], device),
+            remote(small, small_core.at[other - 1], c_send.at[n + 1], c_recv.at[n + 1], device),
+            remote(rt, rt_core.at[other - 1], c_send.at[n + 2], c_recv.at[n + 2], device),
+        ]
+    for copy in core_copies:
+        copy.start()
+    for copy in core_copies:
+        copy.wait()
+    for i in range(4):
+        sums = grad_w[i, :, columns_of(h)].astype(F32)
+        for other in range(1, sz.nh):
+            sums = sums + core_recv[other - 1, i].astype(F32)
+        w_half[i] = sums
+        band_send[i] = sums.astype(BF16)
+    for other in range(1, sz.nh):
+        small[...] = join(small[...], small_core[other - 1])
+        rt[...] = rt[...] + rt_core[other - 1]
+    small_send[0] = small[...]
+
+    def band_of(dp):
+        return pl.ds(pl.multiple_of(dp * band, band), band)
+
+    x_copies = []
+    for k in range(1, sz.nd):
+        to, n = (d + k) % sz.nd, 3 * (k - 1)
+        device = (to, h, z)
+        x_copies += [
+            remote(band_send.at[:, band_of(to), :], band_recv.at[k - 1], x_send.at[n], x_recv.at[n], device),
+            remote(small_send.at[0], small_x.at[k - 1], x_send.at[n + 1], x_recv.at[n + 1], device),
+            remote(rt.at[:, band_of(to)], rt_x.at[k - 1], x_send.at[n + 2], x_recv.at[n + 2], device),
+        ]
+    for copy in x_copies:
+        copy.start()
+
+    mix = gathered(mix_copies, mix_own, mix_recv)
+    output_out[...] = (hidden_ref[...] + mix)[0 : sz.rows].astype(BF16)
+
+    for copy in x_copies:
+        copy.wait()
+    router_sum = rt[:, band_of(d)]
+    for k in range(1, sz.nd):
+        small[...] = join(small[...], small_x[k - 1])
+        router_sum = router_sum + rt_x[k - 1]
+    rt_z[sz.nt - 1] = router_sum
+    small_send[1] = small[...]
+    for i in range(4):
+        sums = w_half[i, band_of(d), :]
+        for k in range(1, sz.nd):
+            sums = sums + band_recv[k - 1, i].astype(F32)
+        w_half[i, 0:band, :] = sums
+        line_send[i] = sums.astype(BF16)
+
+    def rows_of(zz):
+        return pl.ds(pl.multiple_of(zz * rp, rp), rp)
+
+    z_copies = []
+    for j in range(1, sz.nt):
+        to, n = at.next_z(j), 3 * (j - 1)
+        device = at.line(to)
+        z_copies += [
+            remote(line_send.at[:, rows_of(to), :], line_recv.at[j - 1], l_send.at[n], l_recv.at[n], device),
+            remote(small_send.at[1], small_z.at[j - 1], l_send.at[n + 1], l_recv.at[n + 1], device),
+            remote(rt_z.at[sz.nt - 1], rt_z.at[j - 1], l_send.at[n + 2], l_recv.at[n + 2], device),
+        ]
+    for copy in z_copies:
+        copy.start()
+    for copy in z_copies:
+        copy.wait()
+    totals = small[...]
+    router_sum = rt_z[sz.nt - 1]
+    for j in range(1, sz.nt):
+        totals = join(totals, small_z[j - 1])
+        router_sum = router_sum + rt_z[j - 1]
+    gains_out[...] = totals
+    router_out[...] = router_sum
+    for i in range(4):
+        sums = w_half[i, rows_of(z), :]
+        for j in range(1, sz.nt):
+            sums = sums + line_recv[j - 1, i].astype(F32)
+        weight_out[i] = sums
+
+    tau = tau_ref[...]
+    factor = jnp.sqrt(tau / jnp.maximum(totals[2:3, 0:128], tau))
+    column = iota((1, cp), 1) // HEAD_DIM + h * (cp // HEAD_DIM)
+    scale_row = jnp.zeros((1, cp), F32)
+    for head in range(HEADS):
+        scale_row = jnp.where(column == head, factor[:, head : head + 1], scale_row)
+    for i in range(2):
+        clipped_out[i] = (w_qkv_ref[i].astype(F32) * scale_row).astype(BF16)
+
+
+def fast_body(
+    sz, inputs, cotangent, routes, gain_attn, gain_expert, tau, w_qkv, w_out_attn, w_router, w_in, w_out
+):
+    ng, nz, nd, nh, pad, width = sz.groups, sz.nt, sz.nd, sz.nh, sz.pad, sz.width
+    vmem, hbm = pl.BlockSpec(memory_space=pltpu.VMEM), pl.BlockSpec(memory_space=pl.ANY)
+    dma = pltpu.SemaphoreType.DMA
+    gain_one, gain_two = gain_attn[None, :], gain_expert[None, :]
+
+    def shape(dims, dtype):
+        return jax.ShapeDtypeStruct(dims, dtype)
+
+    slot_shape = (ng, sz.group_slots, width)
+    (slots, cot_slots, gate_slots, w_full, router_t, qkv, probs, mixed, hidden, block, gates, peak) = pl.pallas_call(
+        functools.partial(front_kernel, sz),
+        out_shape=(
+            shape(slot_shape, BF16), shape(slot_shape, BF16), shape((ng, sz.experts, 128), F32),
+            shape((4, width, width), BF16), shape((sz.experts, width), BF16), shape((3, pad, width), BF16),
+            shape((HEADS, pad, pad), BF16), shape((pad, width), BF16), shape((pad, width), F32),
+            shape((sz.block, width), BF16), shape((sz.experts, sz.block), F32), shape((8, 128), F32),
+        ),
+        in_specs=[vmem] * 8,
+        out_specs=(hbm, hbm) + (vmem,) * 10,
+        scratch_shapes=[
+            pltpu.VMEM((4, sz.row_piece, sz.col_piece), BF16),
+            pltpu.VMEM((sz.router_rows, 128), BF16), pltpu.VMEM((width, 128), BF16),
+            pltpu.VMEM((sz.block, 128), F32), pltpu.VMEM((sz.slots, sz.block), BF16),
+            pltpu.VMEM((sz.block, width), BF16),
+            pltpu.VMEM(slot_shape, BF16), pltpu.VMEM(slot_shape, BF16), pltpu.VMEM((sz.experts, 128), F32),
+            dma((nz - 1,)), dma((nz - 1,)), dma((nd - 1,)), dma((nd - 1,)),
+            dma((nd * (nh - 1),)), dma((nd * (nh - 1),)), dma((ng - 1,)), dma((ng - 1,)),
+            dma((nz - 1,)), dma((nz - 1,)), dma((nz - 1,)), dma((nz - 1,)),
+            dma((ng,)), dma((ng,)), dma((ng,)), dma((ng,)), dma((ng - 1,)), dma((ng - 1,)), dma((2,)),
+        ],
+        compiler_params=pltpu.CompilerParams(collective_id=0, has_side_effects=True, vmem_limit_bytes=56 * 2**20),
+        name="front",
+    )(inputs, cotangent, routes, gain_one, gain_two, w_qkv, w_out_attn, w_router)
+
+    slot_spec = pl.BlockSpec((ng, sz.cap, width), lambda e: (0, e, 0))
+    first_spec = pl.BlockSpec((1, width, sz.hidden), lambda e: (e, 0, 0))
+    second_spec = pl.BlockSpec((1, sz.hidden, width), lambda e: (e, 0, 0))
+    many = ng * sz.cap
+    grad_slots, values, dgate, grad_first, grad_second = pl.pallas_call(
+        functools.partial(expert_kernel, sz),
+        grid=(sz.own,),
+        out_shape=(
+            shape(slot_shape, BF16), shape(slot_shape, BF16), shape((8, many), F32),
+            shape(w_in.shape, F32), shape(w_out.shape, F32),
+        ),
+        in_specs=[slot_spec, slot_spec, pl.BlockSpec((ng, sz.experts, 128), lambda e: (0, 0, 0)), first_spec, second_spec],
+        out_specs=(slot_spec, slot_spec, pl.BlockSpec((8, many), lambda e: (0, 0)), first_spec, second_spec),
+        compiler_params=pltpu.CompilerParams(vmem_limit_bytes=48 * 2**20),
+        name="experts",
+    )(slots, cot_slots, gate_slots, w_in, w_out)
+
+    tau_row = jnp.pad(tau, (0, 128 - tau.shape[0]), constant_values=1.0)[None, :]
+    rp, cp, band = sz.row_piece, sz.col_piece, sz.band
+    output, grad_input, gains, weight, router, clipped = pl.pallas_call(
+        functools.partial(back_kernel, sz),
+        out_shape=(
+            shape(inputs.shape, BF16), shape(inputs.shape, BF16), shape((8, width), F32),
+            shape((4, rp, cp), F32), shape((sz.experts, band), F32), shape((2, rp, cp), BF16),
+        ),
+        in_specs=[hbm, hbm] + [vmem] * 17,
+        out_specs=(vmem,) * 6,
+        scratch_shapes=[
+            pltpu.VMEM((sz.block, 128), F32), pltpu.VMEM((sz.block, sz.slots), BF16),
+            pltpu.VMEM(slot_shape, BF16), pltpu.VMEM(slot_shape, BF16),
+            pltpu.VMEM((ng, 8, many), F32), pltpu.VMEM((sz.experts, 128), F32),
+            pltpu.VMEM((sz.block, width), F32), pltpu.VMEM((pad, width), F32),
+            pltpu.VMEM((nz - 1, pad, width), BF16), pltpu.VMEM((nz - 1, pad, width), BF16),
+            pltpu.VMEM((pad, width), F32),
+            pltpu.VMEM((nz - 1, pad, width), BF16), pltpu.VMEM((nz - 1, pad, width), BF16),
+            pltpu.VMEM((pad, width), BF16), pltpu.VMEM((3, pad, width), BF16),
+            pltpu.VMEM((4, width, width), BF16), pltpu.VMEM((4, width, cp), F32),
+            pltpu.VMEM((nh - 1, 4, width, cp), BF16), pltpu.VMEM((4, width, cp), BF16),
+            pltpu.VMEM((nd - 1, 4, band, cp), BF16), pltpu.VMEM((4, band, cp), BF16),
+            pltpu.VMEM((nz - 1, 4, rp, cp), BF16),
+            pltpu.VMEM((8, width), F32), pltpu.VMEM((2, 8, width), F32), pltpu.VMEM((nh - 1, 8, width), F32),
+            pltpu.VMEM((nd - 1, 8, width), F32), pltpu.VMEM((nz - 1, 8, width), F32),
+            pltpu.VMEM((sz.experts, width), F32), pltpu.VMEM((nh - 1, sz.experts, width), F32),
+            pltpu.VMEM((nd - 1, sz.experts, band), F32), pltpu.VMEM((nz, sz.experts, band), F32),
+            dma((ng,)), dma((ng,)), dma((ng,)), dma((ng,)), dma((ng - 1,)), dma((ng - 1,)),
+            dma((nz - 1,)), dma((nz - 1,)), dma((nz - 1,)), dma((nz - 1,)),
+            dma((3 * (nh - 1),)), dma((3 * (nh - 1),)), dma((3 * (nd - 1),)), dma((3 * (nd - 1),)),
+            dma((3 * (nz - 1),)), dma((3 * (nz - 1),)), dma((2,)),
+        ],
+        compiler_params=pltpu.CompilerParams(collective_id=1, has_side_effects=True, vmem_limit_bytes=58 * 2**20),
+        name="back",
+    )(
+        grad_slots, values, dgate, inputs, cotangent, routes, gain_one, gain_two, tau_row, w_qkv,
+        w_full, router_t, qkv, probs, mixed, hidden, block, gates, peak,
+    )
+    heads_at = lax.axis_index("heads")
+    router_grad = lax.dynamic_slice_in_dim(router, heads_at * sz.router_rows, sz.router_rows, 1).T
+    return (
+        output, grad_input, gains[0], gains[1], weight[0:3], weight[3].T, router_grad,
+        grad_first, grad_second, clipped,
+    )
 
 
 def gelu_tanh(inputs):
@@ -16,20 +781,15 @@
     )
 
 
-def normalize(inputs):
+def unit_and_factor(inputs):
     centered = inputs - jnp.mean(inputs, -1, keepdims=True)
     factor = lax.rsqrt(jnp.mean(centered * centered, -1, keepdims=True) + 1e-06)
     return (centered * factor, factor)
 
 
-def norm_back(grad_norm, unit_rows, factor, gain):
-    grad_hat = grad_norm * gain
-    inner_sum = (
-        grad_hat
-        - jnp.mean(grad_hat, -1, keepdims=True)
-        - unit_rows * jnp.mean(grad_hat * unit_rows, -1, keepdims=True)
-    )
-    return (factor * inner_sum, jnp.sum(grad_norm * unit_rows, 0))
+def general_norm_back(grad_norm, unit_rows, factor, gain):
+    grad, gain_row = norm_back(grad_norm, unit_rows, factor, gain)
+    return grad, gain_row[0]
 
 
 def attn_forward(block_parts):
@@ -77,7 +837,7 @@
     return (grad_query, grad_key, grad_value)
 
 
-def body(
+def general_body(
     inputs, cotangent, routes, gain_attn, gain_expert, tau, w_qkv, w_out_attn, w_router, w_in, w_out
 ):
     row_count, width = inputs.shape
@@ -89,7 +849,7 @@
     own_heads = col_piece // HEAD_DIM
     head_start = lax.axis_index("heads") * col_piece
     x_float = inputs.astype(jnp.float32)
-    unit_one, factor_one = normalize(x_float)
+    unit_one, factor_one = unit_and_factor(x_float)
     normed_one = (unit_one * gain_attn).astype(jnp.bfloat16)
     stack_qkv, stack_out = (
         lax.all_gather(w_qkv[None], ("dp", "heads", "tensor"), axis=0, tiled=True),
@@ -144,7 +904,7 @@
     peak_logit = lax.dynamic_slice_in_dim(
         peak_all, lax.axis_index("heads") * own_heads, own_heads, 0
     )
-    unit_two, factor_two = normalize(hidden)
+    unit_two, factor_two = unit_and_factor(hidden)
     normed_two = (unit_two * gain_expert).astype(jnp.bfloat16)
     group_rows, group_cot = (
         lax.all_gather(normed_two, "tensor", axis=0, tiled=True),
@@ -168,7 +928,8 @@
     counts = jnp.sum(
         (flat_ids[:, None] == jnp.arange(experts, dtype=jnp.int32)[None, :]).astype(jnp.int32), 0
     )
-    starts = jnp.cumsum(counts) - counts
+    expert_ids = jnp.arange(experts, dtype=jnp.int32)
+    starts = jnp.sum(jnp.where(expert_ids[None, :] < expert_ids[:, None], counts[None, :], 0), 1)
     slot_rank = jnp.arange(2 * group_count, dtype=jnp.int32) - starts[sorted_ids]
     slot_table = (
         jnp.full((experts * capacity,), 2 * group_count, jnp.int32)
@@ -253,7 +1014,7 @@
     router_term = jnp.einsum(
         "rd,re->de", normed_two, grad_logits, preferred_element_type=jnp.float32
     )
-    grad_hidden_norm, gain_two_term = norm_back(grad_normed_two, unit_two, factor_two, gain_expert)
+    grad_hidden_norm, gain_two_term = general_norm_back(grad_normed_two, unit_two, factor_two, gain_expert)
     grad_hidden = cotangent.astype(jnp.float32) + grad_hidden_norm
     grad_attn = lax.all_gather(grad_hidden.astype(jnp.bfloat16), "heads", axis=0, tiled=True)
     grad_mixed = jnp.einsum(
@@ -303,7 +1064,7 @@
         lax.psum_scatter(send_qkv, ("dp", "heads", "tensor"), scatter_dimension=0, tiled=True),
         lax.psum_scatter(send_out, ("dp", "heads", "tensor"), scatter_dimension=0, tiled=True),
     )
-    grad_input_norm, gain_one_term = norm_back(grad_normed_one, unit_one, factor_one, gain_attn)
+    grad_input_norm, gain_one_term = general_norm_back(grad_normed_one, unit_one, factor_one, gain_attn)
     grad_input = (grad_hidden + grad_input_norm).astype(jnp.bfloat16)
     gain_one_grad, gain_two_grad, router_all = lax.psum(
         (gain_one_term, gain_two_term, router_term), ("dp", "heads", "tensor")
@@ -328,6 +1089,16 @@
         shard_second,
         clipped,
     )
+
+
+def body(*args):
+    inputs, _, routes, _, _, _, w_qkv, _, w_router, w_in, _ = args
+    sz = Sizes(
+        lax.axis_size("dp"), lax.axis_size("heads"), lax.axis_size("tensor"), inputs, routes, w_qkv, w_router, w_in
+    )
+    if sz.fits():
+        return fast_body(sz, *args)
+    return general_body(*args)
 
 
 def solution(mesh):

time: 1020 us -> 212 us (0.21)
  waiting for transfers between devices: 446 us -> 0 us
  blocking collectives: 247 us -> 0 us
  Pallas kernels: 0 us -> 192 us
  local copies, waits for them, and re-layouts: 117 us -> 19.4 us
  other arithmetic: 89.4 us -> 0 us
  matrix products: 78 us -> 0 us
  between operations: 18.1 us -> 0.68 us
  starting transfers between devices: 14.1 us -> 0 us
    reduce_scatter x4 -> x0, waiting for transfers between devices: 442 us -> none  [the longest x1 134 us: body(): lax.psum_scatter(send_out, ('dp', 'heads', 'tensor'), scatter_dimension=0...]
    pallas_call x0 -> x3, Pallas kernels: none -> 192 us  [the longest x1 95.4 us: fast_body(): pl.pallas_call(functools.partial(back_kernel, sz), out_shape=(shape(input...]
    all_gather x6 -> x0, blocking collectives: 124 us -> none  [the longest x1 75.6 us: body(): lax.all_gather(w_out_attn[None], ('dp', 'heads', 'tensor'), axis=0, tiled...]
    dot_general x21 -> x0, matrix products: 78 us -> none  [the longest x1 13.5 us: body(): jnp.einsum('ecf,edf->ecd', grad_pre, first_w, preferred_element_type=jnp....]
    gather x11 -> x0, local copies, waits for them, and re-layouts: 59.7 us -> none  [the longest x5 21 us: body(): chosen = jnp.take_along_axis(logits, routes, 1)]
    scatter-add x3 -> x0, other arithmetic: 44.2 us -> none  [the longest x1 14.9 us: body(): partial_value = jnp.zeros((group_count + 1, width), jnp.float32).at[slot_...]
    unnamed x3 -> x0, blocking collectives: 43.3 us -> none
    pmax x1 -> x0, blocking collectives: 40.2 us -> none  [body(): peak_all = lax.pmax(peak_full, ('dp', 'heads', 'tensor'))]
  transfers between devices with their start and end apart: 13 -> 0, of which waited for: 6 -> 0; matrix products, arithmetic and copies ran while one was open for 20% -> 0% of each run, Pallas kernels for 0% -> 0%
where the time goes in v1:
time: 212 us
  Pallas kernels  192 us (91%)
  local copies, waits for them, and re-layouts  19.4 us (9%)
    pallas_call x1, Pallas kernels, fast_body(): pl.pallas_call(functools.partial(back_kernel, sz), out_shape=(shape(input...  95.4 us
    pallas_call x1, Pallas kernels, fast_body(): pl.pallas_call(functools.partial(front_kernel, sz), out_shape=(shape(slot...  82.7 us
    pallas_call x1, Pallas kernels, fast_body(): pl.pallas_call(functools.partial(expert_kernel, sz), grid=(sz.own,), out_...  13.6 us
    unnamed x16, local copies, waits for them, and re-layouts  13.2 us

profile of v1, /device:TPU:0, one launch (start us, length us, event | category | flops | bytes accessed | tf_op | source)
XLA Modules:
  0.0 211.8 jit_solution(167062615622339944)
XLA Ops:
  0.6 1.7 copy.21.routes_ref
  2.3 1.4 copy.22.w_out_ref
  3.8 1.4 copy.23.w_router_ref
  5.1 82.7 %front.1 = (bf16[8,256,512]{2,1,0:T(8,128)(2,1)}, bf16[8,256,512]{2,1,0:T(8,128)(2,1)}, f32[8,32,128]{2,1,0:T(8,128)}, bf16[4,512,512]{2,1,0:T(8,128)(2,1)}, bf1...) custom-call(bf16[197,512]{1,0:T(8,128)(2,1)} %x_ref.3, ...), custom_call_target="tpu_custom_call" | custom-call | tf_op jit(solution)/shard_map/front/pallas_call | solution.py:688
  87.8 0.0 copy-start.2
  87.8 0.9 copy-done.2
  88.7 0.0 copy-start.4
  88.7 13.6 %experts.1 = (bf16[8,256,512]{2,1,0:T(8,128)(2,1)S(1)}, bf16[8,256,512]{2,1,0:T(8,128)(2,1)S(1)}, f32[8,512]{1,0:T(8,128)S(1)}, f32[4,512,512]{2,1,0:T(8,128)}, f32[4,512,512]{2,1,0:T(8,128)}) custom-call(bf16[8,256,512]{2,1,0:T(8,128)(2,1)} %get-tuple-element.33.slots_ref, bf16[8,256,512]{2,1,0:T(8,128)(2,1)} %get-tuple-element.34.cot_ref, ...), custom_call_target="tpu_custom_call" | custom-call | tf_op jit(solution)/shard_map/experts/pallas_call | solution.py:717
  102.3 0.0 copy-start
  102.3 1.3 copy-done
  103.6 0.0 copy-start.1
  103.6 1.3 copy-done.1
  104.9 0.0 copy-start.3
  105.0 0.6 copy-done.3
  105.6 0.0 copy-done.4
  105.6 0.5 pad_bitcast_fusion.tau_ref
  106.1 95.4 %back.1 = (bf16[197,512]{1,0:T(8,128)(2,1)}, bf16[197,512]{1,0:T(8,128)(2,1)}, f32[8,512]{1,0:T(8,128)}, f32[4,32,256]{2,1,0:T(8,128)}, f32[32,128]{1,0:T(8,128)}, /*index=5*/bf16[2,32,256]{2,1,0:T(8,128)(2,1)}) custom-call(bf16[8,256,512]{2,1,0:T(8,128)(2,1)} %copy-done, bf16[8,256,512]{2,1,0:T(8,128)(2,1)} %copy-done.1, f32[8,512]{1,0:T(8,128)} %copy-done.3, ...), custom_call_target="tpu_custom_call" | custom-call | tf_op jit(solution)/shard_map/back/pallas_call | solution.py:732
  201.4 1.5 slice.14
  203.0 1.4 slice_bitcast_fusion
  204.4 1.4 dynamic-slice_bitcast_fusion
  205.8 1.4 fusion
  207.1 1.6 copy.28
  208.8 1.6 copy.29
  210.4 1.4 copy.30
Async XLA Ops:
  87.8 0.9 copy-start.2
  88.7 16.8 %copy-start.4 = (f32[8]{0:T(128)S(1)}, f32[8]{0:T(128)}, u32[]{:S(2)}) copy-start(f32[8]{0:T(128)} %param.16) | copy-start | bytes 100
  102.3 1.3 copy-start
  103.6 1.3 copy-start.1
  104.9 0.6 copy-start.3

commit v2 on v0

--- a/solution.py
+++ b/solution.py
@@ -1,11 +1,852 @@
+import functools
 import jax
 import jax.numpy as jnp
 from jax import lax
+from jax.experimental import pallas as pl
+from jax.experimental.pallas import tpu as pltpu
 from jax.sharding import PartitionSpec as P
 
 HEADS = 8
 HEAD_DIM = 64
 SEQ = 197
+F32 = jnp.float32
+BF16 = jnp.bfloat16
+MESH = pl.DeviceIdType.MESH
+NEG = -1e30
+
+
+class Sizes:
+    def __init__(self, n_dp, n_heads, n_tensor, inputs, routes, w_qkv, w_router, w_in):
+        self.nd, self.nh, self.nt = n_dp, n_heads, n_tensor
+        self.groups = n_dp * n_heads
+        self.rows, self.width = inputs.shape
+        self.pad = -(-self.rows // 16) * 16
+        self.block = self.pad * n_tensor
+        self.block_rows = routes.shape[0]
+        self.own = w_in.shape[0]
+        self.hidden = w_in.shape[2]
+        self.experts = self.own * self.groups
+        self.cap = (self.block_rows * 5 // (16 * self.experts) + 1) * 8
+        self.group_slots = self.own * self.cap
+        self.slots = self.experts * self.cap
+        self.row_piece, self.col_piece = w_qkv.shape[1], w_qkv.shape[2]
+        self.band = self.row_piece * n_tensor
+        self.router_rows = w_router.shape[0]
+        self.parts = 4
+
+    def fits(self):
+        return (
+            self.rows == SEQ
+            and self.block_rows == self.rows * self.nt
+            and self.cap == 64
+            and self.experts == 32
+            and self.group_slots % 128 == 0
+            and self.col_piece % 128 == 0
+            and self.row_piece % 16 == 0
+            and self.router_rows % 16 == 0
+            and self.own * self.groups * 4 == 128
+            and self.width == HEADS * HEAD_DIM
+            and self.block * self.width * 2 <= 2**20
+        )
+
+
+def nn(a, b):
+    return jnp.dot(a, b, preferred_element_type=F32)
+
+
+def nt(a, b):
+    return lax.dot_general(a, b, (((1,), (1,)), ((), ())), preferred_element_type=F32)
+
+
+def tn(a, b):
+    return lax.dot_general(a, b, (((0,), (0,)), ((), ())), preferred_element_type=F32)
+
+
+def iota(shape, axis):
+    return lax.broadcasted_iota(jnp.int32, shape, axis)
+
+
+def normalize(rows):
+    centered = rows - jnp.mean(rows, -1, keepdims=True)
+    factor = lax.rsqrt(jnp.mean(centered * centered, -1, keepdims=True) + 1e-06)
+    return centered * factor, factor
+
+
+def norm_back(grad_norm, unit_rows, factor, gain):
+    grad_hat = grad_norm * gain
+    inner = (
+        grad_hat
+        - jnp.mean(grad_hat, -1, keepdims=True)
+        - unit_rows * jnp.mean(grad_hat * unit_rows, -1, keepdims=True)
+    )
+    return factor * inner, jnp.sum(grad_norm * unit_rows, 0, keepdims=True)
+
+
+def split_high_low(values):
+    high = values.astype(BF16)
+    low = (values - high.astype(F32)).astype(BF16)
+    return jnp.concatenate([high, low], 0)
+
+
+class Place:
+    def __init__(self, sz):
+        self.sz = sz
+        self.d = lax.axis_index("dp")
+        self.h = lax.axis_index("heads")
+        self.z = lax.axis_index("tensor")
+        self.group = self.d * sz.nh + self.h
+
+    def plane(self, group):
+        return (group // self.sz.nh, group % self.sz.nh, self.z)
+
+    def line(self, z):
+        return (self.d, self.h, z)
+
+    def next_group(self, k):
+        return (self.group + k) % self.sz.groups
+
+    def next_z(self, j):
+        return (self.z + j) % self.sz.nt
+
+    def enter(self):
+        sz = self.sz
+        barrier = pltpu.get_barrier_semaphore()
+        for k in range(1, sz.groups):
+            pl.semaphore_signal(barrier, inc=1, device_id=self.plane(self.next_group(k)), device_id_type=MESH)
+        for j in range(1, sz.nt):
+            pl.semaphore_signal(barrier, inc=1, device_id=self.line(self.next_z(j)), device_id_type=MESH)
+        pl.semaphore_wait(barrier, sz.groups + sz.nt - 2)
+
+
+def remote(src, dst, send, recv, device):
+    return pltpu.make_async_remote_copy(
+        src_ref=src, dst_ref=dst, send_sem=send, recv_sem=recv, device_id=device, device_id_type=MESH
+    )
+
+
+def route_table(sz, routes_ref, table):
+    table[...] = jnp.full_like(table, -1.0)
+    for z in range(sz.nt):
+        table[0:2, z * sz.pad : z * sz.pad + sz.rows] = routes_ref[:, z * sz.rows : (z + 1) * sz.rows].astype(F32)
+
+
+def block_kernel(
+    sz, x_ref, cot_ref, routes_ref, gain_one_ref, gain_two_ref, w_qkv_ref, w_out_ref, w_router_ref, first_hbm, second_hbm,
+    output_out, grad_input_out, small_out, weight_out, router_out, grad_first_out, grad_second_out,
+    w_own, w_full, router_own, router_full, router_t, route_rows, route_columns, select, select_t,
+    cot_block, rows_block, send_a, send_b, cot_slots, slots, grad_slots, values,
+    first, second, act, grad_pre, grad_act, grad_first, grad_second,
+    gate_send, gate_recv, gates_at, dgate_send, dgate_recv, dgate_rows,
+    qkv, probs, mixed, hidden_at, peak_at, part, part_own, part_send, part_recv, mix_own, mix_send, mix_recv,
+    grad_mixed, grad_qkv, core_send, core_recv, w_half, band_send, band_recv, line_send, line_recv,
+    small, small_send, small_core, small_x, small_z, rt, rt_core, rt_x, rt_z,
+    wz_s, wz_r, wx_s, wx_r, wc_s, wc_r, r_s, r_r, qz_s, qz_r, nz_s, nz_r, qa_s, qa_r, na_s, na_r, ga_s, ga_r,
+    d0_s, d0_r, da_s, da_r, va_s, va_r, dg_s, dg_r, pz_s, pz_r, mz_s, mz_r, gc_s, gc_r, gx_s, gx_r, gl_s, gl_r,
+    sc_s, sc_r, sx_s, sx_r, sz_s, sz_r, local_sem,
+):
+    at = Place(sz)
+    d, h, z, me = at.d, at.h, at.z, at.group
+    nd, nh, nz, ng = sz.nd, sz.nh, sz.nt, sz.groups
+    band, rp, cp, pad, width = sz.band, sz.row_piece, sz.col_piece, sz.pad, sz.width
+    many = ng * sz.cap
+    parts, part_width = sz.parts, width // sz.parts
+
+    def lanes(c):
+        return pl.ds(c * part_width, part_width)
+
+    def rows_at(n, size):
+        return pl.ds(pl.multiple_of(n * size, size), size)
+
+    own_block, own_columns = rows_at(z, pad), rows_at(h, cp)
+
+    w_own[0:3] = w_qkv_ref[...]
+    w_own[3] = w_out_ref[...]
+    router_own[...] = jnp.zeros_like(router_own)
+    router_own[:, 0 : sz.router_rows] = w_router_ref[...]
+    cot_block[own_block] = jnp.concatenate(
+        [cot_ref[...].astype(F32), jnp.zeros((pad - sz.rows, width), F32)], 0
+    ).astype(BF16)
+
+    at.enter()
+
+    w_rows = rows_at(d * nz + z, rp)
+    w_z = [
+        remote(w_own, w_full.at[:, w_rows, own_columns], wz_s.at[j - 1], wz_r.at[j - 1], at.line(at.next_z(j)))
+        for j in range(1, nz)
+    ]
+    for copy in w_z:
+        copy.start()
+    loads = [
+        pltpu.make_async_copy(first_hbm, first, local_sem.at[0]),
+        pltpu.make_async_copy(second_hbm, second, local_sem.at[1]),
+    ]
+    for copy in loads:
+        copy.start()
+    routers = [
+        remote(router_own, router_full.at[me], r_s.at[k - 1], r_r.at[k - 1], at.plane(at.next_group(k)))
+        for k in range(1, ng)
+    ]
+    for copy in routers:
+        copy.start()
+    w_full[:, w_rows, own_columns] = w_own[...]
+    router_full[me] = router_own[...]
+
+    zeros = jnp.zeros((pad - sz.rows, width), F32)
+    x_rows = jnp.concatenate([x_ref[...].astype(F32), zeros], 0)
+    unit_one, _ = normalize(x_rows)
+    normed_one = (unit_one * gain_one_ref[...]).astype(BF16)
+
+    for copy in w_z:
+        copy.wait()
+
+    def to_core(i, dp, other):
+        place = w_full.at[:, rows_at(dp, band), own_columns]
+        return remote(place, place, wc_s.at[i], wc_r.at[i], (d, (h + other) % nh, z))
+
+    w_band = w_full.at[:, rows_at(d, band), own_columns]
+    w_x = [
+        remote(w_band, w_band, wx_s.at[k - 1], wx_r.at[k - 1], ((d + k) % nd, h, z)) for k in range(1, nd)
+    ]
+    for copy in w_x:
+        copy.start()
+    w_c = [to_core((other - 1) * nd, d, other) for other in range(1, nh)]
+    for copy in w_c:
+        copy.start()
+
+    def along(block, send_sems, recv_sems, c):
+        place = block.at[own_block, lanes(c)]
+        return [
+            remote(place, place, send_sems.at[c, j - 1], recv_sems.at[c, j - 1], at.line(at.next_z(j)))
+            for j in range(1, nz)
+        ]
+
+    for c in range(parts):
+        for copy in along(cot_block, qz_s, qz_r, c):
+            copy.start()
+
+    route_table(sz, routes_ref, route_rows)
+    route_a, route_b = route_rows[0:1, :], route_rows[1:2, :]
+    expert = iota((sz.experts, sz.block), 0).astype(F32)
+    named_a, named_b = route_a == expert, route_b == expert
+    named = jnp.logical_or(named_a, named_b)
+    before = (iota((sz.block, sz.block), 0) < iota((sz.block, sz.block), 1)).astype(BF16)
+    rank = nn(named.astype(BF16), before) + expert * float(sz.cap)
+    slot_a = jnp.sum(jnp.where(named_a, rank, 0.0), 0, keepdims=True)
+    slot_b = jnp.sum(jnp.where(named_b, rank, 0.0), 0, keepdims=True)
+    slot_a = jnp.where(route_a < 0.0, -1.0, slot_a)
+    slot_b = jnp.where(route_b < 0.0, -1.0, slot_b)
+    slot_pair = jnp.concatenate([slot_a, slot_b] * 64, 0)
+    route_columns[...] = slot_pair.T
+
+    def fill(g, carry):
+        slot = iota((sz.group_slots, sz.block), 0).astype(F32) + (g * sz.group_slots).astype(F32)
+        hit = jnp.logical_or(slot == slot_a, slot == slot_b)
+        select[rows_at(g, sz.group_slots), :] = jnp.where(hit, 1.0, 0.0).astype(BF16)
+        return carry
+
+    lax.fori_loop(0, ng, fill, 0)
+
+    def dispatch(c, block, send, out):
+        def step(g, carry):
+            send[g, :, lanes(c)] = nn(select[rows_at(g, sz.group_slots), :], block[:, lanes(c)]).astype(BF16)
+            return carry
+
+        lax.fori_loop(0, ng, step, 0)
+        out[me, :, lanes(c)] = send[me, :, lanes(c)]
+
+    def exchange(c, k, send, out, send_sems, recv_sems):
+        g = (me + k) % ng
+        return remote(
+            send.at[g, :, lanes(c)], out.at[me, :, lanes(c)], send_sems.at[c, k], recv_sems.at[c, k], at.plane(g)
+        )
+
+    def start_part(c, *flow):
+        def step(i, carry):
+            exchange(c, ng - 1 - i, *flow).start()
+            return carry
+
+        lax.fori_loop(0, ng - 1, step, 0)
+
+    def wait_part(c, *flow):
+        def step(i, carry):
+            exchange(c, i + 1, *flow).wait()
+            return carry
+
+        lax.fori_loop(0, ng - 1, step, 0)
+
+    cot_flow = (send_a, cot_slots, qa_s, qa_r)
+    row_flow = (send_b, slots, na_s, na_r)
+
+    def send_cot(c):
+        for copy in along(cot_block, qz_s, qz_r, c):
+            copy.wait()
+        dispatch(c, cot_block, send_a, cot_slots)
+
+    send_cot(0)
+    for k in range(1, nd):
+        w_x[k - 1].wait_recv()
+        for other in range(1, nh):
+            copy = to_core((other - 1) * nd + k, (d - k + nd) % nd, other)
+            copy.start()
+            w_c.append(copy)
+    start_part(0, *cot_flow)
+    for copy in w_c:
+        copy.wait()
+    for copy in w_x:
+        copy.wait_send()
+
+    for i in range(3):
+        qkv[i] = nn(normed_one, w_full[i]).astype(BF16)
+    lane = iota((1, 2 * HEAD_DIM), 1)
+    halves = (lane < HEAD_DIM, lane >= HEAD_DIM)
+    key_valid = iota((1, pad), 1) < sz.rows
+    row_valid = iota((pad, 1), 0) < sz.rows
+    peak_lane = iota((1, 128), 1)
+    peak_at[...] = jnp.full_like(peak_at, NEG)
+    scale = HEAD_DIM ** (-0.5)
+
+    def attend(pair, carry):
+        columns = rows_at(pair, 2 * HEAD_DIM)
+        q_pair, k_pair, v_pair = (qkv[i, :, columns] for i in range(3))
+        sides = []
+        for side in range(2):
+            q_own = jnp.where(halves[side], q_pair, jnp.zeros_like(q_pair))
+            scores = jnp.where(key_valid, nt(q_own, k_pair) * scale, NEG)
+            row_peak = jnp.max(scores, -1, keepdims=True)
+            exponent = jnp.exp(scores - row_peak)
+            weights = (exponent / jnp.sum(exponent, -1, keepdims=True)).astype(BF16)
+            head = pair * 2 + side
+            probs[head] = weights
+            sides.append(nn(weights, v_pair))
+            peak = jnp.max(jnp.where(row_valid, row_peak, NEG), 0, keepdims=True)
+            peak_at[0:1, :] = jnp.where(peak_lane == head, peak, peak_at[0:1, :])
+        mixed[:, columns] = jnp.where(halves[0], sides[0], sides[1]).astype(BF16)
+        return carry
+
+    pairs = HEADS // 2
+    sent = 1
+    for turn in range(2):
+        until = 1 + ((parts - 1) * (turn + 1)) // 2
+        for c in range(sent, until):
+            send_cot(c)
+            start_part(c, *cot_flow)
+        sent = until
+        lax.fori_loop(turn * pairs // 2, (turn + 1) * pairs // 2, attend, 0)
+
+    hidden = x_rows + nt(mixed[...], w_full[3])
+    hidden_at[...] = hidden
+    unit_two, _ = normalize(hidden)
+    rows_block[own_block] = jnp.where(row_valid, unit_two * gain_two_ref[...], 0.0).astype(BF16)
+    for c in range(parts):
+        for copy in along(rows_block, nz_s, nz_r, c):
+            copy.start()
+
+    def fill_t(i, carry):
+        rows = rows_at(i, pad)
+        slot = iota((pad, sz.slots), 1).astype(F32)
+        hit = jnp.logical_or(slot == route_columns[rows, 0:1], slot == route_columns[rows, 1:2])
+        select_t[rows, :] = jnp.where(hit, 1.0, 0.0).astype(BF16)
+        return carry
+
+    lax.fori_loop(0, nz, fill_t, 0)
+    for copy in routers:
+        copy.wait()
+    for g in range(ng):
+        router_t[:, g * sz.router_rows : (g + 1) * sz.router_rows] = router_full[g, :, 0 : sz.router_rows]
+
+    def expert_rows(ref, e):
+        return ref[:, rows_at(e, sz.cap), :].reshape(many, width)
+
+    def cot_grad(e, carry):
+        grad_act[e] = nt(expert_rows(cot_slots, e), second[e])
+        return carry
+
+    for c in range(parts):
+        for copy in along(rows_block, nz_s, nz_r, c):
+            copy.wait()
+        dispatch(c, rows_block, send_b, slots)
+        start_part(c, *row_flow)
+        if c == parts // 2 - 1:
+            for i in range(parts):
+                wait_part(i, *cot_flow)
+            for copy in loads:
+                copy.wait()
+            lax.fori_loop(0, sz.own, cot_grad, 0)
+
+    logits = jnp.where(named, nt(router_t[...], rows_block[...]), NEG)
+    exponent = jnp.where(named, jnp.exp(logits - jnp.max(logits, 0, keepdims=True)), 0.0)
+    total = jnp.sum(exponent, 0, keepdims=True)
+    gates = exponent / jnp.where(total > 0.0, total, 1.0)
+    gates_at[...] = gates
+    by_slot = nt(split_high_low(gates), select[...])
+    by_slot = by_slot[0 : sz.experts] + by_slot[sz.experts :]
+    own_slot = iota((sz.experts, sz.slots), 1) // sz.cap == iota((sz.experts, sz.slots), 0)
+    by_slot = jnp.where(own_slot, by_slot, 0.0)
+    folded = by_slot[:, 0:128]
+    for i in range(1, sz.slots // 128):
+        folded = folded + by_slot[:, i * 128 : (i + 1) * 128]
+    gate_send[...] = folded
+    gate_copies = [
+        remote(gate_send, gate_recv.at[me], ga_s.at[k - 1], ga_r.at[k - 1], at.plane(at.next_group(k)))
+        for k in range(1, ng)
+    ]
+    for copy in gate_copies:
+        copy.start()
+    gate_recv[me] = folded
+    for copy in gate_copies:
+        copy.wait()
+    for c in range(parts):
+        wait_part(c, *row_flow)
+
+    def gate_of(e):
+        turned = gate_recv[:, pl.ds(me * sz.own + e, 1), :].reshape(ng, 128).T
+        columns = jnp.where((e % 2) == 1, turned[sz.cap : 2 * sz.cap], turned[0 : sz.cap])
+        return jnp.concatenate([columns[:, s : s + 1] for s in range(ng)], 0)
+
+    def first_piece(e, k):
+        g = (me + k) % ng
+        piece = (rows_at(e, sz.cap), lanes(0))
+        return remote(
+            send_a.at[(g, *piece)], grad_slots.at[(me, *piece)], d0_s.at[e, k], d0_r.at[e, k], at.plane(g)
+        )
+
+    def expert_back(e, carry):
+        gate = gate_of(e)
+        half_rows = many // 2
+        for part_at in range(2):
+            some = slice(part_at * half_rows, (part_at + 1) * half_rows)
+            groups = slice(part_at * ng // 2, (part_at + 1) * ng // 2)
+            pre = nn(slots[groups, rows_at(e, sz.cap), :].reshape(half_rows, width), first[e])
+            const, cubic = 0.7978845608028654, 0.044715
+            square = pre * pre
+            bent = jnp.tanh(const * pre * (1.0 + cubic * square))
+            half = 0.5 * (1.0 + bent)
+            act[e, some] = (pre * half).astype(BF16)
+            slope = half + 0.5 * pre * (1.0 - bent * bent) * const * (1.0 + 3.0 * cubic * square)
+            grads = (grad_act[e, some] * gate[some] * slope).astype(BF16)
+            grad_pre[e, some] = grads
+            send_a[groups, rows_at(e, sz.cap), :] = (
+                nt(grads, first[e]).astype(BF16).reshape(ng // 2, sz.cap, width)
+            )
+
+        def step(i, carry):
+            first_piece(e, ng - 1 - i).start()
+            return carry
+
+        lax.fori_loop(0, ng - 1, step, 0)
+        return carry
+
+    lax.fori_loop(0, sz.own, expert_back, 0)
+    grad_flow = (send_a, grad_slots, da_s, da_r)
+    value_flow = (send_b, values, va_s, va_r)
+    for c in range(1, parts):
+        start_part(c, *grad_flow)
+    grad_slots[me] = send_a[me]
+
+    dgate_send[...] = jnp.zeros_like(dgate_send)
+
+    def expert_value(e, carry):
+        value = nn(act[e], second[e])
+        send_b[:, rows_at(e, sz.cap), :] = (value * gate_of(e)).astype(BF16).reshape(ng, sz.cap, width)
+        product = (value * expert_rows(cot_slots, e).astype(F32)).astype(BF16)
+        dgate = nt(jnp.ones((8, width), BF16), product)
+        dgate_send[...] = jnp.where(iota((8, many), 0) == e, dgate, dgate_send[...])
+        return carry
+
+    lax.fori_loop(0, sz.own, expert_value, 0)
+    values[me] = send_b[me]
+    dgates = [
+        remote(dgate_send, dgate_recv.at[me], dg_s.at[k - 1], dg_r.at[k - 1], at.plane(at.next_group(k)))
+        for k in range(1, ng)
+    ]
+    for copy in dgates:
+        copy.start()
+    dgate_recv[me] = dgate_send[...]
+
+    def weight_grads(e, carry):
+        grad_value = (expert_rows(cot_slots, e).astype(F32) * gate_of(e)).astype(BF16)
+        grad_second[e] = tn(act[e], grad_value).astype(BF16)
+        grad_first[e] = tn(expert_rows(slots, e), grad_pre[e]).astype(BF16)
+        return carry
+
+    for copy in dgates:
+        copy.wait()
+    mine = iota((8, many), 1) // sz.cap == me
+    for g in range(ng):
+        masked = jnp.where(mine, dgate_recv[g], 0.0)
+        folded = masked[:, 0:128]
+        for i in range(1, many // 128):
+            folded = folded + masked[:, i * 128 : (i + 1) * 128]
+        folded = folded + pltpu.roll(folded, 64, 1)
+        dgate_rows[g * sz.own : (g + 1) * sz.own, :] = folded[0 : sz.own]
+    spread = jnp.concatenate([dgate_rows[...]] * (sz.slots // 128), 1)
+    own_slot = iota((sz.experts, sz.slots), 1) // sz.cap == iota((sz.experts, sz.slots), 0)
+    dgate = nt(split_high_low(jnp.where(own_slot, spread, 0.0)), select_t[...])
+    dgate = dgate[0 : sz.experts] + dgate[sz.experts :]
+    gates = gates_at[...]
+    dlogits = (gates * (dgate - jnp.sum(gates * dgate, 0, keepdims=True))).astype(BF16)
+    rt[...] = nn(dlogits, rows_block[...])
+    part[...] = tn(dlogits, router_t[...])
+
+    def line_copy(c, j, send, recv, send_sems, recv_sems):
+        return remote(
+            send.at[j - 1, :, lanes(c)], recv.at[j - 1, :, lanes(c)], send_sems.at[c, j - 1], recv_sems.at[c, j - 1],
+            at.line(at.next_z(j)),
+        )
+
+    def scatter(c, source, base, own, *flow):
+        flat = source[:, :, lanes(c)].reshape(sz.slots, part_width)
+        for j in [*range(1, nz), 0]:
+            tokens = rows_at(at.next_z(j), pad)
+            sums = nn(select_t[tokens, :], flat)
+            if base is not None:
+                sums = sums + base[tokens, lanes(c)]
+            if j == 0:
+                own[:, lanes(c)] = sums
+            else:
+                flow[0][j - 1, :, lanes(c)] = sums.astype(BF16)
+                line_copy(c, j, *flow).start()
+
+    def gathered(own, *flow):
+        for c in range(parts):
+            for j in range(1, nz):
+                line_copy(c, j, *flow).wait()
+        sums = own[...]
+        for j in range(1, nz):
+            sums = sums + flow[1][j - 1].astype(F32)
+        return sums
+
+    part_flow = (part_send, part_recv, pz_s, pz_r)
+    mix_flow = (mix_send, mix_recv, mz_s, mz_r)
+
+    def wait_first(e, carry):
+        def step(i, carry):
+            first_piece(e, i + 1).wait()
+            return carry
+
+        return lax.fori_loop(0, ng - 1, step, carry)
+
+    done = 0
+    for c in range(parts):
+        if c == 0:
+            lax.fori_loop(0, sz.own, wait_first, 0)
+        else:
+            wait_part(c, *grad_flow)
+        if c == parts - 1:
+            for i in range(parts):
+                start_part(i, *value_flow)
+        scatter(c, grad_slots, part, part_own, *part_flow)
+        until = sz.own * (c + 1) // parts
+        lax.fori_loop(done, until, weight_grads, 0)
+        done = until
+    stores = [
+        pltpu.make_async_copy(grad_first, grad_first_out, local_sem.at[2]),
+        pltpu.make_async_copy(grad_second, grad_second_out, local_sem.at[3]),
+    ]
+    for copy in stores:
+        copy.start()
+
+    unit_two, factor_two = normalize(hidden_at[...])
+    grad_normed = jnp.where(row_valid, gathered(part_own, *part_flow), 0.0)
+    grad_hidden, gain_two = norm_back(grad_normed, unit_two, factor_two, gain_two_ref[...])
+    grad_hidden = jnp.concatenate([cot_ref[...].astype(F32), zeros], 0) + jnp.where(row_valid, grad_hidden, 0.0)
+    part_own[...] = grad_hidden
+    grad_attn = grad_hidden.astype(BF16)
+
+    def core_copy(i, other):
+        n = 4 * (other - 1) + i
+        return remote(
+            core_send.at[other - 1, i], core_recv.at[other - 1, i], gc_s.at[n], gc_r.at[n], (d, (h + other) % nh, z)
+        )
+
+    def half_sum(i, sums):
+        for other in range(1, nh):
+            core_copy(i, other).wait()
+            sums = sums + core_recv[other - 1, i].astype(F32)
+        w_half[i] = sums
+        band_send[i] = sums.astype(BF16)
+
+    def band_copy(k, matrices, n):
+        to = (d + k) % nd
+        n = 2 * (k - 1) + n
+        return remote(
+            band_send.at[matrices, rows_at(to, band), :], band_recv.at[k - 1, matrices], gx_s.at[n], gx_r.at[n], (to, h, z)
+        )
+
+    for other in [*range(1, nh), 0]:
+        sums = tn(grad_attn, mixed[:, rows_at((h + other) % nh, cp)])
+        if other:
+            core_send[other - 1, 3] = sums.astype(BF16)
+            core_copy(3, other).start()
+        else:
+            w_half[3] = sums
+    grad_mixed[...] = nn(grad_attn, w_full[3]).astype(BF16)
+    half_sum(3, w_half[3])
+    out_band = [band_copy(k, pl.ds(3, 1), 0) for k in range(1, nd)]
+    for copy in out_band:
+        copy.start()
+
+    def attend_back(pair):
+        columns = rows_at(pair, 2 * HEAD_DIM)
+        q_pair, k_pair, v_pair = (qkv[i, :, columns] for i in range(3))
+        g_pair = grad_mixed[:, columns]
+        dq, dk, dv = [], [], []
+        for side in range(2):
+            weights = probs[pair * 2 + side]
+            soft = weights.astype(F32)
+            g_own = jnp.where(halves[side], g_pair, jnp.zeros_like(g_pair))
+            grad_soft = nt(g_own, v_pair)
+            inner = jnp.sum(soft * grad_soft, -1, keepdims=True)
+            grad_scores = (soft * (grad_soft - inner)).astype(BF16)
+            dq.append(nn(grad_scores, k_pair))
+            dk.append(tn(grad_scores, q_pair))
+            dv.append(tn(weights, g_pair))
+        grad_qkv[0, :, columns] = (jnp.where(halves[0], dq[0], dq[1]) * scale).astype(BF16)
+        grad_qkv[1, :, columns] = (jnp.where(halves[0], dk[0], dk[1]) * scale).astype(BF16)
+        grad_qkv[2, :, columns] = jnp.where(halves[0], dv[0], dv[1]).astype(BF16)
+
+    unit_one, factor_one = normalize(jnp.concatenate([x_ref[...].astype(F32), zeros], 0))
+    normed_one = (unit_one * gain_one_ref[...]).astype(BF16)
+    core_pairs = cp // (2 * HEAD_DIM)
+    turns, mixed_parts = nh * core_pairs, 0
+    turn = 0
+    for other in [*range(1, nh), 0]:
+        core = (h + other) % nh
+        for q in range(core_pairs):
+            attend_back(core * core_pairs + q)
+            turn += 1
+            if turn < turns:
+                until = parts * turn // turns
+                for c in range(mixed_parts, until):
+                    wait_part(c, *value_flow)
+                    scatter(c, values, None, mix_own, *mix_flow)
+                mixed_parts = until
+        for i in range(3):
+            sums = tn(normed_one, grad_qkv[i, :, rows_at(core, cp)])
+            if other:
+                core_send[other - 1, i] = sums.astype(BF16)
+                core_copy(i, other).start()
+            else:
+                half_sum(i, sums)
+    qkv_band = [band_copy(k, pl.ds(0, 3), 1) for k in range(1, nd)]
+    for copy in qkv_band:
+        copy.start()
+
+    grad_one = jnp.zeros((pad, width), F32)
+    for i in range(3):
+        grad_one = grad_one + nt(grad_qkv[i], w_full[i])
+    grad_one = jnp.where(row_valid, grad_one, 0.0)
+    grad_input, gain_one = norm_back(grad_one, unit_one, factor_one, gain_one_ref[...])
+    grad_input_out[...] = (part_own[...] + grad_input)[0 : sz.rows].astype(BF16)
+
+    small[...] = jnp.zeros_like(small)
+    small[0:1, :] = gain_one
+    small[1:2, :] = gain_two
+    small[2:3, 0:128] = peak_at[0:1, :]
+    peak_row = iota(small.shape, 0) == 2
+
+    def join(a, b):
+        return jnp.where(peak_row, jnp.maximum(a, b), a + b)
+
+    small_copies = []
+    for other in range(1, nh):
+        device, n = (d, (h + other) % nh, z), 2 * (other - 1)
+        small_copies += [
+            remote(small, small_core.at[other - 1], sc_s.at[n], sc_r.at[n], device),
+            remote(rt, rt_core.at[other - 1], sc_s.at[n + 1], sc_r.at[n + 1], device),
+        ]
+    for copy in small_copies:
+        copy.start()
+    for copy in small_copies:
+        copy.wait()
+    for other in range(1, nh):
+        small[...] = join(small[...], small_core[other - 1])
+        rt[...] = rt[...] + rt_core[other - 1]
+    small_send[0] = small[...]
+    small_copies = []
+    for k in range(1, nd):
+        to, n = (d + k) % nd, 2 * (k - 1)
+        small_copies += [
+            remote(small_send.at[0], small_x.at[k - 1], sx_s.at[n], sx_r.at[n], (to, h, z)),
+            remote(rt.at[:, rows_at(to, band)], rt_x.at[k - 1], sx_s.at[n + 1], sx_r.at[n + 1], (to, h, z)),
+        ]
+    for copy in small_copies:
+        copy.start()
+
+    for c in range(mixed_parts, parts):
+        wait_part(c, *value_flow)
+        scatter(c, values, None, mix_own, *mix_flow)
+
+    for copy in small_copies:
+        copy.wait()
+    router_sum = rt[:, rows_at(d, band)]
+    for k in range(1, nd):
+        small[...] = join(small[...], small_x[k - 1])
+        router_sum = router_sum + rt_x[k - 1]
+    rt_z[nz - 1] = router_sum
+    small_send[1] = small[...]
+    for copy in out_band:
+        copy.wait()
+    for copy in qkv_band:
+        copy.wait()
+    for i in range(4):
+        sums = w_half[i, rows_at(d, band), :]
+        for k in range(1, nd):
+            sums = sums + band_recv[k - 1, i].astype(F32)
+        w_half[i, 0:band, :] = sums
+        line_send[i] = sums.astype(BF16)
+    z_copies = []
+    for j in range(1, nz):
+        to, n = at.next_z(j), 3 * (j - 1)
+        device = at.line(to)
+        z_copies += [
+            remote(line_send.at[:, rows_at(to, rp), :], line_recv.at[j - 1], gl_s.at[n], gl_r.at[n], device),
+            remote(small_send.at[1], small_z.at[j - 1], gl_s.at[n + 1], gl_r.at[n + 1], device),
+            remote(rt_z.at[nz - 1], rt_z.at[j - 1], gl_s.at[n + 2], gl_r.at[n + 2], device),
+        ]
+    for copy in z_copies:
+        copy.start()
+
+    mix = gathered(mix_own, *mix_flow)
+    output_out[...] = (hidden_at[...] + mix)[0 : sz.rows].astype(BF16)
+
+    for copy in z_copies:
+        copy.wait()
+    totals = small[...]
+    router_sum = rt_z[nz - 1]
+    for j in range(1, nz):
+        totals = join(totals, small_z[j - 1])
+        router_sum = router_sum + rt_z[j - 1]
+    small_out[...] = totals
+    router_out[...] = router_sum
+    for i in range(4):
+        sums = w_half[i, rows_at(z, rp), :]
+        for j in range(1, nz):
+            sums = sums + line_recv[j - 1, i].astype(F32)
+        weight_out[i] = sums
+    for copy in stores:
+        copy.wait()
+
+
+def finish_kernel(
+    sz, output_ref, grad_input_ref, small_ref, weight_ref, router_ref, grad_first_ref, grad_second_ref, tau_ref, w_qkv_ref,
+    output, grad_input, gain_one, gain_two, grad_qkv, grad_out, grad_router, grad_first, grad_second, clipped,
+):
+    grad_first[...] = grad_first_ref[...].astype(F32)
+    grad_second[...] = grad_second_ref[...].astype(F32)
+
+    @pl.when(pl.program_id(0) == 0)
+    def _():
+        h = lax.axis_index("heads")
+        cp, rr = sz.col_piece, sz.router_rows
+        output[...] = output_ref[...]
+        grad_input[...] = grad_input_ref[...]
+        gain_one[...] = small_ref[0:1, :]
+        gain_two[...] = small_ref[1:2, :]
+        grad_qkv[...] = weight_ref[0:3]
+        grad_out[...] = weight_ref[3]
+        piece = router_ref[:, 0:rr]
+        for i in range(1, sz.nh):
+            piece = jnp.where(h == i, router_ref[:, i * rr : (i + 1) * rr], piece)
+        grad_router[...] = piece
+        tau = tau_ref[...]
+        factor = jnp.sqrt(tau / jnp.maximum(small_ref[2:3, 0:HEADS], tau))
+        column = iota((1, cp), 1) // HEAD_DIM + h * (cp // HEAD_DIM)
+        scale_row = jnp.zeros((1, cp), F32)
+        for head in range(HEADS):
+            scale_row = jnp.where(column == head, factor[:, head : head + 1], scale_row)
+        for i in range(2):
+            clipped[i] = (w_qkv_ref[i].astype(F32) * scale_row).astype(BF16)
+
+
+def fast_body(
+    sz, inputs, cotangent, routes, gain_attn, gain_expert, tau, w_qkv, w_out_attn, w_router, w_in, w_out
+):
+    ng, nz, nd, nh, pad, width, own = sz.groups, sz.nt, sz.nd, sz.nh, sz.pad, sz.width, sz.own
+    rp, cp, band, parts, block = sz.row_piece, sz.col_piece, sz.band, sz.parts, sz.block
+    many, hidden = ng * sz.cap, sz.hidden
+    on_chip, anywhere = pl.BlockSpec(memory_space=pltpu.VMEM), pl.BlockSpec(memory_space=pl.ANY)
+
+    def shape(dims, dtype):
+        return jax.ShapeDtypeStruct(dims, dtype)
+
+    def half(*dims):
+        return pltpu.VMEM(dims, BF16)
+
+    def full(*dims):
+        return pltpu.VMEM(dims, F32)
+
+    def pair(*dims):
+        return [pltpu.SemaphoreType.DMA(dims)] * 2
+
+    slot_buffer = half(ng, sz.group_slots, width)
+    line_buffer = half(nz - 1, pad, width)
+    packed = pl.pallas_call(
+        functools.partial(block_kernel, sz),
+        out_shape=(
+            shape(inputs.shape, BF16), shape(inputs.shape, BF16), shape((8, width), F32), shape((4, rp, cp), F32),
+            shape((sz.experts, band), F32), shape(w_in.shape, BF16), shape(w_out.shape, BF16),
+        ),
+        in_specs=[on_chip] * 8 + [anywhere] * 2,
+        out_specs=(on_chip,) * 5 + (anywhere,) * 2,
+        scratch_shapes=[
+            half(4, rp, cp), half(4, width, width), half(sz.experts, 128), half(ng, sz.experts, 128),
+            half(sz.experts, width), full(8, block), full(block, 128), half(sz.slots, block), half(block, sz.slots),
+            half(block, width), half(block, width), *[slot_buffer] * 6,
+            half(own, width, hidden), half(own, hidden, width), half(own, many, hidden), half(own, many, hidden),
+            full(own, many, hidden), half(own, width, hidden), half(own, hidden, width),
+            full(sz.experts, 128), full(ng, sz.experts, 128), full(sz.experts, block), full(8, many),
+            full(ng, 8, many), full(sz.experts, 128),
+            half(3, pad, width), half(HEADS, pad, pad), half(pad, width), full(pad, width), full(8, 128),
+            full(block, width), full(pad, width), line_buffer, line_buffer, full(pad, width), line_buffer, line_buffer,
+            half(pad, width), half(3, pad, width), half(nh - 1, 4, width, cp), half(nh - 1, 4, width, cp),
+            full(4, width, cp), half(4, width, cp), half(nd - 1, 4, band, cp), half(4, band, cp),
+            half(nz - 1, 4, rp, cp),
+            full(8, width), full(2, 8, width), full(nh - 1, 8, width), full(nd - 1, 8, width), full(nz - 1, 8, width),
+            full(sz.experts, width), full(nh - 1, sz.experts, width), full(nd - 1, sz.experts, band),
+            full(nz, sz.experts, band),
+            *pair(nz - 1), *pair(nd - 1), *pair(nd * (nh - 1)), *pair(ng - 1), *pair(parts, nz - 1),
+            *pair(parts, nz - 1), *pair(parts, ng), *pair(parts, ng), *pair(ng - 1), *pair(own, ng), *pair(parts, ng),
+            *pair(parts, ng), *pair(ng - 1), *pair(parts, nz - 1), *pair(parts, nz - 1), *pair(4 * (nh - 1)),
+            *pair(2 * (nd - 1)), *pair(3 * (nz - 1)), *pair(2 * (nh - 1)), *pair(2 * (nd - 1)),
+            *pair(1), pltpu.SemaphoreType.DMA((4,)),
+        ],
+        compiler_params=pltpu.CompilerParams(collective_id=0, has_side_effects=True, vmem_limit_bytes=62 * 2**20),
+        name="block",
+    )(
+        inputs, cotangent, routes.T, gain_attn[None, :], gain_expert[None, :], w_qkv, w_out_attn.T, w_router.T,
+        w_in, w_out,
+    )
+
+    rr = sz.router_rows
+
+    def same(*dims):
+        return pl.BlockSpec(dims, lambda e: (0,) * len(dims))
+
+    first_spec = pl.BlockSpec((1, width, hidden), lambda e: (e, 0, 0))
+    second_spec = pl.BlockSpec((1, hidden, width), lambda e: (e, 0, 0))
+    results = (
+        shape(inputs.shape, BF16), shape(inputs.shape, BF16), shape((1, width), F32), shape((1, width), F32),
+        shape((3, rp, cp), F32), shape((rp, cp), F32), shape((sz.experts, rr), F32), shape(w_in.shape, F32),
+        shape(w_out.shape, F32), shape((2, rp, cp), BF16),
+    )
+    output, grad_input, gain_one, gain_two, grad_qkv, grad_out, grad_router, grad_first, grad_second, clipped = (
+        pl.pallas_call(
+            functools.partial(finish_kernel, sz),
+            grid=(own,),
+            out_shape=results,
+            in_specs=[same(*p.shape) for p in packed[:5]]
+            + [first_spec, second_spec, same(1, HEADS), same(*w_qkv.shape)],
+            out_specs=[
+                {7: first_spec, 8: second_spec}.get(i, same(*r.shape)) for i, r in enumerate(results)
+            ],
+            name="finish",
+        )(*packed, tau[None, :], w_qkv)
+    )
+    return (
+        output, grad_input, gain_one[0], gain_two[0], grad_qkv, grad_out.T, grad_router.T, grad_first, grad_second,
+        clipped,
+    )
 
 
 def gelu_tanh(inputs):
@@ -16,20 +857,15 @@
     )
 
 
-def normalize(inputs):
+def unit_and_factor(inputs):
     centered = inputs - jnp.mean(inputs, -1, keepdims=True)
     factor = lax.rsqrt(jnp.mean(centered * centered, -1, keepdims=True) + 1e-06)
     return (centered * factor, factor)
 
 
-def norm_back(grad_norm, unit_rows, factor, gain):
-    grad_hat = grad_norm * gain
-    inner_sum = (
-        grad_hat
-        - jnp.mean(grad_hat, -1, keepdims=True)
-        - unit_rows * jnp.mean(grad_hat * unit_rows, -1, keepdims=True)
-    )
-    return (factor * inner_sum, jnp.sum(grad_norm * unit_rows, 0))
+def general_norm_back(grad_norm, unit_rows, factor, gain):
+    grad, gain_row = norm_back(grad_norm, unit_rows, factor, gain)
+    return grad, gain_row[0]
 
 
 def attn_forward(block_parts):
@@ -77,7 +913,7 @@
     return (grad_query, grad_key, grad_value)
 
 
-def body(
+def general_body(
     inputs, cotangent, routes, gain_attn, gain_expert, tau, w_qkv, w_out_attn, w_router, w_in, w_out
 ):
     row_count, width = inputs.shape
@@ -89,7 +925,7 @@
     own_heads = col_piece // HEAD_DIM
     head_start = lax.axis_index("heads") * col_piece
     x_float = inputs.astype(jnp.float32)
-    unit_one, factor_one = normalize(x_float)
+    unit_one, factor_one = unit_and_factor(x_float)
     normed_one = (unit_one * gain_attn).astype(jnp.bfloat16)
     stack_qkv, stack_out = (
         lax.all_gather(w_qkv[None], ("dp", "heads", "tensor"), axis=0, tiled=True),
@@ -144,7 +980,7 @@
     peak_logit = lax.dynamic_slice_in_dim(
         peak_all, lax.axis_index("heads") * own_heads, own_heads, 0
     )
-    unit_two, factor_two = normalize(hidden)
+    unit_two, factor_two = unit_and_factor(hidden)
     normed_two = (unit_two * gain_expert).astype(jnp.bfloat16)
     group_rows, group_cot = (
         lax.all_gather(normed_two, "tensor", axis=0, tiled=True),
@@ -168,7 +1004,8 @@
     counts = jnp.sum(
         (flat_ids[:, None] == jnp.arange(experts, dtype=jnp.int32)[None, :]).astype(jnp.int32), 0
     )
-    starts = jnp.cumsum(counts) - counts
+    expert_ids = jnp.arange(experts, dtype=jnp.int32)
+    starts = jnp.sum(jnp.where(expert_ids[None, :] < expert_ids[:, None], counts[None, :], 0), 1)
     slot_rank = jnp.arange(2 * group_count, dtype=jnp.int32) - starts[sorted_ids]
     slot_table = (
         jnp.full((experts * capacity,), 2 * group_count, jnp.int32)
@@ -253,7 +1090,7 @@
     router_term = jnp.einsum(
         "rd,re->de", normed_two, grad_logits, preferred_element_type=jnp.float32
     )
-    grad_hidden_norm, gain_two_term = norm_back(grad_normed_two, unit_two, factor_two, gain_expert)
+    grad_hidden_norm, gain_two_term = general_norm_back(grad_normed_two, unit_two, factor_two, gain_expert)
     grad_hidden = cotangent.astype(jnp.float32) + grad_hidden_norm
     grad_attn = lax.all_gather(grad_hidden.astype(jnp.bfloat16), "heads", axis=0, tiled=True)
     grad_mixed = jnp.einsum(
@@ -303,7 +1140,7 @@
         lax.psum_scatter(send_qkv, ("dp", "heads", "tensor"), scatter_dimension=0, tiled=True),
         lax.psum_scatter(send_out, ("dp", "heads", "tensor"), scatter_dimension=0, tiled=True),
     )
-    grad_input_norm, gain_one_term = norm_back(grad_normed_one, unit_one, factor_one, gain_attn)
+    grad_input_norm, gain_one_term = general_norm_back(grad_normed_one, unit_one, factor_one, gain_attn)
     grad_input = (grad_hidden + grad_input_norm).astype(jnp.bfloat16)
     gain_one_grad, gain_two_grad, router_all = lax.psum(
         (gain_one_term, gain_two_term, router_term), ("dp", "heads", "tensor")
@@ -328,6 +1165,16 @@
         shard_second,
         clipped,
     )
+
+
+def body(*args):
+    inputs, _, routes, _, _, _, w_qkv, _, w_router, w_in, _ = args
+    sz = Sizes(
+        lax.axis_size("dp"), lax.axis_size("heads"), lax.axis_size("tensor"), inputs, routes, w_qkv, w_router, w_in
+    )
+    if sz.fits():
+        return fast_body(sz, *args)
+    return general_body(*args)
 
 
 def solution(mesh):

time: 1020 us -> 172 us (0.17)
  waiting for transfers between devices: 446 us -> 0 us
  blocking collectives: 247 us -> 0 us
  Pallas kernels: 0 us -> 171 us
  local copies, waits for them, and re-layouts: 117 us -> 0 us
  other arithmetic: 89.4 us -> 0 us
  matrix products: 78 us -> 0 us
  between operations: 18.1 us -> 0.83 us
  starting transfers between devices: 14.1 us -> 0 us
    reduce_scatter x4 -> x0, waiting for transfers between devices: 442 us -> none  [the longest x1 134 us: body(): lax.psum_scatter(send_out, ('dp', 'heads', 'tensor'), scatter_dimension=0...]
    pallas_call x0 -> x2, Pallas kernels: none -> 171 us  [the longest x1 164 us: fast_body(): pl.pallas_call(functools.partial(block_kernel, sz), out_shape=(shape(inpu...]
    all_gather x6 -> x0, blocking collectives: 124 us -> none  [the longest x1 75.6 us: body(): lax.all_gather(w_out_attn[None], ('dp', 'heads', 'tensor'), axis=0, tiled...]
    dot_general x21 -> x0, matrix products: 78 us -> none  [the longest x1 13.5 us: body(): jnp.einsum('ecf,edf->ecd', grad_pre, first_w, preferred_element_type=jnp....]
    gather x11 -> x0, local copies, waits for them, and re-layouts: 59.7 us -> none  [the longest x5 21 us: body(): chosen = jnp.take_along_axis(logits, routes, 1)]
    scatter-add x3 -> x0, other arithmetic: 44.2 us -> none  [the longest x1 14.9 us: body(): partial_value = jnp.zeros((group_count + 1, width), jnp.float32).at[slot_...]
    unnamed x3 -> x0, blocking collectives: 43.3 us -> none
    pmax x1 -> x0, blocking collectives: 40.2 us -> none  [body(): peak_all = lax.pmax(peak_full, ('dp', 'heads', 'tensor'))]
  transfers between devices with their start and end apart: 13 -> 0, of which waited for: 6 -> 0; matrix products, arithmetic and copies ran while one was open for 20% -> 0% of each run, Pallas kernels for 0% -> 0%
where the time goes in v2:
time: 172 us; the launch traced here: 171 us
  Pallas kernels  171 us (99%)
    pallas_call x1, Pallas kernels, fast_body(): pl.pallas_call(functools.partial(block_kernel, sz), out_shape=(shape(inpu...  164 us
    pallas_call x1, Pallas kernels, fast_body(): pl.pallas_call(functools.partial(finish_kernel, sz), grid=(own,), out_sha...  6.44 us

profile of v2, /device:TPU:0, one launch (start us, length us, event | category | flops | bytes accessed | tf_op | source)
XLA Modules:
  0.0 171.4 jit_solution(6201937305704667825)
XLA Ops:
  0.6 164.2 %block.1 = (bf16[197,512]{1,0:T(8,128)(2,1)}, bf16[197,512]{1,0:T(8,128)(2,1)}, f32[8,512]{1,0:T(8,128)}, f32[4,32,256]{2,1,0:T(8,128)}, f32[32,128]{1,0:T(8,128...) custom-call(bf16[197,512]{1,0:T(8,128)(2,1)} %x_ref.1, bf16[197,512]{1,0:T(8,128)(2,1)} %cot_ref.1, ...), custom_call_target="tpu_custom_call" | custom-call | tf_op jit(solution)/shard_map/block/pallas_call | solution.py:784
  164.8 6.4 %finish.1 = (bf16[197,512]{1,0:T(8,128)(2,1)}, bf16[197,512]{1,0:T(8,128)(2,1)}, f32[1,512]{1,0:T(1,128)}, f32[1,512]{1,0:T(1,128)}, f32[3,32,256]{2,1,0:T(8,128...) custom-call(bf16[197,512]{1,0:T(8,128)(2,1)} %get-tuple-element.27.o, ...), custom_call_target="tpu_custom_call" | custom-call | tf_op jit(solution)/shard_map/finish/pallas_call | solution.py:834

commit v3 on v2

--- a/solution.py
+++ b/solution.py
@@ -47,6 +47,11 @@
             and self.own * self.groups * 4 == 128
             and self.width == HEADS * HEAD_DIM
             and self.block * self.width * 2 <= 2**20
+            and self.own * self.width <= self.slots
+            and self.hidden <= self.block
+            and self.hidden == self.width
+            and self.cap % (16 * self.nt) == 0
+            and self.width // self.parts % 128 == 0
         )
 
 
@@ -131,18 +136,19 @@
 
 
 def block_kernel(
-    sz, x_ref, cot_ref, routes_ref, gain_one_ref, gain_two_ref, w_qkv_ref, w_out_ref, w_router_ref, first_hbm, second_hbm,
-    output_out, grad_input_out, small_out, weight_out, router_out, grad_first_out, grad_second_out,
-    w_own, w_full, router_own, router_full, router_t, route_rows, route_columns, select, select_t,
+    sz, x_ref, cot_ref, routes_ref, gain_one_ref, gain_two_ref, w_qkv_ref, w_out_ref, w_router_ref, tau_ref, first_hbm,
+    second_hbm, output_out, grad_input_out, gain_one_out, gain_two_out, qkv_out, out_out, router_out, clipped_out,
+    grad_first_out, grad_second_out,
+    w_own, w_full, router_own, router_full, router_t, route_rows, route_columns, select, select_t, select_qt,
     cot_block, rows_block, send_a, send_b, cot_slots, slots, grad_slots, values,
-    first, second, act, grad_pre, grad_act, grad_first, grad_second,
+    grads_q, grads_line, grads_sum, grads_back, first, second, act, grad_pre, grad_act, grad_second,
     gate_send, gate_recv, gates_at, dgate_send, dgate_recv, dgate_rows,
     qkv, probs, mixed, hidden_at, peak_at, part, part_own, part_send, part_recv, mix_own, mix_send, mix_recv,
     grad_mixed, grad_qkv, core_send, core_recv, w_half, band_send, band_recv, line_send, line_recv,
     small, small_send, small_core, small_x, small_z, rt, rt_core, rt_x, rt_z,
     wz_s, wz_r, wx_s, wx_r, wc_s, wc_r, r_s, r_r, qz_s, qz_r, nz_s, nz_r, qa_s, qa_r, na_s, na_r, ga_s, ga_r,
     d0_s, d0_r, da_s, da_r, va_s, va_r, dg_s, dg_r, pz_s, pz_r, mz_s, mz_r, gc_s, gc_r, gx_s, gx_r, gl_s, gl_r,
-    sc_s, sc_r, sx_s, sx_r, sz_s, sz_r, local_sem,
+    sc_s, sc_r, sx_s, sx_r, dl_s, dl_r, dq_s, dq_r, local_sem,
 ):
     at = Place(sz)
     d, h, z, me = at.d, at.h, at.z, at.group
@@ -245,6 +251,17 @@
         return carry
 
     lax.fori_loop(0, ng, fill, 0)
+
+    quarter = sz.cap // nz
+    few = ng * sz.own * quarter
+
+    def quarter_slot(dims, axis):
+        n = iota(dims, axis)
+        return (n // quarter * sz.cap + z * quarter + n % quarter).astype(F32)
+
+    def quarter_move(k, send, landing, send_sems, recv_sems):
+        g = (me + k) % ng
+        return remote(send.at[g], landing.at[me], send_sems.at[k - 1], recv_sems.at[k - 1], at.plane(g))
 
     def dispatch(c, block, send, out):
         def step(g, carry):
@@ -346,6 +363,9 @@
         slot = iota((pad, sz.slots), 1).astype(F32)
         hit = jnp.logical_or(slot == route_columns[rows, 0:1], slot == route_columns[rows, 1:2])
         select_t[rows, :] = jnp.where(hit, 1.0, 0.0).astype(BF16)
+        some = quarter_slot((pad, few), 1)
+        hit = jnp.logical_or(some == route_columns[rows, 0:1], some == route_columns[rows, 1:2])
+        select_qt[rows, :] = jnp.where(hit, 1.0, 0.0).astype(BF16)
         return carry
 
     lax.fori_loop(0, nz, fill_t, 0)
@@ -387,27 +407,37 @@
         folded = folded + by_slot[:, i * 128 : (i + 1) * 128]
     gate_send[...] = folded
     gate_copies = [
-        remote(gate_send, gate_recv.at[me], ga_s.at[k - 1], ga_r.at[k - 1], at.plane(at.next_group(k)))
+        remote(
+            gate_send.at[rows_at(at.next_group(k) * sz.own // 8, 8)], gate_recv.at[me], ga_s.at[k - 1], ga_r.at[k - 1],
+            at.plane(at.next_group(k)),
+        )
         for k in range(1, ng)
     ]
     for copy in gate_copies:
         copy.start()
-    gate_recv[me] = folded
+    gate_recv[me] = gate_send[rows_at(me * sz.own // 8, 8)]
     for copy in gate_copies:
         copy.wait()
     for c in range(parts):
         wait_part(c, *row_flow)
 
     def gate_of(e):
-        turned = gate_recv[:, pl.ds(me * sz.own + e, 1), :].reshape(ng, 128).T
+        turned = gate_recv[:, pl.ds(me * sz.own % 8 + e, 1), :].reshape(ng, 128).T
         columns = jnp.where((e % 2) == 1, turned[sz.cap : 2 * sz.cap], turned[0 : sz.cap])
         return jnp.concatenate([columns[:, s : s + 1] for s in range(ng)], 0)
 
     def first_piece(e, k):
         g = (me + k) % ng
-        piece = (rows_at(e, sz.cap), lanes(0))
+        piece = (rows_at(e, sz.cap), lanes(1))
         return remote(
             send_a.at[(g, *piece)], grad_slots.at[(me, *piece)], d0_s.at[e, k], d0_r.at[e, k], at.plane(g)
+        )
+
+    def grads_piece(e, j):
+        piece = (slice(None), rows_at(e, quarter), slice(None))
+        return remote(
+            grads_q.at[(at.next_z(j), *piece)], grads_line.at[(j - 1, *piece)], dl_s.at[e, j - 1], dl_r.at[e, j - 1],
+            at.line(at.next_z(j)),
         )
 
     def expert_back(e, carry):
@@ -421,62 +451,77 @@
             square = pre * pre
             bent = jnp.tanh(const * pre * (1.0 + cubic * square))
             half = 0.5 * (1.0 + bent)
-            act[e, some] = (pre * half).astype(BF16)
+            hidden_units = (pre * half).astype(BF16)
+            act[e, some] = hidden_units
             slope = half + 0.5 * pre * (1.0 - bent * bent) * const * (1.0 + 3.0 * cubic * square)
-            grads = (grad_act[e, some] * gate[some] * slope).astype(BF16)
+            through = grad_act[e, some]
+            dgate = nt(jnp.ones((8, sz.hidden), BF16), (hidden_units.astype(F32) * through).astype(BF16))
+            dgate_send[:, some] = jnp.where(iota((8, half_rows), 0) == e, dgate, dgate_send[:, some])
+            grads = (through * gate[some] * slope).astype(BF16)
             grad_pre[e, some] = grads
-            send_a[groups, rows_at(e, sz.cap), :] = (
-                nt(grads, first[e]).astype(BF16).reshape(ng // 2, sz.cap, width)
-            )
+            spread = nt(grads, first[e]).astype(BF16).reshape(ng // 2, sz.cap, width)
+            send_a[groups, rows_at(e, sz.cap), :] = spread
+            for i in range(nz):
+                grads_q[i, groups, rows_at(e, quarter), :] = spread[:, i * quarter : (i + 1) * quarter, 0:part_width]
 
         def step(i, carry):
             first_piece(e, ng - 1 - i).start()
             return carry
 
         lax.fori_loop(0, ng - 1, step, 0)
+        for j in range(1, nz):
+            grads_piece(e, j).start()
         return carry
 
+    dgate_send[...] = jnp.zeros_like(dgate_send)
     lax.fori_loop(0, sz.own, expert_back, 0)
-    grad_flow = (send_a, grad_slots, da_s, da_r)
-    value_flow = (send_b, values, va_s, va_r)
-    for c in range(1, parts):
-        start_part(c, *grad_flow)
-    grad_slots[me] = send_a[me]
-
-    dgate_send[...] = jnp.zeros_like(dgate_send)
-
-    def expert_value(e, carry):
-        value = nn(act[e], second[e])
-        send_b[:, rows_at(e, sz.cap), :] = (value * gate_of(e)).astype(BF16).reshape(ng, sz.cap, width)
-        product = (value * expert_rows(cot_slots, e).astype(F32)).astype(BF16)
-        dgate = nt(jnp.ones((8, width), BF16), product)
-        dgate_send[...] = jnp.where(iota((8, many), 0) == e, dgate, dgate_send[...])
-        return carry
-
-    lax.fori_loop(0, sz.own, expert_value, 0)
-    values[me] = send_b[me]
     dgates = [
-        remote(dgate_send, dgate_recv.at[me], dg_s.at[k - 1], dg_r.at[k - 1], at.plane(at.next_group(k)))
+        remote(
+            dgate_send.at[:, rows_at(at.next_group(k) * sz.cap // 128, 128)], dgate_recv.at[me], dg_s.at[k - 1],
+            dg_r.at[k - 1], at.plane(at.next_group(k)),
+        )
         for k in range(1, ng)
     ]
     for copy in dgates:
         copy.start()
-    dgate_recv[me] = dgate_send[...]
+    dgate_recv[me] = dgate_send[:, rows_at(me * sz.cap // 128, 128)]
+    grad_flow = (send_a, grad_slots, da_s, da_r)
+    value_flow = (send_b, values, va_s, va_r)
+    for c in range(2, parts):
+        start_part(c, *grad_flow)
+    grad_slots[me] = send_a[me]
+
+    def expert_value(e, carry):
+        value = nn(act[e], second[e])
+        gated = (value * gate_of(e)).astype(BF16).reshape(ng, sz.cap, width)
+        send_b[:, rows_at(e, sz.cap), :] = gated
+        return carry
+
+    lax.fori_loop(0, sz.own, expert_value, 0)
+    values[me] = send_b[me]
+
+    def quarter_total(own, line, sums):
+        total = own[z].astype(F32)
+        for j in range(1, nz):
+            total = total + line[j - 1].astype(F32)
+        sums[...] = total.astype(BF16)
+
+    def wait_pieces(e, carry):
+        for j in range(1, nz):
+            grads_piece(e, j).wait()
+        return carry
 
     def weight_grads(e, carry):
         grad_value = (expert_rows(cot_slots, e).astype(F32) * gate_of(e)).astype(BF16)
         grad_second[e] = tn(act[e], grad_value).astype(BF16)
-        grad_first[e] = tn(expert_rows(slots, e), grad_pre[e]).astype(BF16)
+        select[rows_at(e, width), 0 : sz.hidden] = tn(expert_rows(slots, e), grad_pre[e]).astype(BF16)
         return carry
 
     for copy in dgates:
         copy.wait()
-    mine = iota((8, many), 1) // sz.cap == me
+    mine = iota((8, 128), 1) // sz.cap == me * sz.cap % 128 // sz.cap
     for g in range(ng):
-        masked = jnp.where(mine, dgate_recv[g], 0.0)
-        folded = masked[:, 0:128]
-        for i in range(1, many // 128):
-            folded = folded + masked[:, i * 128 : (i + 1) * 128]
+        folded = jnp.where(mine, dgate_recv[g], 0.0)
         folded = folded + pltpu.roll(folded, 64, 1)
         dgate_rows[g * sz.own : (g + 1) * sz.own, :] = folded[0 : sz.own]
     spread = jnp.concatenate([dgate_rows[...]] * (sz.slots // 128), 1)
@@ -495,10 +540,13 @@
         )
 
     def scatter(c, source, base, own, *flow):
-        flat = source[:, :, lanes(c)].reshape(sz.slots, part_width)
+        if source is grads_back:
+            places, flat = select_qt, source[...].reshape(few, part_width)
+        else:
+            places, flat = select_t, source[:, :, lanes(c)].reshape(sz.slots, part_width)
         for j in [*range(1, nz), 0]:
             tokens = rows_at(at.next_z(j), pad)
-            sums = nn(select_t[tokens, :], flat)
+            sums = nn(places[tokens, :], flat)
             if base is not None:
                 sums = sums + base[tokens, lanes(c)]
             if j == 0:
@@ -526,22 +574,41 @@
 
         return lax.fori_loop(0, ng - 1, step, carry)
 
+    def exchange_quarters():
+        lax.fori_loop(0, sz.own, wait_pieces, 0)
+        quarter_total(grads_q, grads_line, grads_sum)
+        for copy in grads_moves:
+            copy.start()
+        grads_back[me] = grads_sum[me]
+
+    grads_moves = [quarter_move(k, grads_sum, grads_back, dq_s, dq_r) for k in range(1, ng)]
+    order = [1, 2, 0, *range(3, parts)]
     done = 0
-    for c in range(parts):
+    for turn, c in enumerate(order):
         if c == 0:
+            for copy in grads_moves:
+                copy.wait()
+        elif c == 1:
             lax.fori_loop(0, sz.own, wait_first, 0)
         else:
             wait_part(c, *grad_flow)
-        if c == parts - 1:
-            for i in range(parts):
+        if turn == parts - 1:
+            for i in range(parts // 2):
                 start_part(i, *value_flow)
-        scatter(c, grad_slots, part, part_own, *part_flow)
-        until = sz.own * (c + 1) // parts
+        scatter(c, grads_back if c == 0 else grad_slots, part, part_own, *part_flow)
+        if turn == 0:
+            exchange_quarters()
+        until = sz.own * (turn + 1) // parts
         lax.fori_loop(done, until, weight_grads, 0)
         done = until
     stores = [
-        pltpu.make_async_copy(grad_first, grad_first_out, local_sem.at[2]),
-        pltpu.make_async_copy(grad_second, grad_second_out, local_sem.at[3]),
+        pltpu.make_async_copy(grad_second, grad_second_out, local_sem.at[2]),
+        *[
+            pltpu.make_async_copy(
+                select.at[e * width : (e + 1) * width, 0 : sz.hidden], grad_first_out.at[e], local_sem.at[3 + e]
+            )
+            for e in range(sz.own)
+        ],
     ]
     for copy in stores:
         copy.start()
@@ -608,19 +675,10 @@
     unit_one, factor_one = normalize(jnp.concatenate([x_ref[...].astype(F32), zeros], 0))
     normed_one = (unit_one * gain_one_ref[...]).astype(BF16)
     core_pairs = cp // (2 * HEAD_DIM)
-    turns, mixed_parts = nh * core_pairs, 0
-    turn = 0
     for other in [*range(1, nh), 0]:
         core = (h + other) % nh
         for q in range(core_pairs):
             attend_back(core * core_pairs + q)
-            turn += 1
-            if turn < turns:
-                until = parts * turn // turns
-                for c in range(mixed_parts, until):
-                    wait_part(c, *value_flow)
-                    scatter(c, values, None, mix_own, *mix_flow)
-                mixed_parts = until
         for i in range(3):
             sums = tn(normed_one, grad_qkv[i, :, rows_at(core, cp)])
             if other:
@@ -631,6 +689,13 @@
     qkv_band = [band_copy(k, pl.ds(0, 3), 1) for k in range(1, nd)]
     for copy in qkv_band:
         copy.start()
+
+    def send_mix(c):
+        wait_part(c, *value_flow)
+        scatter(c, values, None, mix_own, *mix_flow)
+
+    send_mix(0)
+    send_mix(1)
 
     grad_one = jnp.zeros((pad, width), F32)
     for i in range(3):
@@ -673,10 +738,7 @@
     for copy in small_copies:
         copy.start()
 
-    for c in range(mixed_parts, parts):
-        wait_part(c, *value_flow)
-        scatter(c, values, None, mix_own, *mix_flow)
-
+    start_part(parts // 2, *value_flow)
     for copy in small_copies:
         copy.wait()
     router_sum = rt[:, rows_at(d, band)]
@@ -689,6 +751,8 @@
         copy.wait()
     for copy in qkv_band:
         copy.wait()
+    for i in range(parts // 2 + 1, parts):
+        start_part(i, *value_flow)
     for i in range(4):
         sums = w_half[i, rows_at(d, band), :]
         for k in range(1, nd):
@@ -706,7 +770,8 @@
         ]
     for copy in z_copies:
         copy.start()
-
+    for c in range(parts // 2, parts):
+        send_mix(c)
     mix = gathered(mix_own, *mix_flow)
     output_out[...] = (hidden_at[...] + mix)[0 : sz.rows].astype(BF16)
 
@@ -717,46 +782,52 @@
     for j in range(1, nz):
         totals = join(totals, small_z[j - 1])
         router_sum = router_sum + rt_z[j - 1]
-    small_out[...] = totals
-    router_out[...] = router_sum
+    gain_one_out[...] = totals[0:1]
+    gain_two_out[...] = totals[1:2]
+    rr = sz.router_rows
+    own_router = router_sum[:, 0:rr]
+    for i in range(1, nh):
+        own_router = jnp.where(h == i, router_sum[:, i * rr : (i + 1) * rr], own_router)
+    router_out[...] = own_router
+    tau = tau_ref[...]
+    factor = jnp.sqrt(tau / jnp.maximum(totals[2:3, 0:HEADS], tau))
+    column = iota((1, cp), 1) // HEAD_DIM + h * (cp // HEAD_DIM)
+    scale_row = jnp.zeros((1, cp), F32)
+    for head in range(HEADS):
+        scale_row = jnp.where(column == head, factor[:, head : head + 1], scale_row)
+    for i in range(2):
+        clipped_out[i] = (w_qkv_ref[i].astype(F32) * scale_row).astype(BF16)
     for i in range(4):
         sums = w_half[i, rows_at(z, rp), :]
         for j in range(1, nz):
             sums = sums + line_recv[j - 1, i].astype(F32)
-        weight_out[i] = sums
+        if i < 3:
+            qkv_out[i] = sums
+        else:
+            out_out[...] = sums
     for copy in stores:
         copy.wait()
 
 
-def finish_kernel(
-    sz, output_ref, grad_input_ref, small_ref, weight_ref, router_ref, grad_first_ref, grad_second_ref, tau_ref, w_qkv_ref,
-    output, grad_input, gain_one, gain_two, grad_qkv, grad_out, grad_router, grad_first, grad_second, clipped,
-):
-    grad_first[...] = grad_first_ref[...].astype(F32)
-    grad_second[...] = grad_second_ref[...].astype(F32)
-
-    @pl.when(pl.program_id(0) == 0)
-    def _():
-        h = lax.axis_index("heads")
-        cp, rr = sz.col_piece, sz.router_rows
-        output[...] = output_ref[...]
-        grad_input[...] = grad_input_ref[...]
-        gain_one[...] = small_ref[0:1, :]
-        gain_two[...] = small_ref[1:2, :]
-        grad_qkv[...] = weight_ref[0:3]
-        grad_out[...] = weight_ref[3]
-        piece = router_ref[:, 0:rr]
-        for i in range(1, sz.nh):
-            piece = jnp.where(h == i, router_ref[:, i * rr : (i + 1) * rr], piece)
-        grad_router[...] = piece
-        tau = tau_ref[...]
-        factor = jnp.sqrt(tau / jnp.maximum(small_ref[2:3, 0:HEADS], tau))
-        column = iota((1, cp), 1) // HEAD_DIM + h * (cp // HEAD_DIM)
-        scale_row = jnp.zeros((1, cp), F32)
-        for head in range(HEADS):
-            scale_row = jnp.where(column == head, factor[:, head : head + 1], scale_row)
-        for i in range(2):
-            clipped[i] = (w_qkv_ref[i].astype(F32) * scale_row).astype(BF16)
+def finish_kernel(sz, *refs):
+    sources, results, held = refs[0:10], refs[10:20], refs[20:28]
+    halves_in, full_out, in_sems, out_sems, small_in, small_out = refs[28:]
+    pieces = [(i, e) for e in range(sz.own) for i in range(2)]
+    loads = [pltpu.make_async_copy(sources[8 + i].at[e], halves_in.at[i, e], in_sems.at[i, e]) for i, e in pieces]
+    stores = [pltpu.make_async_copy(full_out.at[i, e], results[8 + i].at[e], out_sems.at[i, e]) for i, e in pieces]
+    small_loads = [pltpu.make_async_copy(sources[n], held[n], small_in.at[n]) for n in range(8)]
+    small_stores = [pltpu.make_async_copy(held[n], results[n], small_out.at[n]) for n in range(8)]
+    for copy in loads + small_loads:
+        copy.start()
+    for (i, e), load, store in zip(pieces, loads, stores):
+        load.wait()
+        full_out[i, e] = halves_in[i, e].astype(F32)
+        store.start()
+    for load, store in zip(small_loads, small_stores):
+        load.wait()
+        store.start()
+    for copy in stores + small_stores:
+        copy.wait()
 
 
 def fast_body(
@@ -765,7 +836,7 @@
     ng, nz, nd, nh, pad, width, own = sz.groups, sz.nt, sz.nd, sz.nh, sz.pad, sz.width, sz.own
     rp, cp, band, parts, block = sz.row_piece, sz.col_piece, sz.band, sz.parts, sz.block
     many, hidden = ng * sz.cap, sz.hidden
-    on_chip, anywhere = pl.BlockSpec(memory_space=pltpu.VMEM), pl.BlockSpec(memory_space=pl.ANY)
+    on_chip, anywhere = pl.BlockSpec(memory_space=pltpu.VMEM), pl.BlockSpec(memory_space=pltpu.HBM)
 
     def shape(dims, dtype):
         return jax.ShapeDtypeStruct(dims, dtype)
@@ -781,22 +852,28 @@
 
     slot_buffer = half(ng, sz.group_slots, width)
     line_buffer = half(nz - 1, pad, width)
+    quarter_dims = (ng, own * (sz.cap // nz), width // parts)
+    quarter_buffer, few = half(*quarter_dims), ng * own * (sz.cap // nz)
+    rr = sz.router_rows
+    smalls = (
+        shape(inputs.shape, BF16), shape(inputs.shape, BF16), shape((1, width), F32), shape((1, width), F32),
+        shape((3, rp, cp), F32), shape((rp, cp), F32), shape((sz.experts, rr), F32), shape((2, rp, cp), BF16),
+    )
     packed = pl.pallas_call(
         functools.partial(block_kernel, sz),
-        out_shape=(
-            shape(inputs.shape, BF16), shape(inputs.shape, BF16), shape((8, width), F32), shape((4, rp, cp), F32),
-            shape((sz.experts, band), F32), shape(w_in.shape, BF16), shape(w_out.shape, BF16),
-        ),
-        in_specs=[on_chip] * 8 + [anywhere] * 2,
-        out_specs=(on_chip,) * 5 + (anywhere,) * 2,
+        out_shape=(*smalls, shape(w_in.shape, BF16), shape(w_out.shape, BF16)),
+        in_specs=[on_chip] * 9 + [anywhere] * 2,
+        out_specs=(on_chip,) * 8 + (anywhere,) * 2,
         scratch_shapes=[
             half(4, rp, cp), half(4, width, width), half(sz.experts, 128), half(ng, sz.experts, 128),
-            half(sz.experts, width), full(8, block), full(block, 128), half(sz.slots, block), half(block, sz.slots),
+            half(sz.experts, width), full(8, block), full(block, 128), half(sz.slots, block), half(block, sz.slots), half(block, few),
             half(block, width), half(block, width), *[slot_buffer] * 6,
+            half(nz, *quarter_dims), half(nz - 1, *quarter_dims), quarter_buffer,
+            quarter_buffer,
             half(own, width, hidden), half(own, hidden, width), half(own, many, hidden), half(own, many, hidden),
-            full(own, many, hidden), half(own, width, hidden), half(own, hidden, width),
-            full(sz.experts, 128), full(ng, sz.experts, 128), full(sz.experts, block), full(8, many),
-            full(ng, 8, many), full(sz.experts, 128),
+            full(own, many, hidden), half(own, hidden, width),
+            full(sz.experts, 128), full(ng, 8, 128), full(sz.experts, block), full(8, many),
+            full(ng, 8, 128), full(sz.experts, 128),
             half(3, pad, width), half(HEADS, pad, pad), half(pad, width), full(pad, width), full(8, 128),
             full(block, width), full(pad, width), line_buffer, line_buffer, full(pad, width), line_buffer, line_buffer,
             half(pad, width), half(3, pad, width), half(nh - 1, 4, width, cp), half(nh - 1, 4, width, cp),
@@ -809,39 +886,30 @@
             *pair(parts, nz - 1), *pair(parts, ng), *pair(parts, ng), *pair(ng - 1), *pair(own, ng), *pair(parts, ng),
             *pair(parts, ng), *pair(ng - 1), *pair(parts, nz - 1), *pair(parts, nz - 1), *pair(4 * (nh - 1)),
             *pair(2 * (nd - 1)), *pair(3 * (nz - 1)), *pair(2 * (nh - 1)), *pair(2 * (nd - 1)),
-            *pair(1), pltpu.SemaphoreType.DMA((4,)),
+            *pair(own, nz - 1), *pair(ng - 1),
+            pltpu.SemaphoreType.DMA((3 + own,)),
         ],
         compiler_params=pltpu.CompilerParams(collective_id=0, has_side_effects=True, vmem_limit_bytes=62 * 2**20),
         name="block",
     )(
         inputs, cotangent, routes.T, gain_attn[None, :], gain_expert[None, :], w_qkv, w_out_attn.T, w_router.T,
-        w_in, w_out,
-    )
-
-    rr = sz.router_rows
-
-    def same(*dims):
-        return pl.BlockSpec(dims, lambda e: (0,) * len(dims))
-
-    first_spec = pl.BlockSpec((1, width, hidden), lambda e: (e, 0, 0))
-    second_spec = pl.BlockSpec((1, hidden, width), lambda e: (e, 0, 0))
-    results = (
-        shape(inputs.shape, BF16), shape(inputs.shape, BF16), shape((1, width), F32), shape((1, width), F32),
-        shape((3, rp, cp), F32), shape((rp, cp), F32), shape((sz.experts, rr), F32), shape(w_in.shape, F32),
-        shape(w_out.shape, F32), shape((2, rp, cp), BF16),
-    )
-    output, grad_input, gain_one, gain_two, grad_qkv, grad_out, grad_router, grad_first, grad_second, clipped = (
+        tau[None, :], w_in, w_out,
+    )
+
+    both, dma = (2, *w_in.shape), pltpu.SemaphoreType.DMA
+    output, grad_input, gain_one, gain_two, grad_qkv, grad_out, grad_router, clipped, grad_first, grad_second = (
         pl.pallas_call(
             functools.partial(finish_kernel, sz),
-            grid=(own,),
-            out_shape=results,
-            in_specs=[same(*p.shape) for p in packed[:5]]
-            + [first_spec, second_spec, same(1, HEADS), same(*w_qkv.shape)],
-            out_specs=[
-                {7: first_spec, 8: second_spec}.get(i, same(*r.shape)) for i, r in enumerate(results)
+            out_shape=(*smalls, shape(w_in.shape, F32), shape(w_out.shape, F32)),
+            in_specs=[anywhere] * 10,
+            out_specs=(anywhere,) * 10,
+            scratch_shapes=[
+                *[pltpu.VMEM(x.shape, x.dtype) for x in smalls], half(*both), full(*both), dma((2, own)), dma((2, own)),
+                dma((8,)), dma((8,)),
             ],
+            compiler_params=pltpu.CompilerParams(vmem_limit_bytes=62 * 2**20),
             name="finish",
-        )(*packed, tau[None, :], w_qkv)
+        )(*packed)
     )
     return (
         output, grad_input, gain_one[0], gain_two[0], grad_qkv, grad_out.T, grad_router.T, grad_first, grad_second,

time: 172 us -> 161 us (0.936)
  Pallas kernels: 171 us -> 160 us
    pallas_call x2, Pallas kernels: 171 us -> 160 us  [the longest x1 155 us: fast_body(): pl.pallas_call(functools.partial(block_kernel, sz), out_shape=(*smalls, s...]
where the time goes in v3:
time: 161 us
  Pallas kernels  160 us (99%)
    pallas_call x1, Pallas kernels, fast_body(): pl.pallas_call(functools.partial(block_kernel, sz), out_shape=(*smalls, s...  155 us
    pallas_call x1, Pallas kernels, fast_body(): pl.pallas_call(functools.partial(finish_kernel, sz), out_shape=(*smalls,...  4.94 us

profile of v3, /device:TPU:0, one launch (start us, length us, event | category | flops | bytes accessed | tf_op | source)
XLA Modules:
  0.0 160.9 jit_solution(8746275507266516685)
XLA Ops:
  0.6 155.1 %block.1 = (bf16[197,512]{1,0:T(8,128)(2,1)}, bf16[197,512]{1,0:T(8,128)(2,1)}, f32[1,512]{1,0:T(1,128)}, f32[1,512]{1,0:T(1,128)}, f32[3,32,256]{2,1,0:T(8,128)...) custom-call(bf16[197,512]{1,0:T(8,128)(2,1)} %x_ref.1, ...), custom_call_target="tpu_custom_call" | custom-call | tf_op jit(solution)/shard_map/block/pallas_call | solution.py:862
  155.7 4.9 %finish.1 = (bf16[197,512]{1,0:T(8,128)(2,1)}, bf16[197,512]{1,0:T(8,128)(2,1)}, f32[1,512]{1,0:T(1,128)}, f32[1,512]{1,0:T(1,128)}, f32[3,32,256]{2,1,0:T(8,128...) custom-call(bf16[197,512]{1,0:T(8,128)(2,1)} %get-tuple-element.30.r, ...), custom_call_target="tpu_custom_call" | custom-call | tf_op jit(solution)/shard_map/finish/pallas_call | solution.py:901

commit v4 on v3

--- a/solution.py
+++ b/solution.py
@@ -37,6 +37,8 @@
     def fits(self):
         return (
             self.rows == SEQ
+            and self.nt == 4
+            and self.parts == 4
             and self.block_rows == self.rows * self.nt
             and self.cap == 64
             and self.experts == 32
@@ -113,6 +115,12 @@
     def next_z(self, j):
         return (self.z + j) % self.sz.nt
 
+    def inner(self):
+        return (self.z + 1) % 4 // 2
+
+    def mates(self):
+        return self.z + 1 - 2 * (self.z % 2), (self.z + 2) % 4, 3 - self.z
+
     def enter(self):
         sz = self.sz
         barrier = pltpu.get_barrier_semaphore()
@@ -127,6 +135,11 @@
     return pltpu.make_async_remote_copy(
         src_ref=src, dst_ref=dst, send_sem=send, recv_sem=recv, device_id=device, device_id_type=MESH
     )
+
+
+def drain(send_sem, recv_sem, sent, landed):
+    pltpu.make_async_copy(sent, sent, send_sem).wait()
+    pltpu.make_async_copy(landed, landed, recv_sem).wait()
 
 
 def route_table(sz, routes_ref, table):
@@ -148,7 +161,8 @@
     small, small_send, small_core, small_x, small_z, rt, rt_core, rt_x, rt_z,
     wz_s, wz_r, wx_s, wx_r, wc_s, wc_r, r_s, r_r, qz_s, qz_r, nz_s, nz_r, qa_s, qa_r, na_s, na_r, ga_s, ga_r,
     d0_s, d0_r, da_s, da_r, va_s, va_r, dg_s, dg_r, pz_s, pz_r, mz_s, mz_r, gc_s, gc_r, gx_s, gx_r, gl_s, gl_r,
-    sc_s, sc_r, sx_s, sx_r, dl_s, dl_r, dq_s, dq_r, local_sem,
+    sc_s, sc_r, sx_s, sx_r, dl_s, dl_r, dq_s, dq_r, pr_r, mr_r,
+    local_sem,
 ):
     at = Place(sz)
     d, h, z, me = at.d, at.h, at.z, at.group
@@ -173,11 +187,14 @@
         [cot_ref[...].astype(F32), jnp.zeros((pad - sz.rows, width), F32)], 0
     ).astype(BF16)
 
+    part_recv[2] = jnp.zeros((pad, width), BF16)
+    mix_recv[2] = jnp.zeros((pad, width), BF16)
+
     at.enter()
 
     w_rows = rows_at(d * nz + z, rp)
     w_z = [
-        remote(w_own, w_full.at[:, w_rows, own_columns], wz_s.at[j - 1], wz_r.at[j - 1], at.line(at.next_z(j)))
+        remote(w_own, w_full.at[:, w_rows, own_columns], wz_s.at[0], wz_r.at[0], at.line(at.next_z(j)))
         for j in range(1, nz)
     ]
     for copy in w_z:
@@ -189,7 +206,7 @@
     for copy in loads:
         copy.start()
     routers = [
-        remote(router_own, router_full.at[me], r_s.at[k - 1], r_r.at[k - 1], at.plane(at.next_group(k)))
+        remote(router_own, router_full.at[me], r_s.at[0], r_r.at[0], at.plane(at.next_group(k)))
         for k in range(1, ng)
     ]
     for copy in routers:
@@ -202,12 +219,13 @@
     unit_one, _ = normalize(x_rows)
     normed_one = (unit_one * gain_one_ref[...]).astype(BF16)
 
-    for copy in w_z:
-        copy.wait()
-
-    def to_core(i, dp, other):
+    others = pl.ds(0, ng - 1)
+    three = w_full.at[:, pl.ds(0, (nz - 1) * rp), own_columns]
+    drain(wz_s.at[0], wz_r.at[0], three, three)
+
+    def to_core(dp, other):
         place = w_full.at[:, rows_at(dp, band), own_columns]
-        return remote(place, place, wc_s.at[i], wc_r.at[i], (d, (h + other) % nh, z))
+        return remote(place, place, wc_s.at[other - 1], wc_r.at[other - 1], (d, (h + other) % nh, z))
 
     w_band = w_full.at[:, rows_at(d, band), own_columns]
     w_x = [
@@ -215,16 +233,20 @@
     ]
     for copy in w_x:
         copy.start()
-    w_c = [to_core((other - 1) * nd, d, other) for other in range(1, nh)]
+    w_c = [to_core(d, other) for other in range(1, nh)]
     for copy in w_c:
         copy.start()
 
     def along(block, send_sems, recv_sems, c):
         place = block.at[own_block, lanes(c)]
         return [
-            remote(place, place, send_sems.at[c, j - 1], recv_sems.at[c, j - 1], at.line(at.next_z(j)))
+            remote(place, place, send_sems.at[c], recv_sems.at[c], at.line(at.next_z(j)))
             for j in range(1, nz)
         ]
+
+    def wait_along(block, send_sems, recv_sems, c):
+        place = block.at[pl.ds(0, (nz - 1) * pad), lanes(c)]
+        drain(send_sems.at[c], recv_sems.at[c], place, place)
 
     for c in range(parts):
         for copy in along(cot_block, qz_s, qz_r, c):
@@ -261,7 +283,7 @@
 
     def quarter_move(k, send, landing, send_sems, recv_sems):
         g = (me + k) % ng
-        return remote(send.at[g], landing.at[me], send_sems.at[k - 1], recv_sems.at[k - 1], at.plane(g))
+        return remote(send.at[g], landing.at[me], send_sems.at[0], recv_sems.at[0], at.plane(g))
 
     def dispatch(c, block, send, out):
         def step(g, carry):
@@ -274,7 +296,7 @@
     def exchange(c, k, send, out, send_sems, recv_sems):
         g = (me + k) % ng
         return remote(
-            send.at[g, :, lanes(c)], out.at[me, :, lanes(c)], send_sems.at[c, k], recv_sems.at[c, k], at.plane(g)
+            send.at[g, :, lanes(c)], out.at[me, :, lanes(c)], send_sems.at[c], recv_sems.at[c], at.plane(g)
         )
 
     def start_part(c, *flow):
@@ -284,31 +306,25 @@
 
         lax.fori_loop(0, ng - 1, step, 0)
 
-    def wait_part(c, *flow):
-        def step(i, carry):
-            exchange(c, i + 1, *flow).wait()
-            return carry
-
-        lax.fori_loop(0, ng - 1, step, 0)
+    def wait_part(c, send, out, send_sems, recv_sems):
+        drain(send_sems.at[c], recv_sems.at[c], send.at[others, :, lanes(c)], out.at[others, :, lanes(c)])
 
     cot_flow = (send_a, cot_slots, qa_s, qa_r)
     row_flow = (send_b, slots, na_s, na_r)
 
     def send_cot(c):
-        for copy in along(cot_block, qz_s, qz_r, c):
-            copy.wait()
+        wait_along(cot_block, qz_s, qz_r, c)
         dispatch(c, cot_block, send_a, cot_slots)
 
     send_cot(0)
     for k in range(1, nd):
         w_x[k - 1].wait_recv()
         for other in range(1, nh):
-            copy = to_core((other - 1) * nd + k, (d - k + nd) % nd, other)
-            copy.start()
-            w_c.append(copy)
+            to_core((d - k + nd) % nd, other).start()
     start_part(0, *cot_flow)
-    for copy in w_c:
-        copy.wait()
+    for other in range(1, nh):
+        columns = w_full.at[:, :, own_columns]
+        drain(wc_s.at[other - 1], wc_r.at[other - 1], columns, columns)
     for copy in w_x:
         copy.wait_send()
 
@@ -369,8 +385,7 @@
         return carry
 
     lax.fori_loop(0, nz, fill_t, 0)
-    for copy in routers:
-        copy.wait()
+    drain(r_s.at[0], r_r.at[0], router_full.at[others], router_full.at[others])
     for g in range(ng):
         router_t[:, g * sz.router_rows : (g + 1) * sz.router_rows] = router_full[g, :, 0 : sz.router_rows]
 
@@ -382,8 +397,7 @@
         return carry
 
     for c in range(parts):
-        for copy in along(rows_block, nz_s, nz_r, c):
-            copy.wait()
+        wait_along(rows_block, nz_s, nz_r, c)
         dispatch(c, rows_block, send_b, slots)
         start_part(c, *row_flow)
         if c == parts // 2 - 1:
@@ -408,7 +422,7 @@
     gate_send[...] = folded
     gate_copies = [
         remote(
-            gate_send.at[rows_at(at.next_group(k) * sz.own // 8, 8)], gate_recv.at[me], ga_s.at[k - 1], ga_r.at[k - 1],
+            gate_send.at[rows_at(at.next_group(k) * sz.own // 8, 8)], gate_recv.at[me], ga_s.at[0], ga_r.at[0],
             at.plane(at.next_group(k)),
         )
         for k in range(1, ng)
@@ -416,8 +430,7 @@
     for copy in gate_copies:
         copy.start()
     gate_recv[me] = gate_send[rows_at(me * sz.own // 8, 8)]
-    for copy in gate_copies:
-        copy.wait()
+    drain(ga_s.at[0], ga_r.at[0], gate_recv.at[others], gate_recv.at[others])
     for c in range(parts):
         wait_part(c, *row_flow)
 
@@ -430,13 +443,13 @@
         g = (me + k) % ng
         piece = (rows_at(e, sz.cap), lanes(1))
         return remote(
-            send_a.at[(g, *piece)], grad_slots.at[(me, *piece)], d0_s.at[e, k], d0_r.at[e, k], at.plane(g)
+            send_a.at[(g, *piece)], grad_slots.at[(me, *piece)], d0_s.at[e], d0_r.at[e], at.plane(g)
         )
 
     def grads_piece(e, j):
         piece = (slice(None), rows_at(e, quarter), slice(None))
         return remote(
-            grads_q.at[(at.next_z(j), *piece)], grads_line.at[(j - 1, *piece)], dl_s.at[e, j - 1], dl_r.at[e, j - 1],
+            grads_q.at[(at.next_z(j), *piece)], grads_line.at[(j - 1, *piece)], dl_s.at[0], dl_r.at[0],
             at.line(at.next_z(j)),
         )
 
@@ -477,8 +490,8 @@
     lax.fori_loop(0, sz.own, expert_back, 0)
     dgates = [
         remote(
-            dgate_send.at[:, rows_at(at.next_group(k) * sz.cap // 128, 128)], dgate_recv.at[me], dg_s.at[k - 1],
-            dg_r.at[k - 1], at.plane(at.next_group(k)),
+            dgate_send.at[:, rows_at(at.next_group(k) * sz.cap // 128, 128)], dgate_recv.at[me], dg_s.at[0],
+            dg_r.at[0], at.plane(at.next_group(k)),
         )
         for k in range(1, ng)
     ]
@@ -506,10 +519,6 @@
             total = total + line[j - 1].astype(F32)
         sums[...] = total.astype(BF16)
 
-    def wait_pieces(e, carry):
-        for j in range(1, nz):
-            grads_piece(e, j).wait()
-        return carry
 
     def weight_grads(e, carry):
         grad_value = (expert_rows(cot_slots, e).astype(F32) * gate_of(e)).astype(BF16)
@@ -517,8 +526,7 @@
         select[rows_at(e, width), 0 : sz.hidden] = tn(expert_rows(slots, e), grad_pre[e]).astype(BF16)
         return carry
 
-    for copy in dgates:
-        copy.wait()
+    drain(dg_s.at[0], dg_r.at[0], dgate_recv.at[others], dgate_recv.at[others])
     mine = iota((8, 128), 1) // sz.cap == me * sz.cap % 128 // sz.cap
     for g in range(ng):
         folded = jnp.where(mine, dgate_recv[g], 0.0)
@@ -533,10 +541,19 @@
     rt[...] = nn(dlogits, rows_block[...])
     part[...] = tn(dlogits, router_t[...])
 
-    def line_copy(c, j, send, recv, send_sems, recv_sems):
+    inner = at.inner()
+    beside, across, mirror = at.mates()
+
+    def line_copy(c, slot, send, recv, send_sems, recv_sems, relay_sems, last):
+        if slot < 2:
+            return remote(
+                send.at[slot, :, lanes(c)], recv.at[slot, :, lanes(c)], send_sems.at[c], recv_sems.at[c],
+                at.line((beside, across)[slot]),
+            )
+        by_way = 1 - inner if c != last else 0
+        to = mirror + by_way * (beside - mirror)
         return remote(
-            send.at[j - 1, :, lanes(c)], recv.at[j - 1, :, lanes(c)], send_sems.at[c, j - 1], recv_sems.at[c, j - 1],
-            at.line(at.next_z(j)),
+            send.at[2, :, lanes(c)], recv.at[2 + by_way, :, lanes(c)], send_sems.at[c], relay_sems.at[c, by_way], at.line(to)
         )
 
     def scatter(c, source, base, own, *flow):
@@ -544,56 +561,72 @@
             places, flat = select_qt, source[...].reshape(few, part_width)
         else:
             places, flat = select_t, source[:, :, lanes(c)].reshape(sz.slots, part_width)
-        for j in [*range(1, nz), 0]:
-            tokens = rows_at(at.next_z(j), pad)
+        for slot, target in ((2, mirror), (1, across), (0, beside), (None, z)):
+            tokens = rows_at(target, pad)
             sums = nn(places[tokens, :], flat)
             if base is not None:
                 sums = sums + base[tokens, lanes(c)]
-            if j == 0:
+            if slot is None:
                 own[:, lanes(c)] = sums
+                continue
+            flow[0][slot, :, lanes(c)] = sums.astype(BF16)
+            if slot == 1 and c != flow[-1]:
+
+                @pl.when(inner == 0)
+                def _():
+                    line_copy(c, 1, *flow).start()
             else:
-                flow[0][j - 1, :, lanes(c)] = sums.astype(BF16)
-                line_copy(c, j, *flow).start()
-
-    def gathered(own, *flow):
+                line_copy(c, slot, *flow).start()
+
+    def relay(c, send, recv, send_sems, recv_sems, relay_sems, last):
+        @pl.when(inner == 1)
+        def _():
+            landed = recv.at[3, :, lanes(c)]
+            pltpu.make_async_copy(landed, landed, relay_sems.at[c, 1]).wait()
+            send[1, :, lanes(c)] = (send[1, :, lanes(c)].astype(F32) + recv[3, :, lanes(c)].astype(F32)).astype(BF16)
+            line_copy(c, 1, send, recv, send_sems, recv_sems, relay_sems, last).start()
+
+    def gathered(own, send, recv, send_sems, recv_sems, relay_sems, last):
         for c in range(parts):
-            for j in range(1, nz):
-                line_copy(c, j, *flow).wait()
+            drain(send_sems.at[c], recv_sems.at[c], send.at[:, :, lanes(c)], recv.at[pl.ds(0, 2), :, lanes(c)])
+
+            @pl.when(inner == 1 if c != last else True)
+            def _(c=c):
+                landed = recv.at[2, :, lanes(c)]
+                pltpu.make_async_copy(landed, landed, relay_sems.at[c, 0]).wait()
+
         sums = own[...]
-        for j in range(1, nz):
-            sums = sums + flow[1][j - 1].astype(F32)
+        for slot in range(3):
+            sums = sums + recv[slot].astype(F32)
         return sums
 
-    part_flow = (part_send, part_recv, pz_s, pz_r)
-    mix_flow = (mix_send, mix_recv, mz_s, mz_r)
+    part_flow = (part_send, part_recv, pz_s, pz_r, pr_r, 0)
+    mix_flow = (mix_send, mix_recv, mz_s, mz_r, mr_r, parts - 1)
 
     def wait_first(e, carry):
-        def step(i, carry):
-            first_piece(e, i + 1).wait()
-            return carry
-
-        return lax.fori_loop(0, ng - 1, step, carry)
+        piece = (others, rows_at(e, sz.cap), lanes(1))
+        drain(d0_s.at[e], d0_r.at[e], send_a.at[piece], grad_slots.at[piece])
+        return carry
 
     def exchange_quarters():
-        lax.fori_loop(0, sz.own, wait_pieces, 0)
+        drain(dl_s.at[0], dl_r.at[0], grads_line, grads_line)
         quarter_total(grads_q, grads_line, grads_sum)
         for copy in grads_moves:
             copy.start()
         grads_back[me] = grads_sum[me]
 
     grads_moves = [quarter_move(k, grads_sum, grads_back, dq_s, dq_r) for k in range(1, ng)]
-    order = [1, 2, 0, *range(3, parts)]
+    order = [*range(1, parts), 0]
     done = 0
     for turn, c in enumerate(order):
         if c == 0:
-            for copy in grads_moves:
-                copy.wait()
+            drain(dq_s.at[0], dq_r.at[0], grads_back.at[others], grads_back.at[others])
         elif c == 1:
             lax.fori_loop(0, sz.own, wait_first, 0)
         else:
             wait_part(c, *grad_flow)
-        if turn == parts - 1:
-            for i in range(parts // 2):
+        if c == parts - 1:
+            for i in range(parts):
                 start_part(i, *value_flow)
         scatter(c, grads_back if c == 0 else grad_slots, part, part_own, *part_flow)
         if turn == 0:
@@ -601,6 +634,8 @@
         until = sz.own * (turn + 1) // parts
         lax.fori_loop(done, until, weight_grads, 0)
         done = until
+        if turn > 0:
+            relay(order[turn - 1], *part_flow)
     stores = [
         pltpu.make_async_copy(grad_second, grad_second_out, local_sem.at[2]),
         *[
@@ -633,11 +668,10 @@
         w_half[i] = sums
         band_send[i] = sums.astype(BF16)
 
-    def band_copy(k, matrices, n):
+    def band_copy(k, i):
         to = (d + k) % nd
-        n = 2 * (k - 1) + n
         return remote(
-            band_send.at[matrices, rows_at(to, band), :], band_recv.at[k - 1, matrices], gx_s.at[n], gx_r.at[n], (to, h, z)
+            band_send.at[i, rows_at(to, band), :], band_recv.at[k - 1, i], gx_s.at[i], gx_r.at[i], (to, h, z)
         )
 
     for other in [*range(1, nh), 0]:
@@ -649,9 +683,17 @@
             w_half[3] = sums
     grad_mixed[...] = nn(grad_attn, w_full[3]).astype(BF16)
     half_sum(3, w_half[3])
-    out_band = [band_copy(k, pl.ds(3, 1), 0) for k in range(1, nd)]
-    for copy in out_band:
-        copy.start()
+    for k in range(1, nd):
+        band_copy(k, 3).start()
+
+    def send_mix(c):
+        wait_part(c, *value_flow)
+        scatter(c, values, None, mix_own, *mix_flow)
+        if c:
+            relay(c - 1, *mix_flow)
+
+    for c in range(parts // 2):
+        send_mix(c)
 
     def attend_back(pair):
         columns = rows_at(pair, 2 * HEAD_DIM)
@@ -686,16 +728,12 @@
                 core_copy(i, other).start()
             else:
                 half_sum(i, sums)
-    qkv_band = [band_copy(k, pl.ds(0, 3), 1) for k in range(1, nd)]
-    for copy in qkv_band:
-        copy.start()
-
-    def send_mix(c):
-        wait_part(c, *value_flow)
-        scatter(c, values, None, mix_own, *mix_flow)
-
-    send_mix(0)
-    send_mix(1)
+        if other == nh - 1:
+            send_mix(2)
+    for i in range(3):
+        for k in range(1, nd):
+            band_copy(k, i).start()
+    send_mix(3)
 
     grad_one = jnp.zeros((pad, width), F32)
     for i in range(3):
@@ -730,53 +768,47 @@
     small_send[0] = small[...]
     small_copies = []
     for k in range(1, nd):
-        to, n = (d + k) % nd, 2 * (k - 1)
+        to = (d + k) % nd
         small_copies += [
-            remote(small_send.at[0], small_x.at[k - 1], sx_s.at[n], sx_r.at[n], (to, h, z)),
-            remote(rt.at[:, rows_at(to, band)], rt_x.at[k - 1], sx_s.at[n + 1], sx_r.at[n + 1], (to, h, z)),
+            remote(small_send.at[0], small_x.at[k - 1], sx_s.at[0], sx_r.at[0], (to, h, z)),
+            remote(rt.at[:, rows_at(to, band)], rt_x.at[k - 1], sx_s.at[1], sx_r.at[1], (to, h, z)),
         ]
     for copy in small_copies:
         copy.start()
 
-    start_part(parts // 2, *value_flow)
-    for copy in small_copies:
-        copy.wait()
+    def line_piece(i, j):
+        to = at.next_z(j)
+        return remote(line_send.at[i, rows_at(to, rp), :], line_recv.at[j - 1, i], gl_s.at[i], gl_r.at[i], at.line(to))
+
+    for i in (3, 0, 1, 2):
+        drain(gx_s.at[i], gx_r.at[i], band_recv.at[:, i], band_recv.at[:, i])
+        sums = w_half[i, rows_at(d, band), :]
+        for k in range(1, nd):
+            sums = sums + band_recv[k - 1, i].astype(F32)
+        w_half[i, 0:band, :] = sums
+        line_send[i] = sums.astype(BF16)
+        for j in range(1, nz):
+            line_piece(i, j).start()
+    drain(sx_s.at[0], sx_r.at[0], small_x, small_x)
+    drain(sx_s.at[1], sx_r.at[1], rt_x, rt_x)
     router_sum = rt[:, rows_at(d, band)]
     for k in range(1, nd):
         small[...] = join(small[...], small_x[k - 1])
         router_sum = router_sum + rt_x[k - 1]
     rt_z[nz - 1] = router_sum
     small_send[1] = small[...]
-    for copy in out_band:
-        copy.wait()
-    for copy in qkv_band:
-        copy.wait()
-    for i in range(parts // 2 + 1, parts):
-        start_part(i, *value_flow)
-    for i in range(4):
-        sums = w_half[i, rows_at(d, band), :]
-        for k in range(1, nd):
-            sums = sums + band_recv[k - 1, i].astype(F32)
-        w_half[i, 0:band, :] = sums
-        line_send[i] = sums.astype(BF16)
-    z_copies = []
     for j in range(1, nz):
-        to, n = at.next_z(j), 3 * (j - 1)
-        device = at.line(to)
-        z_copies += [
-            remote(line_send.at[:, rows_at(to, rp), :], line_recv.at[j - 1], gl_s.at[n], gl_r.at[n], device),
-            remote(small_send.at[1], small_z.at[j - 1], gl_s.at[n + 1], gl_r.at[n + 1], device),
-            remote(rt_z.at[nz - 1], rt_z.at[j - 1], gl_s.at[n + 2], gl_r.at[n + 2], device),
-        ]
-    for copy in z_copies:
-        copy.start()
-    for c in range(parts // 2, parts):
-        send_mix(c)
+        device = at.line(at.next_z(j))
+        remote(small_send.at[1], small_z.at[j - 1], gl_s.at[4], gl_r.at[4], device).start()
+        remote(rt_z.at[nz - 1], rt_z.at[j - 1], gl_s.at[5], gl_r.at[5], device).start()
+
     mix = gathered(mix_own, *mix_flow)
     output_out[...] = (hidden_at[...] + mix)[0 : sz.rows].astype(BF16)
 
-    for copy in z_copies:
-        copy.wait()
+    for i in range(4):
+        drain(gl_s.at[i], gl_r.at[i], line_recv.at[:, i], line_recv.at[:, i])
+    for n, landed in ((4, small_z), (5, rt_z.at[pl.ds(0, nz - 1)])):
+        drain(gl_s.at[n], gl_r.at[n], landed, landed)
     totals = small[...]
     router_sum = rt_z[nz - 1]
     for j in range(1, nz):
@@ -875,18 +907,18 @@
             full(sz.experts, 128), full(ng, 8, 128), full(sz.experts, block), full(8, many),
             full(ng, 8, 128), full(sz.experts, 128),
             half(3, pad, width), half(HEADS, pad, pad), half(pad, width), full(pad, width), full(8, 128),
-            full(block, width), full(pad, width), line_buffer, line_buffer, full(pad, width), line_buffer, line_buffer,
+            full(block, width), full(pad, width), line_buffer, half(nz, pad, width), full(pad, width), line_buffer,
+            half(nz, pad, width),
             half(pad, width), half(3, pad, width), half(nh - 1, 4, width, cp), half(nh - 1, 4, width, cp),
             full(4, width, cp), half(4, width, cp), half(nd - 1, 4, band, cp), half(4, band, cp),
             half(nz - 1, 4, rp, cp),
             full(8, width), full(2, 8, width), full(nh - 1, 8, width), full(nd - 1, 8, width), full(nz - 1, 8, width),
             full(sz.experts, width), full(nh - 1, sz.experts, width), full(nd - 1, sz.experts, band),
             full(nz, sz.experts, band),
-            *pair(nz - 1), *pair(nd - 1), *pair(nd * (nh - 1)), *pair(ng - 1), *pair(parts, nz - 1),
-            *pair(parts, nz - 1), *pair(parts, ng), *pair(parts, ng), *pair(ng - 1), *pair(own, ng), *pair(parts, ng),
-            *pair(parts, ng), *pair(ng - 1), *pair(parts, nz - 1), *pair(parts, nz - 1), *pair(4 * (nh - 1)),
-            *pair(2 * (nd - 1)), *pair(3 * (nz - 1)), *pair(2 * (nh - 1)), *pair(2 * (nd - 1)),
-            *pair(own, nz - 1), *pair(ng - 1),
+            *pair(1), *pair(nd - 1), *pair(nh - 1), *pair(1), *pair(parts), *pair(parts), *pair(parts), *pair(parts),
+            *pair(1), *pair(own), *pair(parts), *pair(parts), *pair(1), *pair(parts), *pair(parts), *pair(4 * (nh - 1)),
+            *pair(4), *pair(6), *pair(2 * (nh - 1)), *pair(2), *pair(1), *pair(1),
+            *pair(parts, 2),
             pltpu.SemaphoreType.DMA((3 + own,)),
         ],
         compiler_params=pltpu.CompilerParams(collective_id=0, has_side_effects=True, vmem_limit_bytes=62 * 2**20),

time: 161 us -> 148 us (0.919)
  Pallas kernels: 160 us -> 147 us
    pallas_call x1, Pallas kernels: 155 us -> 142 us  [fast_body(): pl.pallas_call(functools.partial(block_kernel, sz), out_shape=(*smalls, s...]
where the time goes in v4:
time: 148 us
  Pallas kernels  147 us (99%)
    pallas_call x1, Pallas kernels, fast_body(): pl.pallas_call(functools.partial(block_kernel, sz), out_shape=(*smalls, s...  142 us
    pallas_call x1, Pallas kernels, fast_body(): pl.pallas_call(functools.partial(finish_kernel, sz), out_shape=(*smalls,...  4.94 us

profile of v4, /device:TPU:0, one launch (start us, length us, event | category | flops | bytes accessed | tf_op | source)
XLA Modules:
  0.0 147.7 jit_solution(15515560024750941216)
XLA Ops:
  0.6 141.9 %block.1 = (bf16[197,512]{1,0:T(8,128)(2,1)}, bf16[197,512]{1,0:T(8,128)(2,1)}, f32[1,512]{1,0:T(1,128)}, f32[1,512]{1,0:T(1,128)}, f32[3,32,256]{2,1,0:T(8,128)...) custom-call(bf16[197,512]{1,0:T(8,128)(2,1)} %x_ref.1, ...), custom_call_target="tpu_custom_call" | custom-call | tf_op jit(solution)/shard_map/block/pallas_call | solution.py:894
  142.6 4.9 %finish.1 = (bf16[197,512]{1,0:T(8,128)(2,1)}, bf16[197,512]{1,0:T(8,128)(2,1)}, f32[1,512]{1,0:T(1,128)}, f32[1,512]{1,0:T(1,128)}, f32[3,32,256]{2,1,0:T(8,128...) custom-call(bf16[197,512]{1,0:T(8,128)(2,1)} %get-tuple-element.30.r, ...), custom_call_target="tpu_custom_call" | custom-call | tf_op jit(solution)/shard_map/finish/pallas_call | solution.py:933

commit v5 on v4

--- a/solution.py
+++ b/solution.py
@@ -193,11 +193,35 @@
     at.enter()
 
     w_rows = rows_at(d * nz + z, rp)
-    w_z = [
-        remote(w_own, w_full.at[:, w_rows, own_columns], wz_s.at[0], wz_r.at[0], at.line(at.next_z(j)))
-        for j in range(1, nz)
+    others = pl.ds(0, ng - 1)
+
+    def send_line(i):
+        for j in range(1, nz):
+            remote(
+                w_own.at[i], w_full.at[i, w_rows, own_columns], wz_s.at[i], wz_r.at[i], at.line(at.next_z(j))
+            ).start()
+
+    def along(block, send_sems, recv_sems, c):
+        place = block.at[own_block, lanes(c)]
+        return [
+            remote(place, place, send_sems.at[c], recv_sems.at[c], at.line(at.next_z(j)))
+            for j in range(1, nz)
+        ]
+
+    def wait_along(block, send_sems, recv_sems, c):
+        place = block.at[pl.ds(0, (nz - 1) * pad), lanes(c)]
+        drain(send_sems.at[c], recv_sems.at[c], place, place)
+
+    for i in range(3):
+        send_line(i)
+    for copy in along(cot_block, qz_s, qz_r, 0):
+        copy.start()
+    send_line(3)
+    routers = [
+        remote(router_own, router_full.at[me], r_s.at[0], r_r.at[0], at.plane(at.next_group(k)))
+        for k in range(1, ng)
     ]
-    for copy in w_z:
+    for copy in routers:
         copy.start()
     loads = [
         pltpu.make_async_copy(first_hbm, first, local_sem.at[0]),
@@ -205,52 +229,41 @@
     ]
     for copy in loads:
         copy.start()
-    routers = [
-        remote(router_own, router_full.at[me], r_s.at[0], r_r.at[0], at.plane(at.next_group(k)))
-        for k in range(1, ng)
-    ]
-    for copy in routers:
-        copy.start()
     w_full[:, w_rows, own_columns] = w_own[...]
     router_full[me] = router_own[...]
+
+    def to_core(i, dp, other):
+        place = w_full.at[i, rows_at(dp, band), own_columns]
+        n = 4 * (other - 1) + i
+        return remote(place, place, wc_s.at[n], wc_r.at[n], (d, (h + other) % nh, z))
+
+    def send_band(i):
+        landed = w_full.at[i, pl.ds(0, (nz - 1) * rp), own_columns]
+        drain(wz_s.at[i], wz_r.at[i], landed, landed)
+        place = w_full.at[i, rows_at(d, band), own_columns]
+        for k in range(1, nd):
+            remote(place, place, wx_s.at[i], wx_r.at[i], ((d + k) % nd, h, z)).start()
+        for other in range(1, nh):
+            to_core(i, d, other).start()
+
+    def pass_on(i):
+        landed = w_full.at[i, pl.ds(0, (nd - 1) * band), own_columns]
+        drain(wx_s.at[i], wx_r.at[i], landed, landed)
+        for k in range(1, nd):
+            for other in range(1, nh):
+                to_core(i, (d + k) % nd, other).start()
+
+    def arrived(i):
+        for other in range(1, nh):
+            n, columns = 4 * (other - 1) + i, w_full.at[i, :, own_columns]
+            drain(wc_s.at[n], wc_r.at[n], columns, columns)
 
     zeros = jnp.zeros((pad - sz.rows, width), F32)
     x_rows = jnp.concatenate([x_ref[...].astype(F32), zeros], 0)
     unit_one, _ = normalize(x_rows)
     normed_one = (unit_one * gain_one_ref[...]).astype(BF16)
-
-    others = pl.ds(0, ng - 1)
-    three = w_full.at[:, pl.ds(0, (nz - 1) * rp), own_columns]
-    drain(wz_s.at[0], wz_r.at[0], three, three)
-
-    def to_core(dp, other):
-        place = w_full.at[:, rows_at(dp, band), own_columns]
-        return remote(place, place, wc_s.at[other - 1], wc_r.at[other - 1], (d, (h + other) % nh, z))
-
-    w_band = w_full.at[:, rows_at(d, band), own_columns]
-    w_x = [
-        remote(w_band, w_band, wx_s.at[k - 1], wx_r.at[k - 1], ((d + k) % nd, h, z)) for k in range(1, nd)
-    ]
-    for copy in w_x:
-        copy.start()
-    w_c = [to_core(d, other) for other in range(1, nh)]
-    for copy in w_c:
-        copy.start()
-
-    def along(block, send_sems, recv_sems, c):
-        place = block.at[own_block, lanes(c)]
-        return [
-            remote(place, place, send_sems.at[c], recv_sems.at[c], at.line(at.next_z(j)))
-            for j in range(1, nz)
-        ]
-
-    def wait_along(block, send_sems, recv_sems, c):
-        place = block.at[pl.ds(0, (nz - 1) * pad), lanes(c)]
-        drain(send_sems.at[c], recv_sems.at[c], place, place)
-
-    for c in range(parts):
-        for copy in along(cot_block, qz_s, qz_r, c):
-            copy.start()
+    for i in range(3):
+        send_band(i)
 
     route_table(sz, routes_ref, route_rows)
     route_a, route_b = route_rows[0:1, :], route_rows[1:2, :]
@@ -285,20 +298,27 @@
         g = (me + k) % ng
         return remote(send.at[g], landing.at[me], send_sems.at[0], recv_sems.at[0], at.plane(g))
 
-    def dispatch(c, block, send, out):
-        def step(g, carry):
-            send[g, :, lanes(c)] = nn(select[rows_at(g, sz.group_slots), :], block[:, lanes(c)]).astype(BF16)
-            return carry
-
-        lax.fori_loop(0, ng, step, 0)
-        out[me, :, lanes(c)] = send[me, :, lanes(c)]
-
     def exchange(c, k, send, out, send_sems, recv_sems):
         g = (me + k) % ng
         return remote(
             send.at[g, :, lanes(c)], out.at[me, :, lanes(c)], send_sems.at[c], recv_sems.at[c], at.plane(g)
         )
 
+    def dispatch(c, block, send, out, send_sems, recv_sems):
+        def step(i, carry):
+            k = ng - 1 - i
+            g = (me + k) % ng
+            send[g, :, lanes(c)] = nn(select[rows_at(g, sz.group_slots), :], block[:, lanes(c)]).astype(BF16)
+
+            @pl.when(k > 0)
+            def _():
+                exchange(c, k, send, out, send_sems, recv_sems).start()
+
+            return carry
+
+        lax.fori_loop(0, ng, step, 0)
+        out[me, :, lanes(c)] = send[me, :, lanes(c)]
+
     def start_part(c, *flow):
         def step(i, carry):
             exchange(c, ng - 1 - i, *flow).start()
@@ -314,22 +334,21 @@
 
     def send_cot(c):
         wait_along(cot_block, qz_s, qz_r, c)
-        dispatch(c, cot_block, send_a, cot_slots)
-
+        dispatch(c, cot_block, *cot_flow)
+
+    send_band(3)
+    for c in range(1, parts):
+        for copy in along(cot_block, qz_s, qz_r, c):
+            copy.start()
+    pass_on(0)
     send_cot(0)
-    for k in range(1, nd):
-        w_x[k - 1].wait_recv()
-        for other in range(1, nh):
-            to_core((d - k + nd) % nd, other).start()
-    start_part(0, *cot_flow)
-    for other in range(1, nh):
-        columns = w_full.at[:, :, own_columns]
-        drain(wc_s.at[other - 1], wc_r.at[other - 1], columns, columns)
-    for copy in w_x:
-        copy.wait_send()
+    pass_on(1)
+    pass_on(2)
 
     for i in range(3):
+        arrived(i)
         qkv[i] = nn(normed_one, w_full[i]).astype(BF16)
+    pass_on(3)
     lane = iota((1, 2 * HEAD_DIM), 1)
     halves = (lane < HEAD_DIM, lane >= HEAD_DIM)
     key_valid = iota((1, pad), 1) < sz.rows
@@ -362,10 +381,10 @@
         until = 1 + ((parts - 1) * (turn + 1)) // 2
         for c in range(sent, until):
             send_cot(c)
-            start_part(c, *cot_flow)
         sent = until
         lax.fori_loop(turn * pairs // 2, (turn + 1) * pairs // 2, attend, 0)
 
+    arrived(3)
     hidden = x_rows + nt(mixed[...], w_full[3])
     hidden_at[...] = hidden
     unit_two, _ = normalize(hidden)
@@ -392,55 +411,56 @@
     def expert_rows(ref, e):
         return ref[:, rows_at(e, sz.cap), :].reshape(many, width)
 
-    def cot_grad(e, carry):
-        grad_act[e] = nt(expert_rows(cot_slots, e), second[e])
-        return carry
+    def send_gates():
+        logits = jnp.where(named, nt(router_t[...], rows_block[...]), NEG)
+        exponent = jnp.where(named, jnp.exp(logits - jnp.max(logits, 0, keepdims=True)), 0.0)
+        total = jnp.sum(exponent, 0, keepdims=True)
+        gates = exponent / jnp.where(total > 0.0, total, 1.0)
+        gates_at[...] = gates
+        by_slot = nt(split_high_low(gates), select[...])
+        by_slot = by_slot[0 : sz.experts] + by_slot[sz.experts :]
+        own_slot = iota((sz.experts, sz.slots), 1) // sz.cap == iota((sz.experts, sz.slots), 0)
+        by_slot = jnp.where(own_slot, by_slot, 0.0)
+        folded = by_slot[:, 0:128]
+        for i in range(1, sz.slots // 128):
+            folded = folded + by_slot[:, i * 128 : (i + 1) * 128]
+        gate_send[...] = folded
+        gate_copies = [
+            remote(
+                gate_send.at[rows_at(at.next_group(k) * sz.own // 8, 8)], gate_recv.at[me], ga_s.at[0], ga_r.at[0],
+                at.plane(at.next_group(k)),
+            )
+            for k in range(1, ng)
+        ]
+        for copy in gate_copies:
+            copy.start()
+        gate_recv[me] = gate_send[rows_at(me * sz.own // 8, 8)]
 
     for c in range(parts):
         wait_along(rows_block, nz_s, nz_r, c)
-        dispatch(c, rows_block, send_b, slots)
-        start_part(c, *row_flow)
-        if c == parts // 2 - 1:
-            for i in range(parts):
-                wait_part(i, *cot_flow)
-            for copy in loads:
-                copy.wait()
-            lax.fori_loop(0, sz.own, cot_grad, 0)
-
-    logits = jnp.where(named, nt(router_t[...], rows_block[...]), NEG)
-    exponent = jnp.where(named, jnp.exp(logits - jnp.max(logits, 0, keepdims=True)), 0.0)
-    total = jnp.sum(exponent, 0, keepdims=True)
-    gates = exponent / jnp.where(total > 0.0, total, 1.0)
-    gates_at[...] = gates
-    by_slot = nt(split_high_low(gates), select[...])
-    by_slot = by_slot[0 : sz.experts] + by_slot[sz.experts :]
-    own_slot = iota((sz.experts, sz.slots), 1) // sz.cap == iota((sz.experts, sz.slots), 0)
-    by_slot = jnp.where(own_slot, by_slot, 0.0)
-    folded = by_slot[:, 0:128]
-    for i in range(1, sz.slots // 128):
-        folded = folded + by_slot[:, i * 128 : (i + 1) * 128]
-    gate_send[...] = folded
-    gate_copies = [
-        remote(
-            gate_send.at[rows_at(at.next_group(k) * sz.own // 8, 8)], gate_recv.at[me], ga_s.at[0], ga_r.at[0],
-            at.plane(at.next_group(k)),
-        )
-        for k in range(1, ng)
-    ]
-    for copy in gate_copies:
-        copy.start()
-    gate_recv[me] = gate_send[rows_at(me * sz.own // 8, 8)]
+        if c == parts - 1:
+            send_gates()
+        dispatch(c, rows_block, *row_flow)
+
     drain(ga_s.at[0], ga_r.at[0], gate_recv.at[others], gate_recv.at[others])
-    for c in range(parts):
-        wait_part(c, *row_flow)
-
     def gate_of(e):
         turned = gate_recv[:, pl.ds(me * sz.own % 8 + e, 1), :].reshape(ng, 128).T
         columns = jnp.where((e % 2) == 1, turned[sz.cap : 2 * sz.cap], turned[0 : sz.cap])
         return jnp.concatenate([columns[:, s : s + 1] for s in range(ng)], 0)
 
-    def first_piece(e, k):
-        g = (me + k) % ng
+    def weigh(e, carry):
+        grad_act[e] = nt(expert_rows(cot_slots, e), second[e]) * gate_of(e)
+        return carry
+
+    for c in range(parts):
+        wait_part(c, *cot_flow)
+    for copy in loads:
+        copy.wait()
+    lax.fori_loop(0, sz.own, weigh, 0)
+    for c in range(parts):
+        wait_part(c, *row_flow)
+
+    def first_piece(e, g):
         piece = (rows_at(e, sz.cap), lanes(1))
         return remote(
             send_a.at[(g, *piece)], grad_slots.at[(me, *piece)], d0_s.at[e], d0_r.at[e], at.plane(g)
@@ -454,7 +474,6 @@
         )
 
     def expert_back(e, carry):
-        gate = gate_of(e)
         half_rows = many // 2
         for part_at in range(2):
             some = slice(part_at * half_rows, (part_at + 1) * half_rows)
@@ -462,15 +481,14 @@
             pre = nn(slots[groups, rows_at(e, sz.cap), :].reshape(half_rows, width), first[e])
             const, cubic = 0.7978845608028654, 0.044715
             square = pre * pre
-            bent = jnp.tanh(const * pre * (1.0 + cubic * square))
-            half = 0.5 * (1.0 + bent)
-            hidden_units = (pre * half).astype(BF16)
-            act[e, some] = hidden_units
-            slope = half + 0.5 * pre * (1.0 - bent * bent) * const * (1.0 + 3.0 * cubic * square)
+            half = 0.5 * jnp.tanh(pre * (const + const * cubic * square)) + 0.5
+            hidden_units = pre * half
+            act[e, some] = hidden_units.astype(BF16)
             through = grad_act[e, some]
-            dgate = nt(jnp.ones((8, sz.hidden), BF16), (hidden_units.astype(F32) * through).astype(BF16))
+            dgate = nt(jnp.ones((8, sz.hidden), BF16), (hidden_units * through).astype(BF16))
             dgate_send[:, some] = jnp.where(iota((8, half_rows), 0) == e, dgate, dgate_send[:, some])
-            grads = (through * gate[some] * slope).astype(BF16)
+            slope = half * (1.0 + (1.0 - half) * (pre * (2.0 * const + 6.0 * const * cubic * square)))
+            grads = (through * slope).astype(BF16)
             grad_pre[e, some] = grads
             spread = nt(grads, first[e]).astype(BF16).reshape(ng // 2, sz.cap, width)
             send_a[groups, rows_at(e, sz.cap), :] = spread
@@ -478,7 +496,7 @@
                 grads_q[i, groups, rows_at(e, quarter), :] = spread[:, i * quarter : (i + 1) * quarter, 0:part_width]
 
         def step(i, carry):
-            first_piece(e, ng - 1 - i).start()
+            first_piece(e, (me + ng - 1 - i) % ng).start()
             return carry
 
         lax.fori_loop(0, ng - 1, step, 0)
@@ -500,7 +518,7 @@
     dgate_recv[me] = dgate_send[:, rows_at(me * sz.cap // 128, 128)]
     grad_flow = (send_a, grad_slots, da_s, da_r)
     value_flow = (send_b, values, va_s, va_r)
-    for c in range(2, parts):
+    for c in range(2, parts - 1):
         start_part(c, *grad_flow)
     grad_slots[me] = send_a[me]
 
@@ -537,7 +555,7 @@
     dgate = nt(split_high_low(jnp.where(own_slot, spread, 0.0)), select_t[...])
     dgate = dgate[0 : sz.experts] + dgate[sz.experts :]
     gates = gates_at[...]
-    dlogits = (gates * (dgate - jnp.sum(gates * dgate, 0, keepdims=True))).astype(BF16)
+    dlogits = (dgate - gates * jnp.sum(dgate, 0, keepdims=True)).astype(BF16)
     rt[...] = nn(dlogits, rows_block[...])
     part[...] = tn(dlogits, router_t[...])
 
@@ -600,7 +618,7 @@
             sums = sums + recv[slot].astype(F32)
         return sums
 
-    part_flow = (part_send, part_recv, pz_s, pz_r, pr_r, 0)
+    part_flow = (part_send, part_recv, pz_s, pz_r, pr_r, parts - 1)
     mix_flow = (mix_send, mix_recv, mz_s, mz_r, mr_r, parts - 1)
 
     def wait_first(e, carry):
@@ -613,10 +631,13 @@
         quarter_total(grads_q, grads_line, grads_sum)
         for copy in grads_moves:
             copy.start()
+        start_part(parts - 1, *grad_flow)
+        start_part(0, *value_flow)
         grads_back[me] = grads_sum[me]
 
     grads_moves = [quarter_move(k, grads_sum, grads_back, dq_s, dq_r) for k in range(1, ng)]
-    order = [*range(1, parts), 0]
+    order = [*range(1, parts - 1), 0, parts - 1]
+    exchange_quarters()
     done = 0
     for turn, c in enumerate(order):
         if c == 0:
@@ -626,11 +647,9 @@
         else:
             wait_part(c, *grad_flow)
         if c == parts - 1:
-            for i in range(parts):
+            for i in range(1, parts):
                 start_part(i, *value_flow)
         scatter(c, grads_back if c == 0 else grad_slots, part, part_own, *part_flow)
-        if turn == 0:
-            exchange_quarters()
         until = sz.own * (turn + 1) // parts
         lax.fori_loop(done, until, weight_grads, 0)
         done = until
@@ -648,6 +667,13 @@
     for copy in stores:
         copy.start()
 
+    def send_mix(c):
+        wait_part(c, *value_flow)
+        scatter(c, values, None, mix_own, *mix_flow)
+        if c:
+            relay(c - 1, *mix_flow)
+
+    send_mix(0)
     unit_two, factor_two = normalize(hidden_at[...])
     grad_normed = jnp.where(row_valid, gathered(part_own, *part_flow), 0.0)
     grad_hidden, gain_two = norm_back(grad_normed, unit_two, factor_two, gain_two_ref[...])
@@ -686,13 +712,7 @@
     for k in range(1, nd):
         band_copy(k, 3).start()
 
-    def send_mix(c):
-        wait_part(c, *value_flow)
-        scatter(c, values, None, mix_own, *mix_flow)
-        if c:
-            relay(c - 1, *mix_flow)
-
-    for c in range(parts // 2):
+    for c in range(1, parts // 2):
         send_mix(c)
 
     def attend_back(pair):
@@ -730,10 +750,9 @@
                 half_sum(i, sums)
         if other == nh - 1:
             send_mix(2)
-    for i in range(3):
+    for i in range(2):
         for k in range(1, nd):
             band_copy(k, i).start()
-    send_mix(3)
 
     grad_one = jnp.zeros((pad, width), F32)
     for i in range(3):
@@ -775,12 +794,15 @@
         ]
     for copy in small_copies:
         copy.start()
+    for k in range(1, nd):
+        band_copy(k, 2).start()
+    send_mix(3)
 
     def line_piece(i, j):
         to = at.next_z(j)
         return remote(line_send.at[i, rows_at(to, rp), :], line_recv.at[j - 1, i], gl_s.at[i], gl_r.at[i], at.line(to))
 
-    for i in (3, 0, 1, 2):
+    def end_band(i):
         drain(gx_s.at[i], gx_r.at[i], band_recv.at[:, i], band_recv.at[:, i])
         sums = w_half[i, rows_at(d, band), :]
         for k in range(1, nd):
@@ -789,6 +811,9 @@
         line_send[i] = sums.astype(BF16)
         for j in range(1, nz):
             line_piece(i, j).start()
+
+    for i in (3, 0, 1):
+        end_band(i)
     drain(sx_s.at[0], sx_r.at[0], small_x, small_x)
     drain(sx_s.at[1], sx_r.at[1], rt_x, rt_x)
     router_sum = rt[:, rows_at(d, band)]
@@ -801,6 +826,7 @@
         device = at.line(at.next_z(j))
         remote(small_send.at[1], small_z.at[j - 1], gl_s.at[4], gl_r.at[4], device).start()
         remote(rt_z.at[nz - 1], rt_z.at[j - 1], gl_s.at[5], gl_r.at[5], device).start()
+    end_band(2)
 
     mix = gathered(mix_own, *mix_flow)
     output_out[...] = (hidden_at[...] + mix)[0 : sz.rows].astype(BF16)
@@ -915,7 +941,7 @@
             full(8, width), full(2, 8, width), full(nh - 1, 8, width), full(nd - 1, 8, width), full(nz - 1, 8, width),
             full(sz.experts, width), full(nh - 1, sz.experts, width), full(nd - 1, sz.experts, band),
             full(nz, sz.experts, band),
-            *pair(1), *pair(nd - 1), *pair(nh - 1), *pair(1), *pair(parts), *pair(parts), *pair(parts), *pair(parts),
+            *pair(4), *pair(4), *pair(4 * (nh - 1)), *pair(1), *pair(parts), *pair(parts), *pair(parts), *pair(parts),
             *pair(1), *pair(own), *pair(parts), *pair(parts), *pair(1), *pair(parts), *pair(parts), *pair(4 * (nh - 1)),
             *pair(4), *pair(6), *pair(2 * (nh - 1)), *pair(2), *pair(1), *pair(1),
             *pair(parts, 2),

time: 148 us -> 141 us (0.953)
  Pallas kernels: 147 us -> 140 us
    pallas_call x1, Pallas kernels: 142 us -> 135 us  [fast_body(): pl.pallas_call(functools.partial(block_kernel, sz), out_shape=(*smalls, s...]
where the time goes in v5:
time: 141 us
  Pallas kernels  140 us (99%)
    pallas_call x1, Pallas kernels, fast_body(): pl.pallas_call(functools.partial(block_kernel, sz), out_shape=(*smalls, s...  135 us
    pallas_call x1, Pallas kernels, fast_body(): pl.pallas_call(functools.partial(finish_kernel, sz), out_shape=(*smalls,...  4.94 us

profile of v5, /device:TPU:0, one launch (start us, length us, event | category | flops | bytes accessed | tf_op | source)
XLA Modules:
  0.0 141.2 jit_solution(2966400898583022642)
XLA Ops:
  0.6 135.5 %block.1 = (bf16[197,512]{1,0:T(8,128)(2,1)}, bf16[197,512]{1,0:T(8,128)(2,1)}, f32[1,512]{1,0:T(1,128)}, f32[1,512]{1,0:T(1,128)}, f32[3,32,256]{2,1,0:T(8,128)...) custom-call(bf16[197,512]{1,0:T(8,128)(2,1)} %x_ref.1, ...), custom_call_target="tpu_custom_call" | custom-call | tf_op jit(solution)/shard_map/block/pallas_call | solution.py:920
  136.1 4.9 %finish.1 = (bf16[197,512]{1,0:T(8,128)(2,1)}, bf16[197,512]{1,0:T(8,128)(2,1)}, f32[1,512]{1,0:T(1,128)}, f32[1,512]{1,0:T(1,128)}, f32[3,32,256]{2,1,0:T(8,128...) custom-call(bf16[197,512]{1,0:T(8,128)(2,1)} %get-tuple-element.30.r, ...), custom_call_target="tpu_custom_call" | custom-call | tf_op jit(solution)/shard_map/finish/pallas_call | solution.py:959

commit v6 on v5

--- a/solution.py
+++ b/solution.py
@@ -152,16 +152,16 @@
     sz, x_ref, cot_ref, routes_ref, gain_one_ref, gain_two_ref, w_qkv_ref, w_out_ref, w_router_ref, tau_ref, first_hbm,
     second_hbm, output_out, grad_input_out, gain_one_out, gain_two_out, qkv_out, out_out, router_out, clipped_out,
     grad_first_out, grad_second_out,
-    w_own, w_full, router_own, router_full, router_t, route_rows, route_columns, select, select_t, select_qt,
+    w_own, w_full, router_own, router_full, router_t, route_rows, route_columns, select, select_t, select_q, select_qt,
     cot_block, rows_block, send_a, send_b, cot_slots, slots, grad_slots, values,
-    grads_q, grads_line, grads_sum, grads_back, first, second, act, grad_pre, grad_act, grad_second,
+    rows_q, rows_line, grads_q, grads_line, grads_sum, grads_back, first, second, act, grad_pre, grad_act, grad_second,
     gate_send, gate_recv, gates_at, dgate_send, dgate_recv, dgate_rows,
     qkv, probs, mixed, hidden_at, peak_at, part, part_own, part_send, part_recv, mix_own, mix_send, mix_recv,
     grad_mixed, grad_qkv, core_send, core_recv, w_half, band_send, band_recv, line_send, line_recv,
     small, small_send, small_core, small_x, small_z, rt, rt_core, rt_x, rt_z,
     wz_s, wz_r, wx_s, wx_r, wc_s, wc_r, r_s, r_r, qz_s, qz_r, nz_s, nz_r, qa_s, qa_r, na_s, na_r, ga_s, ga_r,
     d0_s, d0_r, da_s, da_r, va_s, va_r, dg_s, dg_r, pz_s, pz_r, mz_s, mz_r, gc_s, gc_r, gx_s, gx_r, gl_s, gl_r,
-    sc_s, sc_r, sx_s, sx_r, dl_s, dl_r, dq_s, dq_r, pr_r, mr_r,
+    sc_s, sc_r, sx_s, sx_r, dl_s, dl_r, dq_s, dq_r, nq_s, nq_r, nl_s, nl_r, pr_r, mr_r,
     local_sem,
 ):
     at = Place(sz)
@@ -294,6 +294,9 @@
         n = iota(dims, axis)
         return (n // quarter * sz.cap + z * quarter + n % quarter).astype(F32)
 
+    some_slot = quarter_slot((few, sz.block), 0)
+    select_q[...] = jnp.where(jnp.logical_or(some_slot == slot_a, some_slot == slot_b), 1.0, 0.0).astype(BF16)
+
     def quarter_move(k, send, landing, send_sems, recv_sems):
         g = (me + k) % ng
         return remote(send.at[g], landing.at[me], send_sems.at[0], recv_sems.at[0], at.plane(g))
@@ -376,13 +379,9 @@
         return carry
 
     pairs = HEADS // 2
-    sent = 1
-    for turn in range(2):
-        until = 1 + ((parts - 1) * (turn + 1)) // 2
-        for c in range(sent, until):
-            send_cot(c)
-        sent = until
-        lax.fori_loop(turn * pairs // 2, (turn + 1) * pairs // 2, attend, 0)
+    lax.fori_loop(0, pairs // 2, attend, 0)
+    send_cot(1)
+    lax.fori_loop(pairs // 2, pairs, attend, 0)
 
     arrived(3)
     hidden = x_rows + nt(mixed[...], w_full[3])
@@ -392,6 +391,9 @@
     for c in range(parts):
         for copy in along(rows_block, nz_s, nz_r, c):
             copy.start()
+
+    for c in range(2, parts):
+        send_cot(c)
 
     def fill_t(i, carry):
         rows = rows_at(i, pad)
@@ -438,7 +440,16 @@
 
     for c in range(parts):
         wait_along(rows_block, nz_s, nz_r, c)
+        if c == 0:
+            rows_q[...] = nn(select_q[...], rows_block[:, lanes(0)]).astype(BF16).reshape(rows_q.shape)
+            for k in range(1, ng):
+                quarter_move(k, rows_q, rows_line.at[z], nq_s, nq_r).start()
+            rows_line[z, me] = rows_q[me]
+            continue
         if c == parts - 1:
+            drain(nq_s.at[0], nq_r.at[0], rows_q.at[others], rows_q.at[others])
+            for j in range(1, nz):
+                remote(rows_line.at[z], rows_line.at[z], nl_s.at[0], nl_r.at[0], at.line(at.next_z(j))).start()
             send_gates()
         dispatch(c, rows_block, *row_flow)
 
@@ -457,7 +468,14 @@
     for copy in loads:
         copy.wait()
     lax.fori_loop(0, sz.own, weigh, 0)
-    for c in range(parts):
+    lines = rows_line.at[pl.ds(0, nz - 1)]
+    drain(nl_s.at[0], nl_r.at[0], lines, lines)
+    for i in range(nz):
+        for e in range(sz.own):
+            slots[:, e * sz.cap + i * quarter : e * sz.cap + (i + 1) * quarter, lanes(0)] = rows_line[
+                i, :, e * quarter : (e + 1) * quarter, :
+            ]
+    for c in range(1, parts):
         wait_part(c, *row_flow)
 
     def first_piece(e, g):
@@ -518,7 +536,7 @@
     dgate_recv[me] = dgate_send[:, rows_at(me * sz.cap // 128, 128)]
     grad_flow = (send_a, grad_slots, da_s, da_r)
     value_flow = (send_b, values, va_s, va_r)
-    for c in range(2, parts - 1):
+    for c in range(2, parts):
         start_part(c, *grad_flow)
     grad_slots[me] = send_a[me]
 
@@ -618,7 +636,7 @@
             sums = sums + recv[slot].astype(F32)
         return sums
 
-    part_flow = (part_send, part_recv, pz_s, pz_r, pr_r, parts - 1)
+    part_flow = (part_send, part_recv, pz_s, pz_r, pr_r, 0)
     mix_flow = (mix_send, mix_recv, mz_s, mz_r, mr_r, parts - 1)
 
     def wait_first(e, carry):
@@ -631,12 +649,12 @@
         quarter_total(grads_q, grads_line, grads_sum)
         for copy in grads_moves:
             copy.start()
-        start_part(parts - 1, *grad_flow)
-        start_part(0, *value_flow)
+        for i in range(2):
+            start_part(i, *value_flow)
         grads_back[me] = grads_sum[me]
 
     grads_moves = [quarter_move(k, grads_sum, grads_back, dq_s, dq_r) for k in range(1, ng)]
-    order = [*range(1, parts - 1), 0, parts - 1]
+    order = [*range(1, parts), 0]
     exchange_quarters()
     done = 0
     for turn, c in enumerate(order):
@@ -647,7 +665,7 @@
         else:
             wait_part(c, *grad_flow)
         if c == parts - 1:
-            for i in range(1, parts):
+            for i in range(2, parts):
                 start_part(i, *value_flow)
         scatter(c, grads_back if c == 0 else grad_slots, part, part_own, *part_flow)
         until = sz.own * (turn + 1) // parts
@@ -712,8 +730,8 @@
     for k in range(1, nd):
         band_copy(k, 3).start()
 
-    for c in range(1, parts // 2):
-        send_mix(c)
+
+    send_mix(1)
 
     def attend_back(pair):
         columns = rows_at(pair, 2 * HEAD_DIM)
@@ -924,9 +942,9 @@
         out_specs=(on_chip,) * 8 + (anywhere,) * 2,
         scratch_shapes=[
             half(4, rp, cp), half(4, width, width), half(sz.experts, 128), half(ng, sz.experts, 128),
-            half(sz.experts, width), full(8, block), full(block, 128), half(sz.slots, block), half(block, sz.slots), half(block, few),
+            half(sz.experts, width), full(8, block), full(block, 128), half(sz.slots, block), half(block, sz.slots), half(few, block), half(block, few),
             half(block, width), half(block, width), *[slot_buffer] * 6,
-            half(nz, *quarter_dims), half(nz - 1, *quarter_dims), quarter_buffer,
+            quarter_buffer, half(nz, *quarter_dims), half(nz, *quarter_dims), half(nz - 1, *quarter_dims), quarter_buffer,
             quarter_buffer,
             half(own, width, hidden), half(own, hidden, width), half(own, many, hidden), half(own, many, hidden),
             full(own, many, hidden), half(own, hidden, width),
@@ -943,7 +961,7 @@
             full(nz, sz.experts, band),
             *pair(4), *pair(4), *pair(4 * (nh - 1)), *pair(1), *pair(parts), *pair(parts), *pair(parts), *pair(parts),
             *pair(1), *pair(own), *pair(parts), *pair(parts), *pair(1), *pair(parts), *pair(parts), *pair(4 * (nh - 1)),
-            *pair(4), *pair(6), *pair(2 * (nh - 1)), *pair(2), *pair(1), *pair(1),
+            *pair(4), *pair(6), *pair(2 * (nh - 1)), *pair(2), *pair(1), *pair(1), *pair(1), *pair(1),
             *pair(parts, 2),
             pltpu.SemaphoreType.DMA((3 + own,)),
         ],

time: 141 us -> 137 us (0.972)
  Pallas kernels: 140 us -> 136 us
    pallas_call x1, Pallas kernels: 135 us -> 131 us  [fast_body(): pl.pallas_call(functools.partial(block_kernel, sz), out_shape=(*smalls, s...]
where the time goes in v6:
time: 137 us
  Pallas kernels  136 us (99%)
    pallas_call x1, Pallas kernels, fast_body(): pl.pallas_call(functools.partial(block_kernel, sz), out_shape=(*smalls, s...  131 us
    pallas_call x1, Pallas kernels, fast_body(): pl.pallas_call(functools.partial(finish_kernel, sz), out_shape=(*smalls,...  4.94 us

profile of v6, /device:TPU:0, one launch (start us, length us, event | category | flops | bytes accessed | tf_op | source)
XLA Modules:
  0.0 137.2 jit_solution(17584344645666245523)
XLA Ops:
  0.6 131.4 %block.1 = (bf16[197,512]{1,0:T(8,128)(2,1)}, bf16[197,512]{1,0:T(8,128)(2,1)}, f32[1,512]{1,0:T(1,128)}, f32[1,512]{1,0:T(1,128)}, f32[3,32,256]{2,1,0:T(8,128)...) custom-call(bf16[197,512]{1,0:T(8,128)(2,1)} %x_ref.1, ...), custom_call_target="tpu_custom_call" | custom-call | tf_op jit(solution)/shard_map/block/pallas_call | solution.py:938
  132.1 4.9 %finish.1 = (bf16[197,512]{1,0:T(8,128)(2,1)}, bf16[197,512]{1,0:T(8,128)(2,1)}, f32[1,512]{1,0:T(1,128)}, f32[1,512]{1,0:T(1,128)}, f32[3,32,256]{2,1,0:T(8,128...) custom-call(bf16[197,512]{1,0:T(8,128)(2,1)} %get-tuple-element.30.r, ...), custom_call_target="tpu_custom_call" | custom-call | tf_op jit(solution)/shard_map/finish/pallas_call | solution.py:977

commit v7 on v6

--- a/solution.py
+++ b/solution.py
@@ -154,7 +154,7 @@
     grad_first_out, grad_second_out,
     w_own, w_full, router_own, router_full, router_t, route_rows, route_columns, select, select_t, select_q, select_qt,
     cot_block, rows_block, send_a, send_b, cot_slots, slots, grad_slots, values,
-    rows_q, rows_line, grads_q, grads_line, grads_sum, grads_back, first, second, act, grad_pre, grad_act, grad_second,
+    rows_q, rows_line, grads_q, grads_line, grads_sum, grads_back, first, second, act, grad_pre, grad_act,
     gate_send, gate_recv, gates_at, dgate_send, dgate_recv, dgate_rows,
     qkv, probs, mixed, hidden_at, peak_at, part, part_own, part_send, part_recv, mix_own, mix_send, mix_recv,
     grad_mixed, grad_qkv, core_send, core_recv, w_half, band_send, band_recv, line_send, line_recv,
@@ -558,8 +558,8 @@
 
     def weight_grads(e, carry):
         grad_value = (expert_rows(cot_slots, e).astype(F32) * gate_of(e)).astype(BF16)
-        grad_second[e] = tn(act[e], grad_value).astype(BF16)
-        select[rows_at(e, width), 0 : sz.hidden] = tn(expert_rows(slots, e), grad_pre[e]).astype(BF16)
+        grad_second_out[e] = tn(act[e], grad_value).astype(BF16)
+        grad_first_out[e] = tn(expert_rows(slots, e), grad_pre[e]).astype(BF16)
         return carry
 
     drain(dg_s.at[0], dg_r.at[0], dgate_recv.at[others], dgate_recv.at[others])
@@ -673,18 +673,6 @@
         done = until
         if turn > 0:
             relay(order[turn - 1], *part_flow)
-    stores = [
-        pltpu.make_async_copy(grad_second, grad_second_out, local_sem.at[2]),
-        *[
-            pltpu.make_async_copy(
-                select.at[e * width : (e + 1) * width, 0 : sz.hidden], grad_first_out.at[e], local_sem.at[3 + e]
-            )
-            for e in range(sz.own)
-        ],
-    ]
-    for copy in stores:
-        copy.start()
-
     def send_mix(c):
         wait_part(c, *value_flow)
         scatter(c, values, None, mix_own, *mix_flow)
@@ -881,27 +869,20 @@
             qkv_out[i] = sums
         else:
             out_out[...] = sums
-    for copy in stores:
-        copy.wait()
 
 
 def finish_kernel(sz, *refs):
-    sources, results, held = refs[0:10], refs[10:20], refs[20:28]
-    halves_in, full_out, in_sems, out_sems, small_in, small_out = refs[28:]
-    pieces = [(i, e) for e in range(sz.own) for i in range(2)]
-    loads = [pltpu.make_async_copy(sources[8 + i].at[e], halves_in.at[i, e], in_sems.at[i, e]) for i, e in pieces]
-    stores = [pltpu.make_async_copy(full_out.at[i, e], results[8 + i].at[e], out_sems.at[i, e]) for i, e in pieces]
-    small_loads = [pltpu.make_async_copy(sources[n], held[n], small_in.at[n]) for n in range(8)]
-    small_stores = [pltpu.make_async_copy(held[n], results[n], small_out.at[n]) for n in range(8)]
-    for copy in loads + small_loads:
+    sources, results = refs[0:10], refs[10:20]
+    full_out, out_sems, small_out = refs[20:]
+    small_stores = [pltpu.make_async_copy(sources[n], results[n], small_out.at[n]) for n in range(8)]
+    for copy in small_stores:
         copy.start()
-    for (i, e), load, store in zip(pieces, loads, stores):
-        load.wait()
-        full_out[i, e] = halves_in[i, e].astype(F32)
-        store.start()
-    for load, store in zip(small_loads, small_stores):
-        load.wait()
-        store.start()
+    stores = []
+    for e in range(sz.own):
+        for i in range(2):
+            full_out[i, e] = sources[8 + i][e].astype(F32)
+            stores.append(pltpu.make_async_copy(full_out.at[i, e], results[8 + i].at[e], out_sems.at[i, e]))
+            stores[-1].start()
     for copy in stores + small_stores:
         copy.wait()
 
@@ -937,9 +918,9 @@
     )
     packed = pl.pallas_call(
         functools.partial(block_kernel, sz),
-        out_shape=(*smalls, shape(w_in.shape, BF16), shape(w_out.shape, BF16)),
+        out_shape=(*[pltpu.VMEM(x.shape, x.dtype) for x in smalls], half(*w_in.shape), half(*w_out.shape)),
         in_specs=[on_chip] * 9 + [anywhere] * 2,
-        out_specs=(on_chip,) * 8 + (anywhere,) * 2,
+        out_specs=(on_chip,) * 10,
         scratch_shapes=[
             half(4, rp, cp), half(4, width, width), half(sz.experts, 128), half(ng, sz.experts, 128),
             half(sz.experts, width), full(8, block), full(block, 128), half(sz.slots, block), half(block, sz.slots), half(few, block), half(block, few),
@@ -947,7 +928,7 @@
             quarter_buffer, half(nz, *quarter_dims), half(nz, *quarter_dims), half(nz - 1, *quarter_dims), quarter_buffer,
             quarter_buffer,
             half(own, width, hidden), half(own, hidden, width), half(own, many, hidden), half(own, many, hidden),
-            full(own, many, hidden), half(own, hidden, width),
+            full(own, many, hidden),
             full(sz.experts, 128), full(ng, 8, 128), full(sz.experts, block), full(8, many),
             full(ng, 8, 128), full(sz.experts, 128),
             half(3, pad, width), half(HEADS, pad, pad), half(pad, width), full(pad, width), full(8, 128),
@@ -963,9 +944,9 @@
             *pair(1), *pair(own), *pair(parts), *pair(parts), *pair(1), *pair(parts), *pair(parts), *pair(4 * (nh - 1)),
             *pair(4), *pair(6), *pair(2 * (nh - 1)), *pair(2), *pair(1), *pair(1), *pair(1), *pair(1),
             *pair(parts, 2),
-            pltpu.SemaphoreType.DMA((3 + own,)),
+            pltpu.SemaphoreType.DMA((2,)),
         ],
-        compiler_params=pltpu.CompilerParams(collective_id=0, has_side_effects=True, vmem_limit_bytes=62 * 2**20),
+        compiler_params=pltpu.CompilerParams(collective_id=0, has_side_effects=True, vmem_limit_bytes=57 * 2**20),
         name="block",
     )(
         inputs, cotangent, routes.T, gain_attn[None, :], gain_expert[None, :], w_qkv, w_out_attn.T, w_router.T,
@@ -977,15 +958,12 @@
         pl.pallas_call(
             functools.partial(finish_kernel, sz),
             out_shape=(*smalls, shape(w_in.shape, F32), shape(w_out.shape, F32)),
-            in_specs=[anywhere] * 10,
+            in_specs=[on_chip] * 10,
             out_specs=(anywhere,) * 10,
-            scratch_shapes=[
-                *[pltpu.VMEM(x.shape, x.dtype) for x in smalls], half(*both), full(*both), dma((2, own)), dma((2, own)),
-                dma((8,)), dma((8,)),
-            ],
-            compiler_params=pltpu.CompilerParams(vmem_limit_bytes=62 * 2**20),
+            scratch_shapes=[full(*both), dma((2, own)), dma((8,))],
+            compiler_params=pltpu.CompilerParams(vmem_limit_bytes=48 * 2**20),
             name="finish",
-        )(*packed)
+        )(*[pltpu.with_memory_space_constraint(x, pltpu.VMEM) for x in packed])
     )
     return (
         output, grad_input, gain_one[0], gain_two[0], grad_qkv, grad_out.T, grad_router.T, grad_first, grad_second,

time: 137 us -> 135 us (0.985)
  Pallas kernels: 136 us -> 134 us
where the time goes in v7:
time: 135 us
  Pallas kernels  134 us (99%)
    pallas_call x1, Pallas kernels, fast_body(): pl.pallas_call(functools.partial(block_kernel, sz), out_shape=(*[pltpu.VM...  131 us
    pallas_call x1, Pallas kernels, fast_body(): pl.pallas_call(functools.partial(finish_kernel, sz), out_shape=(*smalls,...  3.66 us

profile of v7, /device:TPU:0, one launch (start us, length us, event | category | flops | bytes accessed | tf_op | source)
XLA Modules:
  0.0 135.1 jit_solution(2032997293919738417)
XLA Ops:
  0.6 130.6 %block.1 = (bf16[197,512]{1,0:T(8,128)(2,1)S(1)}, bf16[197,512]{1,0:T(8,128)(2,1)S(1)}, f32[1,512]{1,0:T(1,128)S(1)}, f32[1,512]{1,0:T(1,128)S(1)}, f32[3,32,256...) custom-call(bf16[197,512]{1,0:T(8,128)(2,1)} %x_ref.1, ...), custom_call_target="tpu_custom_call" | custom-call | tf_op jit(solution)/shard_map/block/pallas_call | solution.py:919
  131.2 3.7 %finish.1 = (bf16[197,512]{1,0:T(8,128)(2,1)}, bf16[197,512]{1,0:T(8,128)(2,1)}, f32[1,512]{1,0:T(1,128)}, f32[1,512]{1,0:T(1,128)}, f32[3,32,256]{2,1,0:T(8,128...) custom-call(bf16[197,512]{1,0:T(8,128)(2,1)S(1)} %get-tuple-element., ...), custom_call_target="tpu_custom_call" | custom-call | tf_op jit(solution)/shard_map/finish/pallas_call | solution.py:958

commit v8 on v7

--- a/solution.py
+++ b/solution.py
@@ -161,7 +161,7 @@
     small, small_send, small_core, small_x, small_z, rt, rt_core, rt_x, rt_z,
     wz_s, wz_r, wx_s, wx_r, wc_s, wc_r, r_s, r_r, qz_s, qz_r, nz_s, nz_r, qa_s, qa_r, na_s, na_r, ga_s, ga_r,
     d0_s, d0_r, da_s, da_r, va_s, va_r, dg_s, dg_r, pz_s, pz_r, mz_s, mz_r, gc_s, gc_r, gx_s, gx_r, gl_s, gl_r,
-    sc_s, sc_r, sx_s, sx_r, dl_s, dl_r, dq_s, dq_r, nq_s, nq_r, nl_s, nl_r, pr_r, mr_r,
+    sc_s, sc_r, sx_s, sx_r, dl_s, dl_r, dq_s, dq_r, nq_s, nq_r, nl_s, nl_r, nb_s, nb_r, pr_r, mr_r,
     local_sem,
 ):
     at = Place(sz)
@@ -178,6 +178,8 @@
         return pl.ds(pl.multiple_of(n * size, size), size)
 
     own_block, own_columns = rows_at(z, pad), rows_at(h, cp)
+    inner = at.inner()
+    beside, across, mirror = at.mates()
 
     w_own[0:3] = w_qkv_ref[...]
     w_own[3] = w_out_ref[...]
@@ -388,9 +390,38 @@
     hidden_at[...] = hidden
     unit_two, _ = normalize(hidden)
     rows_block[own_block] = jnp.where(row_valid, unit_two * gain_two_ref[...], 0.0).astype(BF16)
+
+    def row_copy(c, owner, to, recv_sems):
+        place = rows_block.at[rows_at(owner, pad), lanes(c)]
+        return remote(place, place, nz_s.at[c], recv_sems.at[c], at.line(to))
+
     for c in range(parts):
-        for copy in along(rows_block, nz_s, nz_r, c):
-            copy.start()
+        row_copy(c, z, across, nb_r).start()
+        row_copy(c, z, beside, nz_r).start()
+
+        @pl.when(inner == 1)
+        def _(c=c):
+            row_copy(c, z, mirror, nz_r).start()
+
+    def row_bytes(c, pieces):
+        return rows_block.at[pl.ds(0, pieces * pad), lanes(c)]
+
+    def wait_rows(c):
+        pltpu.make_async_copy(row_bytes(c, 1), row_bytes(c, 1), nb_r.at[c]).wait()
+
+        @pl.when(inner == 1)
+        def _():
+            row_copy(c, across, beside, nz_r).start()
+
+        pltpu.make_async_copy(row_bytes(c, 2), row_bytes(c, 2), nz_r.at[c]).wait()
+
+        @pl.when(inner == 1)
+        def _():
+            pltpu.make_async_copy(row_bytes(c, 4), row_bytes(c, 4), nz_s.at[c]).wait()
+
+        @pl.when(inner == 0)
+        def _():
+            pltpu.make_async_copy(row_bytes(c, 2), row_bytes(c, 2), nz_s.at[c]).wait()
 
     for c in range(2, parts):
         send_cot(c)
@@ -439,7 +470,7 @@
         gate_recv[me] = gate_send[rows_at(me * sz.own // 8, 8)]
 
     for c in range(parts):
-        wait_along(rows_block, nz_s, nz_r, c)
+        wait_rows(c)
         if c == 0:
             rows_q[...] = nn(select_q[...], rows_block[:, lanes(0)]).astype(BF16).reshape(rows_q.shape)
             for k in range(1, ng):
@@ -576,9 +607,6 @@
     dlogits = (dgate - gates * jnp.sum(dgate, 0, keepdims=True)).astype(BF16)
     rt[...] = nn(dlogits, rows_block[...])
     part[...] = tn(dlogits, router_t[...])
-
-    inner = at.inner()
-    beside, across, mirror = at.mates()
 
     def line_copy(c, slot, send, recv, send_sems, recv_sems, relay_sems, last):
         if slot < 2:
@@ -943,7 +971,7 @@
             *pair(4), *pair(4), *pair(4 * (nh - 1)), *pair(1), *pair(parts), *pair(parts), *pair(parts), *pair(parts),
             *pair(1), *pair(own), *pair(parts), *pair(parts), *pair(1), *pair(parts), *pair(parts), *pair(4 * (nh - 1)),
             *pair(4), *pair(6), *pair(2 * (nh - 1)), *pair(2), *pair(1), *pair(1), *pair(1), *pair(1),
-            *pair(parts, 2),
+            *pair(parts), *pair(parts, 2),
             pltpu.SemaphoreType.DMA((2,)),
         ],
         compiler_params=pltpu.CompilerParams(collective_id=0, has_side_effects=True, vmem_limit_bytes=57 * 2**20),

time: 135 us -> 134 us (level)
  no operation moved by 1% of the time
where the time goes in v8:
time: 134 us
  Pallas kernels  133 us (99%)
    pallas_call x1, Pallas kernels, fast_body(): pl.pallas_call(functools.partial(block_kernel, sz), out_shape=(*[pltpu.VM...  129 us
    pallas_call x1, Pallas kernels, fast_body(): pl.pallas_call(functools.partial(finish_kernel, sz), out_shape=(*smalls,...  3.66 us

profile of v8, /device:TPU:0, one launch (start us, length us, event | category | flops | bytes accessed | tf_op | source)
XLA Modules:
  0.0 133.9 jit_solution(2312066354150852957)
XLA Ops:
  0.6 129.4 %block.1 = (bf16[197,512]{1,0:T(8,128)(2,1)S(1)}, bf16[197,512]{1,0:T(8,128)(2,1)S(1)}, f32[1,512]{1,0:T(1,128)S(1)}, f32[1,512]{1,0:T(1,128)S(1)}, f32[3,32,256...) custom-call(bf16[197,512]{1,0:T(8,128)(2,1)} %x_ref.1, ...), custom_call_target="tpu_custom_call" | custom-call | tf_op jit(solution)/shard_map/block/pallas_call | solution.py:947
  130.0 3.7 %finish.1 = (bf16[197,512]{1,0:T(8,128)(2,1)}, bf16[197,512]{1,0:T(8,128)(2,1)}, f32[1,512]{1,0:T(1,128)}, f32[1,512]{1,0:T(1,128)}, f32[3,32,256]{2,1,0:T(8,128...) custom-call(bf16[197,512]{1,0:T(8,128)(2,1)S(1)} %get-tuple-element., ...), custom_call_target="tpu_custom_call" | custom-call | tf_op jit(solution)/shard_map/finish/pallas_call | solution.py:986

commit v9 on v8

--- a/solution.py
+++ b/solution.py
@@ -345,8 +345,8 @@
     for c in range(1, parts):
         for copy in along(cot_block, qz_s, qz_r, c):
             copy.start()
+    send_cot(0)
     pass_on(0)
-    send_cot(0)
     pass_on(1)
     pass_on(2)
 
@@ -677,7 +677,7 @@
         quarter_total(grads_q, grads_line, grads_sum)
         for copy in grads_moves:
             copy.start()
-        for i in range(2):
+        for i in range(3):
             start_part(i, *value_flow)
         grads_back[me] = grads_sum[me]
 
@@ -693,7 +693,7 @@
         else:
             wait_part(c, *grad_flow)
         if c == parts - 1:
-            for i in range(2, parts):
+            for i in range(3, parts):
                 start_part(i, *value_flow)
         scatter(c, grads_back if c == 0 else grad_slots, part, part_own, *part_flow)
         until = sz.own * (turn + 1) // parts

time: 134 us -> 134 us (level)
  no operation moved by 1% of the time
where the time goes in v9:
time: 134 us
  Pallas kernels  133 us (99%)
    pallas_call x1, Pallas kernels, fast_body(): pl.pallas_call(functools.partial(block_kernel, sz), out_shape=(*[pltpu.VM...  129 us
    pallas_call x1, Pallas kernels, fast_body(): pl.pallas_call(functools.partial(finish_kernel, sz), out_shape=(*smalls,...  3.66 us

profile of v9, /device:TPU:0, one launch (start us, length us, event | category | flops | bytes accessed | tf_op | source)
XLA Modules:
  0.0 133.8 jit_solution(5255926077836869150)
XLA Ops:
  0.6 129.3 %block.1 = (bf16[197,512]{1,0:T(8,128)(2,1)S(1)}, bf16[197,512]{1,0:T(8,128)(2,1)S(1)}, f32[1,512]{1,0:T(1,128)S(1)}, f32[1,512]{1,0:T(1,128)S(1)}, f32[3,32,256...) custom-call(bf16[197,512]{1,0:T(8,128)(2,1)} %x_ref.1, ...), custom_call_target="tpu_custom_call" | custom-call | tf_op jit(solution)/shard_map/block/pallas_call | solution.py:947
  129.9 3.7 %finish.1 = (bf16[197,512]{1,0:T(8,128)(2,1)}, bf16[197,512]{1,0:T(8,128)(2,1)}, f32[1,512]{1,0:T(1,128)}, f32[1,512]{1,0:T(1,128)}, f32[3,32,256]{2,1,0:T(8,128...) custom-call(bf16[197,512]{1,0:T(8,128)(2,1)S(1)} %get-tuple-element., ...), custom_call_target="tpu_custom_call" | custom-call | tf_op jit(solution)/shard_map/finish/pallas_call | solution.py:986
